TPU v7x, 512 devices: a whole 4x8x8 slice. The times are simulated.
512 devices in a mesh: strike: 64 (over z, x, core), depth: 8 (over y).
Axes of the slice: x: 4, y: 8, z: 8, core: 2. Of those that a mesh axis runs over, the one named last changes fastest.
Arguments:
- state_dofs: float32 [9, 56, 16384], P(None, None, ('strike', 'depth')), may hold values from -6 to 6
- jacobians: float32 [3, 9, 9, 16384], P(None, None, None, ('strike', 'depth')), may hold values from -2.1 to 2.1
- flux_local: float32 [4, 9, 9, 16384], P(None, None, None, ('strike', 'depth')), may hold values from -1 to 1
- flux_neigh: float32 [4, 9, 9, 16384], P(None, None, None, ('strike', 'depth')), may hold values from -1 to 1
- stiffness: float32 [3, 56, 56], replicated, may hold values from -0.75 to 0.75
- volume: float32 [3, 56, 56], replicated, may hold values from -0.75 to 0.75
- face_proj: float32 [12, 56, 21], replicated, may hold values from -0.75 to 0.75
- face_lift: float32 [4, 21, 56], replicated, may hold values from -1.25 to 1.25
- strength: float32 [16384], P(('strike', 'depth')), may hold values from 0.3 to 3
- cluster: int32 [16384], P(('strike', 'depth')), may hold values from 0 to 1, as said below
- neighbours: int32 [4, 16384], P(None, ('strike', 'depth')), may hold values from 0 to 128, as said below
- face_orient: int32 [4, 16384], P(None, ('strike', 'depth')), may hold values from 0 to 11
- strike_sends: int32 [2, 16384], P(None, ('strike', 'depth')), may hold values from 0 to 31
- strike_orient: int32 [2, 16384], P(None, ('strike', 'depth')), may hold values from 0 to 11
- depth_sends: int32 [2, 8192], P(None, ('strike', 'depth')), may hold values from 0 to 31
- depth_orient: int32 [2, 8192], P(None, ('strike', 'depth')), may hold values from 0 to 11
- fault_elem: int32 [16384], P(('strike', 'depth')), may hold values from 0 to 31
- fault_proj: int32 [16384], P(('strike', 'depth')), may hold values from 0 to 11
Outputs:
- new_dofs: float32 [9, 56, 16384], P(None, None, ('strike', 'depth'))
Inputs may be any that keep to these rules, and one draw needn't show every extreme that they name: 0 marks the fast cluster, 1 the slow one; at most 16 elements of one device are in the fast cluster, and some device has exactly 16. `neighbours`: every received face of a device is named by exactly one face of that device; the largest value marks the slab's outer boundary and occurs on every device.
All inputs are finite; a program needn't handle non-finite values.
Results may differ from a plain program's by a relative error of at most 0.0003.
Values sent between devices are 32-bit elements; how exact they have to be, the bound alone decides.
No kernel may reach another device: no remote copies, remote signals or barrier semaphores. Data moves between devices by JAX's collectives and lax.ppermute only.
A program may use at most 64 MiB of HBM per device.

v0:
```python
import jax
import jax.numpy as jnp
from jax import lax
from jax.experimental import pallas as pl
from jax.experimental.pallas import tpu as pltpu
from jax.sharding import PartitionSpec as P


BASIS = 56
FACE_BASIS = 21
FACE_ROWS = 24
ORDER = 6
PROJS = 12
FACES = 4
WIDE = 32
LANES = 128
TILES = 3
COEFS = 21
CHUNKS = ((0, 32), (32, 24))

fast_step = 0.5
f32 = jnp.float32
bf16 = jnp.bfloat16


def split(values):
    high = values.astype(bf16).astype(f32)
    return high, values - high


def right3(values):
    high, low = split(values)
    return jnp.concatenate([high, high, low], axis=0).astype(bf16)


def left3(weights):
    high, low = split(weights)
    return jnp.concatenate([high, low, high], axis=1).astype(bf16)


def mm(left, right):
    return jnp.dot(left, right, preferred_element_type=f32)


def stacked(tiles):
    return jnp.concatenate([right3(tile) for tile in tiles], axis=1)


def lane_tiled(row):
    return jnp.concatenate([row] * (LANES // row.shape[1]), axis=1)


def build_coefs(source, target):
    def across(pieces):
        return jnp.concatenate(pieces, axis=1)

    kinds = source.shape[2]
    for out in range(2):
        for into in range(2):
            for turn in range(4):
                target[(out * 2 + into) * 4 + turn, 0:kinds, :] = across(
                    [source[4 * out + g, 4 * into + (g - turn) % 4] for g in range(4)]
                )
        target[16 + out, 0:kinds, :] = across([source[4 * out + g, 8] for g in range(4)])
        target[18 + out, 0:kinds, :] = across([source[8, 4 * out + g] for g in range(4)])
    corner = source[8, 8]
    empty = jnp.zeros_like(corner)
    target[20, 0:kinds, :] = across([corner, empty, empty, empty])


def contract(coefs, terms):
    totals = [None, None, None]

    def add(which, kind, slot, values):
        product = coefs[slot, kind : kind + 1, :] * values
        totals[which] = product if totals[which] is None else totals[which] + product

    for kind, tiles in terms:
        for into in range(2):
            for turn in range(4):
                turned = pltpu.roll(tiles[into], WIDE * turn, 1) if turn else tiles[into]
                for out in range(2):
                    add(out, kind, (out * 2 + into) * 4 + turn, turned)
                if turn == 0:
                    add(2, kind, 18 + into, turned)
        for out in range(2):
            add(out, kind, 16 + out, tiles[2])
        add(2, kind, 20, tiles[2])
    last = totals[2]
    last = last + pltpu.roll(last, 2 * WIDE, 1)
    last = last + pltpu.roll(last, WIDE, 1)
    return totals[0], totals[1], last


def volume_like(tiles, weights3, coefs):
    applied = mm(weights3, stacked(tiles))
    pieces = []
    for start, size in CHUNKS:
        terms = []
        for d in range(3):
            rows = applied[BASIS * d + start : BASIS * d + start + size]
            terms.append((d, [rows[:, LANES * t : LANES * (t + 1)] for t in range(TILES)]))
        pieces.append(contract(coefs, terms))
    return [
        jnp.concatenate([piece[t] for piece in pieces], axis=0) for t in range(TILES)
    ]


def integrals(tiles, weights3, coefs, with_second):
    current = tiles
    first = second = None
    factorial = 1.0
    for degree in range(ORDER):
        factorial = factorial * (degree + 1)
        early = fast_step ** (degree + 1)
        late = (2.0 * fast_step) ** (degree + 1) - early
        term = [tile * (early / factorial) for tile in current]
        first = term if first is None else [a + b for a, b in zip(first, term)]
        if with_second:
            term = [tile * (late / factorial) for tile in current]
            second = term if second is None else [a + b for a, b in zip(second, term)]
        if degree + 1 < ORDER:
            current = volume_like(current, weights3, coefs)
    return first, second


def iotas(rows, columns):
    shape = (rows, columns)
    return (
        lax.broadcasted_iota(jnp.int32, shape, 0),
        lax.broadcasted_iota(jnp.int32, shape, 1),
    )


def one_hot(mask):
    return jnp.where(mask, 1.0, 0.0).astype(bf16)


def picking(elements):
    sublane, lane = iotas(LANES, LANES)
    return one_hot(sublane == elements + (lane // WIDE) * WIDE)


def traces(gathered, labels, proj3):
    count = len(gathered)
    right = jnp.concatenate(
        [jnp.concatenate([h, h, l], axis=0).astype(bf16) for h, l in gathered], axis=1
    )
    table = mm(proj3, right)
    found = []
    for i in range(count):
        column = table[:, LANES * i : LANES * (i + 1)]
        picked = column[0:FACE_ROWS]
        for m in range(1, PROJS):
            picked = jnp.where(
                labels[i] == m, column[FACE_ROWS * m : FACE_ROWS * (m + 1)], picked
            )
        found.append(picked)
    return found


def picked_traces(tiles, pickers, labels, proj3):
    parts = []
    for tile in tiles:
        parts.extend(split(tile))
    rows = jnp.concatenate(parts, axis=0).astype(bf16)
    moved = mm(rows, pickers)
    jobs = len(labels)
    gathered, marks = [], []
    for j in range(jobs):
        column = moved[:, LANES * j : LANES * (j + 1)]
        for t in range(TILES):
            at = 2 * BASIS * t
            gathered.append((column[at : at + BASIS], column[at + BASIS : at + 2 * BASIS]))
            marks.append(labels[j])
    found = traces(gathered, marks, proj3)
    return [found[TILES * j : TILES * (j + 1)] for j in range(jobs)]


def load_tiles(ref):
    return [ref[t] for t in range(TILES)]


def store_tiles(ref, tiles):
    for t in range(TILES):
        ref[t] = tiles[t]


def send_kernel(
    state,
    jacobians,
    stiffness,
    face_proj,
    strike_sends,
    strike_orient,
    depth_sends,
    depth_orient,
    base_out,
    first_out,
    second_out,
    jac_coefs,
    stiff3_out,
    proj3_out,
    pickers_out,
    labels_out,
    up_out,
    down_out,
    depth_out,
):
    build_coefs(jacobians, jac_coefs)
    stiff3 = left3(jnp.concatenate([-stiffness[d].T for d in range(3)], axis=0))
    tiles = [state[LANES * t : LANES * (t + 1), :].T for t in range(2)]
    last = state[2 * LANES : 2 * LANES + WIDE, :]
    tiles.append(jnp.concatenate([last] * 4, axis=0).T)
    store_tiles(base_out, tiles)
    first, second = integrals(tiles, stiff3, jac_coefs, True)
    store_tiles(first_out, first)
    store_tiles(second_out, second)
    margin = jnp.zeros((FACE_ROWS - FACE_BASIS, BASIS), f32)
    proj3 = left3(
        jnp.concatenate([piece for m in range(PROJS) for piece in (face_proj[m], margin)], axis=0)
    )
    stiff3_out[...] = stiff3
    proj3_out[...] = proj3

    def jobs(strike, depth):
        return [
            lane_tiled(strike[1:2, :]),
            lane_tiled(strike[0:1, :]),
            lane_tiled(jnp.concatenate([depth[1:2, :], depth[0:1, :]], axis=1)),
        ]

    pickers = jnp.concatenate(
        [picking(elements) for elements in jobs(strike_sends, depth_sends)], axis=1
    )
    labels = jobs(strike_orient, depth_orient)
    pickers_out[...] = pickers
    for j in range(3):
        labels_out[j : j + 1, :] = labels[j]
    up, down, sideways = picked_traces(first, pickers, labels, proj3)
    for t in range(TILES):
        at = FACE_ROWS * t
        up_out[at : at + FACE_ROWS, :] = up[t]
        down_out[at : at + FACE_ROWS, :] = down[t]
        depth_out[at : at + FACE_ROWS, :] = sideways[t]


def local_part(values, base, vol3, jac_coefs, own3, local_coefs, pickers, labels, proj3, outs):
    pre_out, flux_out, near_out = outs
    interior = volume_like(values, vol3, jac_coefs)
    for t in range(TILES):
        pre_out[t] = base[t] + interior[t]
    own = mm(own3, stacked(values))
    for f in range(FACES):
        at = FACE_ROWS * f
        rows = own[at : at + FACE_ROWS]
        fluxes = contract(
            local_coefs, [(f, [rows[:, LANES * t : LANES * (t + 1)] for t in range(TILES)])]
        )
        for t in range(TILES):
            flux_out[t, at : at + FACE_ROWS, :] = fluxes[t]
    near = picked_traces(values, pickers, labels, proj3)
    for f in range(FACES):
        at = FACE_ROWS * f
        for t in range(TILES):
            near_out[t, at : at + FACE_ROWS, :] = near[f][t]


def prepare_kernel(
    values,
    base,
    jac_coefs,
    proj3,
    volume,
    face_proj,
    flux_local,
    flux_neigh,
    face_lift,
    neighbours,
    face_orient,
    pre_out,
    flux_out,
    near_out,
    vol3_out,
    own3_out,
    local_coefs,
    neigh_coefs,
    pickers_out,
    labels_out,
    halo_out,
    lift3_out,
):
    vol3 = left3(jnp.concatenate([volume[d].T for d in range(3)], axis=0))
    vol3_out[...] = vol3
    margin = jnp.zeros((FACE_ROWS - FACE_BASIS, BASIS), f32)
    own3 = left3(
        jnp.concatenate([piece for f in range(FACES) for piece in (face_proj[3 * f], margin)], axis=0)
    )
    own3_out[...] = own3
    build_coefs(flux_local, local_coefs)
    build_coefs(flux_neigh, neigh_coefs)
    lift3_out[...] = left3(
        jnp.concatenate(
            [piece for f in range(FACES) for piece in (face_lift[:, f, :], margin)], axis=0
        ).T
    )
    behind = [lane_tiled(neighbours[f : f + 1, :]) for f in range(FACES)]
    labels = [lane_tiled(face_orient[f : f + 1, :]) for f in range(FACES)]
    sublane, lane = iotas(LANES, LANES)
    group = (lane // WIDE) * WIDE
    pickers = []
    for f in range(FACES):
        labels_out[f : f + 1, :] = labels[f]
        local = jnp.where(behind[f] < WIDE, behind[f], -4 * LANES)
        pickers.append(one_hot(sublane == local + group))
        for block in range(3):
            slot = behind[f] - WIDE * (block + 1)
            slot = jnp.where((slot >= 0) & (slot < WIDE), slot, -4 * LANES)
            halo_out[LANES * block : LANES * (block + 1), LANES * f : LANES * (f + 1)] = one_hot(
                sublane == slot + group
            )
    pickers = jnp.concatenate(pickers, axis=1)
    pickers_out[...] = pickers
    local_part(
        load_tiles(values),
        load_tiles(base),
        vol3,
        jac_coefs,
        own3,
        local_coefs,
        pickers,
        labels,
        proj3[...],
        (pre_out, flux_out, near_out),
    )


def again_kernel(
    values,
    base,
    jac_coefs,
    proj3,
    vol3,
    own3,
    local_coefs,
    pickers,
    labels,
    pre_out,
    flux_out,
    near_out,
):
    local_part(
        load_tiles(values),
        load_tiles(base),
        vol3[...],
        jac_coefs,
        own3[...],
        local_coefs,
        pickers[...],
        [labels[f : f + 1, :] for f in range(FACES)],
        proj3[...],
        (pre_out, flux_out, near_out),
    )


def face_terms(lower, upper, shallow, deep, halo, near, neigh_coefs, flux):
    rows = TILES * FACE_ROWS
    lane = iotas(rows, LANES)[1]
    blocks = [
        lower[...],
        upper[...],
        jnp.where(lane % WIDE < WIDE // 2, shallow[0:rows, :], deep[0:rows, :]),
    ]
    parts = [split(block) for block in blocks]
    left = jnp.concatenate(
        [
            jnp.concatenate([part[0] for part in parts], axis=1),
            jnp.concatenate([part[1] for part in parts], axis=1),
        ],
        axis=0,
    ).astype(bf16)
    moved = mm(left, halo[...])
    moved = moved[0:rows] + moved[rows : 2 * rows]
    sums = [[], [], []]
    for f in range(FACES):
        at = FACE_ROWS * f
        behind = [
            moved[FACE_ROWS * t : FACE_ROWS * (t + 1), LANES * f : LANES * (f + 1)]
            + near[t, at : at + FACE_ROWS, :]
            for t in range(TILES)
        ]
        through = contract(neigh_coefs, [(f, behind)])
        for t in range(TILES):
            sums[t].append(through[t] + flux[t, at : at + FACE_ROWS, :])
    return [jnp.concatenate(pieces, axis=0) for pieces in sums]


def lifted(pre, terms, lift3):
    lifts = mm(lift3[...], stacked(terms))
    return [pre[t] - lifts[:, LANES * t : LANES * (t + 1)] for t in range(TILES)]


def fault_pickers(fault_elem):
    sublane, lane = iotas(LANES, LANES)
    group = lane // WIDE
    source = lane_tiled(fault_elem[...]) + jnp.where(group == 1, WIDE, 3 * WIDE)
    hit = sublane == source
    return [
        one_hot(hit & (group == 0)),
        one_hot(hit & ((group == 1) | (group == 2))),
        one_hot(hit & (group == 3)),
    ]


def middle_kernel(
    lower,
    upper,
    shallow,
    deep,
    halo,
    near,
    neigh_coefs,
    flux,
    pre,
    lift3,
    first,
    second,
    cluster,
    stiff3,
    jac_coefs,
    pickers,
    labels,
    proj3,
    fault_elem,
    fault_proj,
    advanced_out,
    later_out,
    up_out,
    down_out,
    depth_out,
):
    terms = face_terms(lower, upper, shallow, deep, halo, near, neigh_coefs, flux)
    advanced = lifted(pre, terms, lift3)
    store_tiles(advanced_out, advanced)
    repeated = integrals(advanced, stiff3[...], jac_coefs, False)[0]
    is_fast = lane_tiled(cluster[...]) == 0
    later = [jnp.where(is_fast, repeated[t], second[t]) for t in range(TILES)]
    store_tiles(later_out, later)
    up, down, sideways = picked_traces(
        later, pickers[...], [labels[j : j + 1, :] for j in range(3)], proj3[...]
    )
    for t in range(TILES):
        at = FACE_ROWS * t
        up_out[at : at + FACE_ROWS, :] = up[t]
        down_out[at : at + FACE_ROWS, :] = down[t]
        depth_out[at : at + FACE_ROWS, :] = sideways[t]
    parts = []
    for t in range(TILES):
        parts.append(jnp.concatenate(split(first[t] + later[t]), axis=0))
    moved = mm(
        jnp.concatenate(parts, axis=1).astype(bf16),
        jnp.concatenate(fault_pickers(fault_elem), axis=0),
    )
    own = traces(
        [(moved[0:BASIS], moved[BASIS : 2 * BASIS])], [lane_tiled(fault_proj[...])], proj3[...]
    )[0]
    depth_out[TILES * FACE_ROWS :, :] = own


def final_kernel(
    lower,
    upper,
    shallow,
    deep,
    halo,
    near,
    neigh_coefs,
    flux,
    pre,
    lift3,
    sent,
    strength,
    fault_elem,
    fault_proj,
    even,
    result,
):
    at = TILES * FACE_ROWS
    own = sent[at:, :]
    is_even = even[0:1, :] > 0.5
    side = jnp.where(is_even, 1.0, -1.0)
    other = jnp.where(is_even, deep[at:, :], shallow[at:, :])
    group = iotas(FACE_ROWS, LANES)[1] // WIDE
    mean = 0.5 * (own + other)
    jump = side * (0.5 * (other - own))
    shear = mean + pltpu.roll(jump, 2 * WIDE, 1)
    shear = jnp.where(group < 2, shear, pltpu.roll(shear, 2 * WIDE, 1))
    square = shear * shear
    twin = jnp.where(
        group % 2 == 0, pltpu.roll(square, 3 * WIDE, 1), pltpu.roll(square, WIDE, 1)
    )
    limit = lane_tiled(strength[...])
    factor = limit / jnp.maximum(jnp.sqrt(square + twin), limit)
    traction = shear * factor
    jump = jnp.where(group < 2, traction, side * (traction - shear))
    face = lane_tiled(fault_proj[...]) // 3
    placed = jnp.concatenate([jnp.where(face == f, jump, 0.0) for f in range(FACES)], axis=0)
    spread = lax.dot_general(
        jnp.concatenate(split(placed), axis=0).astype(bf16),
        jnp.concatenate(fault_pickers(fault_elem), axis=0),
        (((1,), (1,)), ((), ())),
        preferred_element_type=f32,
    )
    rows = FACES * FACE_ROWS
    spread = spread[0:rows] + spread[rows : 2 * rows]
    terms = face_terms(lower, upper, shallow, deep, halo, near, neigh_coefs, flux)
    terms = [terms[t] - spread[:, LANES * t : LANES * (t + 1)] for t in range(TILES)]
    new = lifted(pre, terms, lift3)
    for t in range(2):
        result[LANES * t : LANES * (t + 1), :] = new[t].T
    result[2 * LANES : 2 * LANES + WIDE, :] = new[2].T[3 * WIDE : 4 * WIDE, :]


def call(kernel, name, outs, *operands):
    vmem = pl.BlockSpec(memory_space=pltpu.VMEM)
    return pl.pallas_call(
        kernel,
        out_shape=[jax.ShapeDtypeStruct(shape, dtype) for shape, dtype in outs],
        in_specs=[vmem] * len(operands),
        out_specs=[vmem] * len(outs),
        compiler_params=pltpu.CompilerParams(vmem_limit_bytes=40 * 1024 * 1024),
        name=name,
    )(*operands)


def passed_along(message, axis, by):
    length = lax.axis_size(axis)
    pairs = [(i, i + by) for i in range(length) if 0 <= i + by < length]
    return lax.ppermute(message, axis, pairs)


def exchanged(up, down, sideways):
    return (
        passed_along(up, "strike", 1),
        passed_along(down, "strike", -1),
        passed_along(sideways, "depth", 1),
        passed_along(sideways, "depth", -1),
    )


def per_device(
    state_dofs,
    jacobians,
    flux_local,
    flux_neigh,
    stiffness,
    volume,
    face_proj,
    face_lift,
    strength,
    cluster,
    neighbours,
    face_orient,
    strike_sends,
    strike_orient,
    depth_sends,
    depth_orient,
    fault_elem,
    fault_proj,
):
    quant, basis, elems = state_dofs.shape
    state = jnp.transpose(state_dofs, (0, 2, 1)).reshape(quant * elems, basis)
    jac = jnp.transpose(jacobians, (1, 2, 0, 3))
    local = jnp.transpose(flux_local, (1, 2, 0, 3))
    neigh = jnp.transpose(flux_neigh, (1, 2, 0, 3))
    proj = jnp.transpose(face_proj, (0, 2, 1))
    lift = jnp.transpose(face_lift, (1, 0, 2))
    strength, cluster, fault_elem, fault_proj = (
        array.reshape(1, -1) for array in (strength, cluster, fault_elem, fault_proj)
    )
    even = jnp.broadcast_to((1 - lax.axis_index("depth") % 2).astype(f32), (1, LANES))

    full = ((TILES, BASIS, LANES), f32)
    faces = ((TILES, FACES * FACE_ROWS, LANES), f32)
    coefs = ((COEFS, 4, LANES), f32)
    message = ((TILES * FACE_ROWS, LANES), f32)
    longer = ((TILES * FACE_ROWS + FACE_ROWS, LANES), f32)

    (
        base,
        first,
        second,
        jac_coefs,
        stiff3,
        proj3,
        pickers,
        labels,
        up,
        down,
        sideways,
    ) = call(
        send_kernel,
        "first_sends",
        [
            full,
            full,
            full,
            coefs,
            ((3 * BASIS, 3 * BASIS), bf16),
            ((PROJS * FACE_ROWS, 3 * BASIS), bf16),
            ((LANES, 3 * LANES), bf16),
            ((3, LANES), jnp.int32),
            message,
            message,
            message,
        ],
        state,
        jac,
        stiffness,
        proj,
        strike_sends,
        strike_orient,
        depth_sends,
        depth_orient,
    )
    arrived = exchanged(up, down, sideways)
    (
        pre,
        flux,
        near,
        vol3,
        own3,
        local_coefs,
        neigh_coefs,
        near_pickers,
        near_labels,
        halo,
        lift3,
    ) = call(
        prepare_kernel,
        "first_local",
        [
            full,
            faces,
            faces,
            ((3 * BASIS, 3 * BASIS), bf16),
            ((FACES * FACE_ROWS, 3 * BASIS), bf16),
            coefs,
            coefs,
            ((LANES, FACES * LANES), bf16),
            ((FACES, LANES), jnp.int32),
            ((3 * LANES, FACES * LANES), bf16),
            ((BASIS, 3 * FACES * FACE_ROWS), bf16),
        ],
        first,
        base,
        jac_coefs,
        proj3,
        volume,
        proj,
        local,
        neigh,
        lift,
        neighbours,
        face_orient,
    )
    advanced, later, up, down, sideways = call(
        middle_kernel,
        "advance",
        [full, full, message, message, longer],
        *arrived,
        halo,
        near,
        neigh_coefs,
        flux,
        pre,
        lift3,
        first,
        second,
        cluster,
        stiff3,
        jac_coefs,
        pickers,
        labels,
        proj3,
        fault_elem,
        fault_proj,
    )
    arrived = exchanged(up, down, sideways)
    pre, flux, near = call(
        again_kernel,
        "later_local",
        [full, faces, faces],
        later,
        advanced,
        jac_coefs,
        proj3,
        vol3,
        own3,
        local_coefs,
        near_pickers,
        near_labels,
    )
    (result,) = call(
        final_kernel,
        "combine",
        [((quant * elems, basis), f32)],
        *arrived,
        halo,
        near,
        neigh_coefs,
        flux,
        pre,
        lift3,
        sideways,
        strength,
        fault_elem,
        fault_proj,
        even,
    )
    return jnp.transpose(result.reshape(quant, elems, basis), (0, 2, 1))


def solution(mesh):
    spread = ("strike", "depth")
    placed = (
        P(None, None, spread),
        P(None, None, None, spread),
        P(None, None, None, spread),
        P(None, None, None, spread),
        P(),
        P(),
        P(),
        P(),
        P(spread),
        P(spread),
        P(None, spread),
        P(None, spread),
        P(None, spread),
        P(None, spread),
        P(None, spread),
        P(None, spread),
        P(spread),
        P(spread),
    )
    return jax.shard_map(
        per_device,
        mesh=mesh,
        in_specs=placed,
        out_specs=P(None, None, spread),
        check_vma=False,
    )
```

profile of v0, /device:TPU:231, one launch (start us, length us, event | category | flops | bytes accessed | tf_op | source)
XLA Modules:
  0.0 52.8 jit_solution(11700345220068020313)
XLA Ops:
  0.0 0.7 %copy-done.16 = s32[2,16]{1,0:T(2,128)S(1)} copy-done((s32[2,16]{1,0:T(2,128)S(1)}, s32[2,16]{1,0:T(2,128)}, u32[]{:S(2)}) %copy-start.16) | copy-done | bytes 152
  0.7 0.0 copy-done.14
  0.7 0.0 copy-done.15
  0.7 0.0 copy-done.13
  0.7 0.9 %copy-done = f32[12,56,21]{1,2,0:T(8,128)S(1)} copy-done((f32[12,56,21]{1,2,0:T(8,128)S(1)}, f32[12,56,21]{1,2,0:T(8,128)}, u32[]{:S(2)}) %copy-start) | copy-done | bytes 56472
  1.6 0.9 %copy-done.2 = f32[3,9,9,32]{3,0,2,1:T(4,128)S(1)} copy-done((f32[3,9,9,32]{3,0,2,1:T(4,128)S(1)}, f32[3,9,9,32]{3,0,2,1:T(4,128)}, u32[]{:S(2)}) %copy-start.2) | copy-done | bytes 31128
  2.6 0.9 %copy-done.5 = f32[9,56,32]{1,2,0:T(8,128)S(1)} copy-done((f32[9,56,32]{1,2,0:T(8,128)S(1)}, f32[9,56,32]{1,2,0:T(8,128)}, u32[]{:S(2)}) %copy-start.5) | copy-done | bytes 64536
  3.5 0.9 %copy-done.6 = f32[3,56,56]{2,1,0:T(8,128)S(1)} copy-done((f32[3,56,56]{2,1,0:T(8,128)S(1)}, f32[3,56,56]{2,1,0:T(8,128)}, u32[]{:S(2)}) %copy-start.6) | copy-done | bytes 37656
  4.4 2.5 %first_sends.1 = (f32[3,56,128]{2,1,0:T(8,128)S(1)}, f32[3,56,128]{2,1,0:T(8,128)S(1)}, f32[3,56,128]{2,1,0:T(8,128)S(1)}, f32[21,4,128]{2,1,0:T(4,128)S(1)}, bf...) custom-call(f32[288,56]{1,0:T(8,128)S(1)} %bitcast.20, ...), custom_call_target="tpu_custom_call" | custom-call | tf_op jit(solution)/shard_map/first_sends/pallas_call | solution.py:526
  6.8 2.3 %collective-permute-start.2 = (f32[72,128]{1,0:T(8,128)S(1)}, f32[72,128]{1,0:T(8,128)S(1)}, u32[]{:S(2)}, u32[]{:S(2)}) collective-permute-start(f32[72,128]{1,0:T(8,128)S(1)} %get-tuple-element.37), channel_id=1, source_target_pairs={{0,1},{1,2},{2,3},{3,4},{4,5},{5,6},{6,7},{8,9},{9,10},{10,11},{11... | collective-permute-start | bytes 110600 | tf_op jit(solution)/shard_map/ppermute | solution.py:539
  9.1 4.2 %collective-permute-start.3 = (f32[72,128]{1,0:T(8,128)S(1)}, f32[72,128]{1,0:T(8,128)S(1)}, u32[]{:S(2)}, u32[]{:S(2)}) collective-permute-start(f32[72,128]{1,0:T(8,128)S(1)} %get-tuple-element.37), channel_id=1, source_target_pairs={{1,0},{2,1},{3,2},{4,3},{5,4},{6,5},{7,6},{9,8},{10,9},{11,10},{12... | collective-permute-start | bytes 110600 | tf_op jit(solution)/shard_map/ppermute | solution.py:539
  13.3 6.2 %collective-permute-start = (f32[72,128]{1,0:T(8,128)S(1)}, f32[72,128]{1,0:T(8,128)S(1)}, u32[]{:S(2)}, u32[]{:S(2)}) collective-permute-start(f32[72,128]{1,0:T(8,128)S(1)} %get-tuple-element.35), channel_id=1, source_target_pairs={{0,8},{8,16},{16,24},{24,32},{32,40},{40,48},{48,56},{56,64},{64,7... | collective-permute-start | bytes 110600 | tf_op jit(solution)/shard_map/ppermute | solution.py:539
  19.6 1.9 %collective-permute-start.1 = (f32[72,128]{1,0:T(8,128)S(1)}, f32[72,128]{1,0:T(8,128)S(1)}, u32[]{:S(2)}, u32[]{:S(2)}) collective-permute-start(f32[72,128]{1,0:T(8,128)S(1)} %get-tuple-element.36), channel_id=1, source_target_pairs={{8,0},{16,8},{24,16},{32,24},{40,32},{48,40},{56,48},{64,56},{72,6... | collective-permute-start | bytes 110600 | tf_op jit(solution)/shard_map/ppermute | solution.py:539
  21.5 0.0 copy-start.12
  21.5 0.0 copy-start.11
  21.6 0.6 %copy-done.12 = s32[4,32]{1,0:T(4,128)S(1)} copy-done((s32[4,32]{1,0:T(4,128)S(1)}, s32[4,32]{1,0:T(4,128)}, u32[]{:S(2)}) %copy-start.12) | copy-done | bytes 536
  22.2 0.0 copy-done.11
  22.2 0.8 %copy-done.8 = f32[4,21,56]{2,0,1:T(4,128)S(1)} copy-done((f32[4,21,56]{2,0,1:T(4,128)S(1)}, f32[4,21,56]{2,0,1:T(4,128)}, u32[]{:S(2)}) %copy-start.8) | copy-done | bytes 18840
  23.0 1.1 %first_local.1 = (f32[3,56,128]{2,1,0:T(8,128)S(1)}, f32[3,96,128]{2,1,0:T(8,128)S(1)}, f32[3,96,128]{2,1,0:T(8,128)S(1)}, bf16[168,168]{1,0:T(8,128)(2,1)S(1)},...) custom-call(f32[3,56,128]{2,1,0:T(8,128)S(1)} %get-tuple-element.38., ...), custom_call_target="tpu_custom_call" | custom-call | tf_op jit(solution)/shard_map/first_local/pallas_call | solution.py:526
  24.1 4.0 %collective-permute-done.1.upper = f32[72,128]{1,0:T(8,128)S(1)} collective-permute-done((f32[72,128]{1,0:T(8,128)S(1)}, f32[72,128]{1,0:T(8,128)S(1)}, u32[]{:S(2)}, u32[]{:S(2)}) %collective-permute-start.1) | collective-permute-done | bytes 36896 | tf_op jit(solution)/shard_map/ppermute | solution.py:539
  28.2 0.6 %copy-done.9 = s32[32]{0:T(128)S(1)} copy-done((s32[32]{0:T(128)S(1)}, s32[32]{0:T(128)}, u32[]{:S(2)}) %copy-start.9) | copy-done | bytes 152
  28.8 0.0 copy-done.10
  28.9 0.0 copy-done.17
  28.9 3.0 %advance.1 = (f32[3,56,128]{2,1,0:T(8,128)S(1)}, f32[3,56,128]{2,1,0:T(8,128)S(1)}, f32[72,128]{1,0:T(8,128)S(1)}, f32[72,128]{1,0:T(8,128)S(1)}, f32[96,128]{1,0:T(8,128)S(1)}) custom-call(f32[72,128]{1,0:T(8,128)S(1)} %collective-permute-done.lower, f32[72,128]{1,0:T(8,128)S(1)} %collective-permute-done.1.upper, ...), custom_call_target="tpu_custom_call" | custom-call | tf_op jit(solution)/shard_map/advance/pallas_call | solution.py:526
  31.9 1.9 %collective-permute-start.6 = (f32[96,128]{1,0:T(8,128)S(1)}, f32[96,128]{1,0:T(8,128)S(1)}, u32[]{:S(2)}, u32[]{:S(2)}) collective-permute-start(f32[96,128]{1,0:T(8,128)S(1)} %get-tuple-element.54.sent), channel_id=1, source_target_pairs={{0,1},{1,2},{2,3},{3,4},{4,5},{5,6},{6,7},{8,9},{9,10},{10,11},{11... | collective-permute-start | bytes 147464 | tf_op jit(solution)/shard_map/ppermute | solution.py:539
  33.9 4.6 %collective-permute-start.7 = (f32[96,128]{1,0:T(8,128)S(1)}, f32[96,128]{1,0:T(8,128)S(1)}, u32[]{:S(2)}, u32[]{:S(2)}) collective-permute-start(f32[96,128]{1,0:T(8,128)S(1)} %get-tuple-element.54.sent), channel_id=1, source_target_pairs={{1,0},{2,1},{3,2},{4,3},{5,4},{6,5},{7,6},{9,8},{10,9},{11,10},{12... | collective-permute-start | bytes 147464 | tf_op jit(solution)/shard_map/ppermute | solution.py:539
  38.4 3.5 %collective-permute-start.4 = (f32[72,128]{1,0:T(8,128)S(1)}, f32[72,128]{1,0:T(8,128)S(1)}, u32[]{:S(2)}, u32[]{:S(2)}) collective-permute-start(f32[72,128]{1,0:T(8,128)S(1)} %get-tuple-element.52), channel_id=1, source_target_pairs={{0,8},{8,16},{16,24},{24,32},{32,40},{40,48},{48,56},{56,64},{64,7... | collective-permute-start | bytes 110600 | tf_op jit(solution)/shard_map/ppermute | solution.py:539
  41.9 1.9 %collective-permute-start.5 = (f32[72,128]{1,0:T(8,128)S(1)}, f32[72,128]{1,0:T(8,128)S(1)}, u32[]{:S(2)}, u32[]{:S(2)}) collective-permute-start(f32[72,128]{1,0:T(8,128)S(1)} %get-tuple-element.53), channel_id=1, source_target_pairs={{8,0},{16,8},{24,16},{32,24},{40,32},{48,40},{56,48},{64,56},{72,6... | collective-permute-start | bytes 110600 | tf_op jit(solution)/shard_map/ppermute | solution.py:539
  43.9 0.7 %later_local.1 = (f32[3,56,128]{2,1,0:T(8,128)S(1)}, f32[3,96,128]{2,1,0:T(8,128)S(1)}, f32[3,96,128]{2,1,0:T(8,128)S(1)}) custom-call(f32[3,56,128]{2,1,0:T(8,128)S(1)} %get-tuple-element.55.values, f32[3,56,128]{2,1,0:T(8,128)S(1)} %get-tuple-element.56.base, f32[21,4,128]{2,1,0:T(4,128)S(1)} %get-tuple-element.40.jac_coefs, ...), custom_call_target="tpu_custom_call" | custom-call | tf_op jit(solution)/shard_map/later_local/pallas_call | solution.py:526
  44.6 6.0 %collective-permute-done.5.upper = f32[72,128]{1,0:T(8,128)S(1)} collective-permute-done((f32[72,128]{1,0:T(8,128)S(1)}, f32[72,128]{1,0:T(8,128)S(1)}, u32[]{:S(2)}, u32[]{:S(2)}) %collective-permute-start.5) | collective-permute-done | bytes 36896 | tf_op jit(solution)/shard_map/ppermute | solution.py:539
  50.6 0.6 %copy-done.18 = f32[32]{0:T(128)S(1)} copy-done((f32[32]{0:T(128)S(1)}, f32[32]{0:T(128)}, u32[]{:S(2)}) %copy-start.18) | copy-done | bytes 152
  51.2 1.6 %combine.1 = f32[288,56]{1,0:T(8,128)} custom-call(f32[72,128]{1,0:T(8,128)S(1)} %collective-permute-done.4.lower, f32[72,128]{1,0:T(8,128)S(1)} %collective-permute-done.5.upper, f32[96,128]{1,0:T(8,128)S(1)} %collective-permute-done.6.shallow, f32[96,128]{1,0:T(8,128)S(1)} %collective-permute-done.7.deep, bf16[384,512]{1,0:T(8,128)(2,1)S(1)} %get-tuple-element.42.halo, ...), custom_call_target="tpu_custom_call" | custom-call | tf_op jit(solution)/shard_map/combine/pallas_call | solution.py:526
  (28 shorter events, 0.1 us)
Async XLA Ops:
  0.0 0.7 %copy-start.16 = (s32[2,16]{1,0:T(2,128)S(1)}, s32[2,16]{1,0:T(2,128)}, u32[]{:S(2)}) copy-start(s32[2,16]{1,0:T(2,128)} %depth_orient.1) | copy-start | bytes 388
  0.0 0.7 %copy-start.14 = (s32[2,32]{1,0:T(2,128)S(1)}, s32[2,32]{1,0:T(2,128)}, u32[]{:S(2)}) copy-start(s32[2,32]{1,0:T(2,128)} %strike_orient.1) | copy-start | bytes 772
  0.0 0.7 %copy-start.15 = (s32[2,16]{1,0:T(2,128)S(1)}, s32[2,16]{1,0:T(2,128)}, u32[]{:S(2)}) copy-start(s32[2,16]{1,0:T(2,128)} %depth_sends.1) | copy-start | bytes 388
  0.0 0.7 %copy-start.13 = (s32[2,32]{1,0:T(2,128)S(1)}, s32[2,32]{1,0:T(2,128)}, u32[]{:S(2)}) copy-start(s32[2,32]{1,0:T(2,128)} %strike_sends.1) | copy-start | bytes 772
  0.7 0.9 %copy-start = (f32[12,56,21]{1,2,0:T(8,128)S(1)}, f32[12,56,21]{1,2,0:T(8,128)}, u32[]{:S(2)}) copy-start(f32[12,56,21]{1,2,0:T(8,128)} %param.24) | copy-start | bytes 169348
  1.6 0.9 %copy-start.2 = (f32[3,9,9,32]{3,0,2,1:T(4,128)S(1)}, f32[3,9,9,32]{3,0,2,1:T(4,128)}, u32[]{:S(2)}) copy-start(f32[3,9,9,32]{3,0,2,1:T(4,128)} %param.19) | copy-start | bytes 93316
  2.6 0.9 %copy-start.5 = (f32[9,56,32]{1,2,0:T(8,128)S(1)}, f32[9,56,32]{1,2,0:T(8,128)}, u32[]{:S(2)}) copy-start(f32[9,56,32]{1,2,0:T(8,128)} %param.18) | copy-start | bytes 193540
  3.5 0.9 %copy-start.6 = (f32[3,56,56]{2,1,0:T(8,128)S(1)}, f32[3,56,56]{2,1,0:T(8,128)}, u32[]{:S(2)}) copy-start(f32[3,56,56]{2,1,0:T(8,128)} %stiffness.1) | copy-start | bytes 112900
  4.4 17.2 %copy-start.1 = (f32[12,56,21]{1,2,0:T(8,128)S(1)}, f32[12,56,21]{1,2,0:T(8,128)}, u32[]{:S(2)}) copy-start(f32[12,56,21]{1,2,0:T(8,128)} %param.24) | copy-start | bytes 169348
  4.4 17.2 %copy-start.3 = (f32[4,9,9,32]{3,0,2,1:T(4,128)S(1)}, f32[4,9,9,32]{3,0,2,1:T(4,128)}, u32[]{:S(2)}) copy-start(f32[4,9,9,32]{3,0,2,1:T(4,128)} %param.20) | copy-start | bytes 124420
  4.4 17.2 %copy-start.4 = (f32[4,9,9,32]{3,0,2,1:T(4,128)S(1)}, f32[4,9,9,32]{3,0,2,1:T(4,128)}, u32[]{:S(2)}) copy-start(f32[4,9,9,32]{3,0,2,1:T(4,128)} %param.21) | copy-start | bytes 124420
  4.4 17.2 %copy-start.7 = (f32[3,56,56]{2,1,0:T(8,128)S(1)}, f32[3,56,56]{2,1,0:T(8,128)}, u32[]{:S(2)}) copy-start(f32[3,56,56]{2,1,0:T(8,128)} %volume.1) | copy-start | bytes 112900
  6.8 17.3 %collective-permute-start.2 = (f32[72,128]{1,0:T(8,128)S(1)}, f32[72,128]{1,0:T(8,128)S(1)}, u32[]{:S(2)}, u32[]{:S(2)}) collective-permute-start(f32[72,128]{1,0:T(8,128)S(1)} %get-tuple-element.37), channel_id=1, source_target_pairs={{0,1},{1,2},{2,3},{3,4},{4,5},{5,6},{6,7},{8,9},{9,10},{10,11},{11... | collective-permute-start | bytes 110600 | tf_op jit(solution)/shard_map/ppermute | solution.py:539
  9.1 15.0 %collective-permute-start.3 = (f32[72,128]{1,0:T(8,128)S(1)}, f32[72,128]{1,0:T(8,128)S(1)}, u32[]{:S(2)}, u32[]{:S(2)}) collective-permute-start(f32[72,128]{1,0:T(8,128)S(1)} %get-tuple-element.37), channel_id=1, source_target_pairs={{1,0},{2,1},{3,2},{4,3},{5,4},{6,5},{7,6},{9,8},{10,9},{11,10},{12... | collective-permute-start | bytes 110600 | tf_op jit(solution)/shard_map/ppermute | solution.py:539
  13.3 10.8 %collective-permute-start = (f32[72,128]{1,0:T(8,128)S(1)}, f32[72,128]{1,0:T(8,128)S(1)}, u32[]{:S(2)}, u32[]{:S(2)}) collective-permute-start(f32[72,128]{1,0:T(8,128)S(1)} %get-tuple-element.35), channel_id=1, source_target_pairs={{0,8},{8,16},{16,24},{24,32},{32,40},{40,48},{48,56},{56,64},{64,7... | collective-permute-start | bytes 110600 | tf_op jit(solution)/shard_map/ppermute | solution.py:539
  19.6 8.6 %collective-permute-start.1 = (f32[72,128]{1,0:T(8,128)S(1)}, f32[72,128]{1,0:T(8,128)S(1)}, u32[]{:S(2)}, u32[]{:S(2)}) collective-permute-start(f32[72,128]{1,0:T(8,128)S(1)} %get-tuple-element.36), channel_id=1, source_target_pairs={{8,0},{16,8},{24,16},{32,24},{40,32},{48,40},{56,48},{64,56},{72,6... | collective-permute-start | bytes 110600 | tf_op jit(solution)/shard_map/ppermute | solution.py:539
  21.5 0.7 %copy-start.12 = (s32[4,32]{1,0:T(4,128)S(1)}, s32[4,32]{1,0:T(4,128)}, u32[]{:S(2)}) copy-start(s32[4,32]{1,0:T(4,128)} %face_orient.1) | copy-start | bytes 1540
  21.5 0.7 %copy-start.11 = (s32[4,32]{1,0:T(4,128)S(1)}, s32[4,32]{1,0:T(4,128)}, u32[]{:S(2)}) copy-start(s32[4,32]{1,0:T(4,128)} %neighbours.1) | copy-start | bytes 1540
  22.2 0.8 %copy-start.8 = (f32[4,21,56]{2,0,1:T(4,128)S(1)}, f32[4,21,56]{2,0,1:T(4,128)}, u32[]{:S(2)}) copy-start(f32[4,21,56]{2,0,1:T(4,128)} %param.25) | copy-start | bytes 56452
  28.2 0.7 %copy-start.9 = (s32[32]{0:T(128)S(1)}, s32[32]{0:T(128)}, u32[]{:S(2)}) copy-start(s32[32]{0:T(128)} %param.34) | copy-start | bytes 388
  28.2 0.7 %copy-start.10 = (s32[32]{0:T(128)S(1)}, s32[32]{0:T(128)}, u32[]{:S(2)}) copy-start(s32[32]{0:T(128)} %param.35) | copy-start | bytes 388
  28.2 0.7 %copy-start.17 = (s32[32]{0:T(128)S(1)}, s32[32]{0:T(128)}, u32[]{:S(2)}) copy-start(s32[32]{0:T(128)} %param.27) | copy-start | bytes 388
  31.9 18.6 %collective-permute-start.6 = (f32[96,128]{1,0:T(8,128)S(1)}, f32[96,128]{1,0:T(8,128)S(1)}, u32[]{:S(2)}, u32[]{:S(2)}) collective-permute-start(f32[96,128]{1,0:T(8,128)S(1)} %get-tuple-element.54.sent), channel_id=1, source_target_pairs={{0,1},{1,2},{2,3},{3,4},{4,5},{5,6},{6,7},{8,9},{9,10},{10,11},{11... | collective-permute-start | bytes 147464 | tf_op jit(solution)/shard_map/ppermute | solution.py:539
  33.9 16.7 %collective-permute-start.7 = (f32[96,128]{1,0:T(8,128)S(1)}, f32[96,128]{1,0:T(8,128)S(1)}, u32[]{:S(2)}, u32[]{:S(2)}) collective-permute-start(f32[96,128]{1,0:T(8,128)S(1)} %get-tuple-element.54.sent), channel_id=1, source_target_pairs={{1,0},{2,1},{3,2},{4,3},{5,4},{6,5},{7,6},{9,8},{10,9},{11,10},{12... | collective-permute-start | bytes 147464 | tf_op jit(solution)/shard_map/ppermute | solution.py:539
  38.4 6.1 %collective-permute-start.4 = (f32[72,128]{1,0:T(8,128)S(1)}, f32[72,128]{1,0:T(8,128)S(1)}, u32[]{:S(2)}, u32[]{:S(2)}) collective-permute-start(f32[72,128]{1,0:T(8,128)S(1)} %get-tuple-element.52), channel_id=1, source_target_pairs={{0,8},{8,16},{16,24},{24,32},{32,40},{40,48},{48,56},{56,64},{64,7... | collective-permute-start | bytes 110600 | tf_op jit(solution)/shard_map/ppermute | solution.py:539
  41.9 8.6 %collective-permute-start.5 = (f32[72,128]{1,0:T(8,128)S(1)}, f32[72,128]{1,0:T(8,128)S(1)}, u32[]{:S(2)}, u32[]{:S(2)}) collective-permute-start(f32[72,128]{1,0:T(8,128)S(1)} %get-tuple-element.53), channel_id=1, source_target_pairs={{8,0},{16,8},{24,16},{32,24},{40,32},{48,40},{56,48},{64,56},{72,6... | collective-permute-start | bytes 110600 | tf_op jit(solution)/shard_map/ppermute | solution.py:539
  50.5 0.7 %copy-start.18 = (f32[32]{0:T(128)S(1)}, f32[32]{0:T(128)}, u32[]{:S(2)}) copy-start(f32[32]{0:T(128)} %param.26) | copy-start | bytes 388
where the time goes:
time: 53.3 us; the launch traced here: 52.8 us
  starting transfers between devices  26.6 us (50%)
  waiting for transfers between devices  10 us (19%)
  Pallas kernels  8.89 us (17%)
  local copies, waits for them, and re-layouts  7.11 us (13%)
    ppermute x8, starting transfers between devices, passed_along(): return lax.ppermute(message, axis, pairs)  26.6 us
    ppermute x8, waiting for transfers between devices, passed_along(): return lax.ppermute(message, axis, pairs)  10 us
    pallas_call x5, Pallas kernels, call(): pl.pallas_call(kernel, out_shape=[jax.ShapeDtypeStruct(shape, dtype) for...  8.89 us
    unnamed x38, local copies, waits for them, and re-layouts  7.11 us
  transfers between devices with their start and end apart: 8, of which 2 were waited for; matrix products, arithmetic and copies ran while one was open for 0% of the time, Pallas kernels for 3%

commit v1 on v0

--- a/solution.py
+++ b/solution.py
@@ -17,6 +17,7 @@
 TILES = 3
 COEFS = 21
 CHUNKS = ((0, 32), (32, 24))
+FAULT_ROW, CLUSTER_ROW, NEAR_ROW, ROWS = 0, 1, 2, 8
 
 fast_step = 0.5
 f32 = jnp.float32
@@ -186,63 +187,106 @@
         ref[t] = tiles[t]
 
 
+def weights_kernel(stiffness, stiff3_out):
+    stiff3_out[...] = left3(jnp.concatenate([-stiffness[d].T for d in range(3)], axis=0))
+
+
+def plan_sends(strike_sends, strike_orient, depth_sends, depth_orient, pickers_out, rows_out):
+    strike_odd = lax.axis_index("strike") % 2
+    depth_odd = lax.axis_index("depth") % 2
+
+    def either(table, odd):
+        twin = table[1:2, :] * (1 - odd) + table[0:1, :] * odd
+        across = table[0:1, :] * (1 - odd) + table[1:2, :] * odd
+        return twin, across
+
+    def jobs(strike, depth):
+        twin, across = either(strike, strike_odd)
+        return [
+            lane_tiled(twin),
+            lane_tiled(across),
+            lane_tiled(jnp.concatenate(either(depth, depth_odd), axis=1)),
+        ]
+
+    elements = jobs(strike_sends, depth_sends)
+    labels = jobs(strike_orient, depth_orient)
+    for j in range(3):
+        pickers_out[:, LANES * j : LANES * (j + 1)] = picking(elements[j])
+        rows_out[j : j + 1, :] = labels[j]
+
+
+def plan_faces(neighbours, face_orient, near_pickers_out, halo_out, marks_out):
+    strike_odd = lax.axis_index("strike") % 2
+    depth_odd = lax.axis_index("depth") % 2
+    sublane, lane = iotas(LANES, LANES)
+    group = (lane // WIDE) * WIDE
+    for f in range(FACES):
+        behind = lane_tiled(neighbours[f : f + 1, :])
+        marks_out[NEAR_ROW + f : NEAR_ROW + f + 1, :] = lane_tiled(face_orient[f : f + 1, :])
+        columns = slice(LANES * f, LANES * (f + 1))
+        local = jnp.where(behind < WIDE, behind, -4 * LANES)
+        near_pickers_out[:, columns] = one_hot(sublane == local + group)
+        strike_slot = (behind - WIDE) ^ (WIDE * (1 - strike_odd))
+        depth_slot = (behind - 3 * WIDE) ^ ((WIDE // 2) * (1 - depth_odd))
+        for block, slot in enumerate((strike_slot, strike_slot - WIDE, depth_slot)):
+            if block < 2:
+                inside = (behind >= WIDE) & (behind < 3 * WIDE)
+            else:
+                inside = (behind >= 3 * WIDE) & (behind < 4 * WIDE)
+            inside = inside & (slot >= 0) & (slot < WIDE)
+            slot = jnp.where(inside, slot, -4 * LANES)
+            halo_out[LANES * block : LANES * (block + 1), columns] = one_hot(
+                sublane == slot + group
+            )
+
+
 def send_kernel(
     state,
     jacobians,
-    stiffness,
     face_proj,
     strike_sends,
     strike_orient,
     depth_sends,
     depth_orient,
+    stiff3,
     base_out,
     first_out,
     second_out,
     jac_coefs,
-    stiff3_out,
     proj3_out,
     pickers_out,
-    labels_out,
-    up_out,
-    down_out,
+    rows_out,
+    twin_out,
+    across_out,
     depth_out,
 ):
     build_coefs(jacobians, jac_coefs)
-    stiff3 = left3(jnp.concatenate([-stiffness[d].T for d in range(3)], axis=0))
+    plan_sends(strike_sends, strike_orient, depth_sends, depth_orient, pickers_out, rows_out)
     tiles = [state[LANES * t : LANES * (t + 1), :].T for t in range(2)]
     last = state[2 * LANES : 2 * LANES + WIDE, :]
     tiles.append(jnp.concatenate([last] * 4, axis=0).T)
     store_tiles(base_out, tiles)
-    first, second = integrals(tiles, stiff3, jac_coefs, True)
+    first, second = integrals(tiles, stiff3[...], jac_coefs, True)
     store_tiles(first_out, first)
     store_tiles(second_out, second)
     margin = jnp.zeros((FACE_ROWS - FACE_BASIS, BASIS), f32)
     proj3 = left3(
         jnp.concatenate([piece for m in range(PROJS) for piece in (face_proj[m], margin)], axis=0)
     )
-    stiff3_out[...] = stiff3
     proj3_out[...] = proj3
-
-    def jobs(strike, depth):
-        return [
-            lane_tiled(strike[1:2, :]),
-            lane_tiled(strike[0:1, :]),
-            lane_tiled(jnp.concatenate([depth[1:2, :], depth[0:1, :]], axis=1)),
-        ]
-
-    pickers = jnp.concatenate(
-        [picking(elements) for elements in jobs(strike_sends, depth_sends)], axis=1
-    )
-    labels = jobs(strike_orient, depth_orient)
-    pickers_out[...] = pickers
-    for j in range(3):
-        labels_out[j : j + 1, :] = labels[j]
-    up, down, sideways = picked_traces(first, pickers, labels, proj3)
-    for t in range(TILES):
-        at = FACE_ROWS * t
-        up_out[at : at + FACE_ROWS, :] = up[t]
-        down_out[at : at + FACE_ROWS, :] = down[t]
-        depth_out[at : at + FACE_ROWS, :] = sideways[t]
+    send(first, pickers_out, rows_out, proj3, twin_out, across_out, depth_out)
+
+
+def send(values, pickers, rows, proj3, *outs):
+    found = picked_traces(
+        values,
+        pickers[...],
+        [rows[j : j + 1, :] for j in range(3)],
+        proj3,
+    )
+    for out, pieces in zip(outs, found):
+        for t in range(TILES):
+            out[FACE_ROWS * t : FACE_ROWS * (t + 1), :] = pieces[t]
 
 
 def local_part(values, base, vol3, jac_coefs, own3, local_coefs, pickers, labels, proj3, outs):
@@ -266,18 +310,26 @@
             near_out[t, at : at + FACE_ROWS, :] = near[f][t]
 
 
+def near_labels(marks):
+    return [marks[NEAR_ROW + f : NEAR_ROW + f + 1, :] for f in range(FACES)]
+
+
 def prepare_kernel(
     values,
     base,
     jac_coefs,
     proj3,
+    neighbours,
+    face_orient,
     volume,
     face_proj,
     flux_local,
     flux_neigh,
     face_lift,
-    neighbours,
-    face_orient,
+    cluster,
+    strength,
+    fault_elem,
+    fault_proj,
     pre_out,
     flux_out,
     near_out,
@@ -285,11 +337,20 @@
     own3_out,
     local_coefs,
     neigh_coefs,
-    pickers_out,
-    labels_out,
+    lift3_out,
+    near_pickers_out,
     halo_out,
-    lift3_out,
+    fault_pickers_out,
+    marks_out,
+    reals_out,
 ):
+    depth_odd = lax.axis_index("depth") % 2
+    fault_pickers_out[...] = jnp.concatenate(fault_pickers(fault_elem), axis=0)
+    marks_out[FAULT_ROW : FAULT_ROW + 1, :] = lane_tiled(fault_proj[...])
+    marks_out[CLUSTER_ROW : CLUSTER_ROW + 1, :] = lane_tiled(cluster[...])
+    reals_out[0:1, :] = lane_tiled(strength[...])
+    reals_out[1:2, :] = jnp.where(iotas(1, LANES)[1] * 0 + depth_odd == 0, 1.0, -1.0)
+    plan_faces(neighbours, face_orient, near_pickers_out, halo_out, marks_out)
     vol3 = left3(jnp.concatenate([volume[d].T for d in range(3)], axis=0))
     vol3_out[...] = vol3
     margin = jnp.zeros((FACE_ROWS - FACE_BASIS, BASIS), f32)
@@ -304,23 +365,6 @@
             [piece for f in range(FACES) for piece in (face_lift[:, f, :], margin)], axis=0
         ).T
     )
-    behind = [lane_tiled(neighbours[f : f + 1, :]) for f in range(FACES)]
-    labels = [lane_tiled(face_orient[f : f + 1, :]) for f in range(FACES)]
-    sublane, lane = iotas(LANES, LANES)
-    group = (lane // WIDE) * WIDE
-    pickers = []
-    for f in range(FACES):
-        labels_out[f : f + 1, :] = labels[f]
-        local = jnp.where(behind[f] < WIDE, behind[f], -4 * LANES)
-        pickers.append(one_hot(sublane == local + group))
-        for block in range(3):
-            slot = behind[f] - WIDE * (block + 1)
-            slot = jnp.where((slot >= 0) & (slot < WIDE), slot, -4 * LANES)
-            halo_out[LANES * block : LANES * (block + 1), LANES * f : LANES * (f + 1)] = one_hot(
-                sublane == slot + group
-            )
-    pickers = jnp.concatenate(pickers, axis=1)
-    pickers_out[...] = pickers
     local_part(
         load_tiles(values),
         load_tiles(base),
@@ -328,8 +372,8 @@
         jac_coefs,
         own3,
         local_coefs,
-        pickers,
-        labels,
+        near_pickers_out[...],
+        near_labels(marks_out),
         proj3[...],
         (pre_out, flux_out, near_out),
     )
@@ -340,11 +384,11 @@
     base,
     jac_coefs,
     proj3,
+    pickers,
+    marks,
     vol3,
     own3,
     local_coefs,
-    pickers,
-    labels,
     pre_out,
     flux_out,
     near_out,
@@ -357,19 +401,19 @@
         own3[...],
         local_coefs,
         pickers[...],
-        [labels[f : f + 1, :] for f in range(FACES)],
+        near_labels(marks),
         proj3[...],
         (pre_out, flux_out, near_out),
     )
 
 
-def face_terms(lower, upper, shallow, deep, halo, near, neigh_coefs, flux):
+def face_terms(twin, across, pair, beyond, halo, near, neigh_coefs, flux):
     rows = TILES * FACE_ROWS
     lane = iotas(rows, LANES)[1]
     blocks = [
-        lower[...],
-        upper[...],
-        jnp.where(lane % WIDE < WIDE // 2, shallow[0:rows, :], deep[0:rows, :]),
+        twin[...],
+        across[...],
+        jnp.where(lane % WIDE < WIDE // 2, pair[0:rows, :], beyond[...]),
     ]
     parts = [split(block) for block in blocks]
     left = jnp.concatenate(
@@ -413,10 +457,10 @@
 
 
 def middle_kernel(
-    lower,
-    upper,
-    shallow,
-    deep,
+    twin,
+    across,
+    pair,
+    beyond,
     halo,
     near,
     neigh_coefs,
@@ -425,53 +469,46 @@
     lift3,
     first,
     second,
-    cluster,
     stiff3,
     jac_coefs,
     pickers,
-    labels,
+    rows,
     proj3,
-    fault_elem,
-    fault_proj,
+    fault_picker,
+    marks,
     advanced_out,
     later_out,
-    up_out,
-    down_out,
+    twin_out,
+    across_out,
     depth_out,
+    pair_out,
 ):
-    terms = face_terms(lower, upper, shallow, deep, halo, near, neigh_coefs, flux)
+    terms = face_terms(twin, across, pair, beyond, halo, near, neigh_coefs, flux)
     advanced = lifted(pre, terms, lift3)
     store_tiles(advanced_out, advanced)
     repeated = integrals(advanced, stiff3[...], jac_coefs, False)[0]
-    is_fast = lane_tiled(cluster[...]) == 0
+    is_fast = marks[CLUSTER_ROW : CLUSTER_ROW + 1, :] == 0
     later = [jnp.where(is_fast, repeated[t], second[t]) for t in range(TILES)]
     store_tiles(later_out, later)
-    up, down, sideways = picked_traces(
-        later, pickers[...], [labels[j : j + 1, :] for j in range(3)], proj3[...]
-    )
-    for t in range(TILES):
-        at = FACE_ROWS * t
-        up_out[at : at + FACE_ROWS, :] = up[t]
-        down_out[at : at + FACE_ROWS, :] = down[t]
-        depth_out[at : at + FACE_ROWS, :] = sideways[t]
+    send(later, pickers, rows, proj3[...], twin_out, across_out, depth_out)
     parts = []
     for t in range(TILES):
         parts.append(jnp.concatenate(split(first[t] + later[t]), axis=0))
-    moved = mm(
-        jnp.concatenate(parts, axis=1).astype(bf16),
-        jnp.concatenate(fault_pickers(fault_elem), axis=0),
-    )
+    moved = mm(jnp.concatenate(parts, axis=1).astype(bf16), fault_picker[...])
     own = traces(
-        [(moved[0:BASIS], moved[BASIS : 2 * BASIS])], [lane_tiled(fault_proj[...])], proj3[...]
+        [(moved[0:BASIS], moved[BASIS : 2 * BASIS])],
+        [marks[FAULT_ROW : FAULT_ROW + 1, :]],
+        proj3[...],
     )[0]
-    depth_out[TILES * FACE_ROWS :, :] = own
+    pair_out[0 : TILES * FACE_ROWS, :] = depth_out[...]
+    pair_out[TILES * FACE_ROWS :, :] = own
 
 
 def final_kernel(
-    lower,
-    upper,
-    shallow,
-    deep,
+    twin,
+    across,
+    pair,
+    beyond,
     halo,
     near,
     neigh_coefs,
@@ -479,46 +516,47 @@
     pre,
     lift3,
     sent,
-    strength,
-    fault_elem,
-    fault_proj,
-    even,
+    marks,
+    reals,
+    fault_picker,
     result,
 ):
     at = TILES * FACE_ROWS
     own = sent[at:, :]
-    is_even = even[0:1, :] > 0.5
-    side = jnp.where(is_even, 1.0, -1.0)
-    other = jnp.where(is_even, deep[at:, :], shallow[at:, :])
+    other = pair[at:, :]
+    limit = reals[0:1, :]
+    side = reals[1:2, :]
     group = iotas(FACE_ROWS, LANES)[1] // WIDE
     mean = 0.5 * (own + other)
     jump = side * (0.5 * (other - own))
     shear = mean + pltpu.roll(jump, 2 * WIDE, 1)
     shear = jnp.where(group < 2, shear, pltpu.roll(shear, 2 * WIDE, 1))
     square = shear * shear
-    twin = jnp.where(
+    mate = jnp.where(
         group % 2 == 0, pltpu.roll(square, 3 * WIDE, 1), pltpu.roll(square, WIDE, 1)
     )
-    limit = lane_tiled(strength[...])
-    factor = limit / jnp.maximum(jnp.sqrt(square + twin), limit)
+    factor = limit / jnp.maximum(jnp.sqrt(square + mate), limit)
     traction = shear * factor
     jump = jnp.where(group < 2, traction, side * (traction - shear))
-    face = lane_tiled(fault_proj[...]) // 3
+    face = marks[FAULT_ROW : FAULT_ROW + 1, :] // 3
     placed = jnp.concatenate([jnp.where(face == f, jump, 0.0) for f in range(FACES)], axis=0)
     spread = lax.dot_general(
         jnp.concatenate(split(placed), axis=0).astype(bf16),
-        jnp.concatenate(fault_pickers(fault_elem), axis=0),
+        fault_picker[...],
         (((1,), (1,)), ((), ())),
         preferred_element_type=f32,
     )
-    rows = FACES * FACE_ROWS
-    spread = spread[0:rows] + spread[rows : 2 * rows]
-    terms = face_terms(lower, upper, shallow, deep, halo, near, neigh_coefs, flux)
+    count = FACES * FACE_ROWS
+    spread = spread[0:count] + spread[count : 2 * count]
+    terms = face_terms(twin, across, pair, beyond, halo, near, neigh_coefs, flux)
     terms = [terms[t] - spread[:, LANES * t : LANES * (t + 1)] for t in range(TILES)]
     new = lifted(pre, terms, lift3)
     for t in range(2):
         result[LANES * t : LANES * (t + 1), :] = new[t].T
     result[2 * LANES : 2 * LANES + WIDE, :] = new[2].T[3 * WIDE : 4 * WIDE, :]
+
+
+COSTS = dict(weights=100000, first_sends=8, first_local=4, advance=8, later_local=4, combine=4)
 
 
 def call(kernel, name, outs, *operands):
@@ -529,23 +567,30 @@
         in_specs=[vmem] * len(operands),
         out_specs=[vmem] * len(outs),
         compiler_params=pltpu.CompilerParams(vmem_limit_bytes=40 * 1024 * 1024),
+        cost_estimate=pl.CostEstimate(
+            flops=COSTS[name] * 10**6, bytes_accessed=COSTS[name] * 10**6, transcendentals=0
+        ),
         name=name,
     )(*operands)
 
 
-def passed_along(message, axis, by):
+def with_twin(message, axis):
     length = lax.axis_size(axis)
-    pairs = [(i, i + by) for i in range(length) if 0 <= i + by < length]
+    return lax.ppermute(message, axis, [(i, i ^ 1) for i in range(length)])
+
+
+def with_other_side(message, axis):
+    length = lax.axis_size(axis)
+    pairs = [(i, (i - 1 ^ 1) + 1) for i in range(1, length - 1)]
     return lax.ppermute(message, axis, pairs)
 
 
-def exchanged(up, down, sideways):
-    return (
-        passed_along(up, "strike", 1),
-        passed_along(down, "strike", -1),
-        passed_along(sideways, "depth", 1),
-        passed_along(sideways, "depth", -1),
-    )
+def exchanged(twin, across, pair, beyond):
+    pair = with_twin(pair, "depth")
+    beyond = with_other_side(beyond, "depth")
+    across = with_other_side(across, "strike")
+    twin = with_twin(twin, "strike")
+    return twin, across, pair, beyond
 
 
 def per_device(
@@ -578,7 +623,6 @@
     strength, cluster, fault_elem, fault_proj = (
         array.reshape(1, -1) for array in (strength, cluster, fault_elem, fault_proj)
     )
-    even = jnp.broadcast_to((1 - lax.axis_index("depth") % 2).astype(f32), (1, LANES))
 
     full = ((TILES, BASIS, LANES), f32)
     faces = ((TILES, FACES * FACE_ROWS, LANES), f32)
@@ -586,19 +630,10 @@
     message = ((TILES * FACE_ROWS, LANES), f32)
     longer = ((TILES * FACE_ROWS + FACE_ROWS, LANES), f32)
 
-    (
-        base,
-        first,
-        second,
-        jac_coefs,
-        stiff3,
-        proj3,
-        pickers,
-        labels,
-        up,
-        down,
-        sideways,
-    ) = call(
+    (stiff3,) = call(
+        weights_kernel, "weights", [((3 * BASIS, 3 * BASIS), bf16)], stiffness
+    )
+    base, first, second, jac_coefs, proj3, pickers, rows, twin, across, sideways = call(
         send_kernel,
         "first_sends",
         [
@@ -606,37 +641,24 @@
             full,
             full,
             coefs,
-            ((3 * BASIS, 3 * BASIS), bf16),
             ((PROJS * FACE_ROWS, 3 * BASIS), bf16),
             ((LANES, 3 * LANES), bf16),
-            ((3, LANES), jnp.int32),
+            ((ROWS, LANES), jnp.int32),
             message,
             message,
             message,
         ],
         state,
         jac,
-        stiffness,
         proj,
         strike_sends,
         strike_orient,
         depth_sends,
         depth_orient,
-    )
-    arrived = exchanged(up, down, sideways)
-    (
-        pre,
-        flux,
-        near,
-        vol3,
-        own3,
-        local_coefs,
-        neigh_coefs,
-        near_pickers,
-        near_labels,
-        halo,
-        lift3,
-    ) = call(
+        stiff3,
+    )
+    arrived = exchanged(twin, across, sideways, sideways)
+    pre, flux, near, vol3, own3, local_coefs, neigh_coefs, *rest = call(
         prepare_kernel,
         "first_local",
         [
@@ -647,27 +669,34 @@
             ((FACES * FACE_ROWS, 3 * BASIS), bf16),
             coefs,
             coefs,
+            ((BASIS, 3 * FACES * FACE_ROWS), bf16),
             ((LANES, FACES * LANES), bf16),
-            ((FACES, LANES), jnp.int32),
             ((3 * LANES, FACES * LANES), bf16),
-            ((BASIS, 3 * FACES * FACE_ROWS), bf16),
+            ((TILES * LANES, LANES), bf16),
+            ((ROWS, LANES), jnp.int32),
+            ((8, LANES), f32),
         ],
         first,
         base,
         jac_coefs,
         proj3,
+        neighbours,
+        face_orient,
         volume,
         proj,
         local,
         neigh,
         lift,
-        neighbours,
-        face_orient,
-    )
-    advanced, later, up, down, sideways = call(
+        cluster,
+        strength,
+        fault_elem,
+        fault_proj,
+    )
+    lift3, near_pickers, halo, fault_picker, marks, reals = rest
+    advanced, later, twin, across, sideways, pair = call(
         middle_kernel,
         "advance",
-        [full, full, message, message, longer],
+        [full, full, message, message, message, longer],
         *arrived,
         halo,
         near,
@@ -677,16 +706,15 @@
         lift3,
         first,
         second,
-        cluster,
         stiff3,
         jac_coefs,
         pickers,
-        labels,
+        rows,
         proj3,
-        fault_elem,
-        fault_proj,
-    )
-    arrived = exchanged(up, down, sideways)
+        fault_picker,
+        marks,
+    )
+    arrived = exchanged(twin, across, pair, sideways)
     pre, flux, near = call(
         again_kernel,
         "later_local",
@@ -695,11 +723,11 @@
         advanced,
         jac_coefs,
         proj3,
+        near_pickers,
+        marks,
         vol3,
         own3,
         local_coefs,
-        near_pickers,
-        near_labels,
     )
     (result,) = call(
         final_kernel,
@@ -712,11 +740,10 @@
         flux,
         pre,
         lift3,
-        sideways,
-        strength,
-        fault_elem,
-        fault_proj,
-        even,
+        pair,
+        marks,
+        reals,
+        fault_picker,
     )
     return jnp.transpose(result.reshape(quant, elems, basis), (0, 2, 1))
 

time: 53.3 us -> 41.4 us (0.78)
  the two profiles are of different devices: /device:TPU:231 before, /device:TPU:215 now
where the time goes in v1:
time: 41.4 us; the launch traced here: 41 us
  starting transfers between devices  27.4 us (66%)
  Pallas kernels  9.01 us (22%)
  local copies, waits for them, and re-layouts  2.24 us (5%)
  waiting for transfers between devices  2.08 us (5%)
    ppermute x4, starting transfers between devices, with_other_side(): return lax.ppermute(message, axis, pairs)  14.6 us
    ppermute x4, starting transfers between devices, with_twin(): return lax.ppermute(message, axis, [(i, i ^ 1) for i in range(length)])  12.8 us
    pallas_call x6, Pallas kernels, call(): pl.pallas_call(kernel, out_shape=[jax.ShapeDtypeStruct(shape, dtype) for...  9.01 us
    unnamed x36, local copies, waits for them, and re-layouts  2.24 us
    ppermute x4, waiting for transfers between devices, with_other_side(): return lax.ppermute(message, axis, pairs)  2.07 us
  transfers between devices with their start and end apart: 8, of which 2 were waited for; matrix products, arithmetic and copies ran while one was open for 0% of the time, Pallas kernels for 5%

profile of v1, /device:TPU:215, one launch (start us, length us, event | category | flops | bytes accessed | tf_op | source)
XLA Modules:
  0.0 41.0 jit_solution(12127084074375005941)
XLA Ops:
  0.0 0.9 %copy-done.17 = f32[3,56,56]{2,1,0:T(8,128)S(1)} copy-done((f32[3,56,56]{2,1,0:T(8,128)S(1)}, f32[3,56,56]{2,1,0:T(8,128)}, u32[]{:S(2)}) %copy-start.17) | copy-done | bytes 37656
  1.0 0.2 weights.1.stiff3
  1.2 0.0 copy-start.9
  1.2 0.5 %copy-done.10 = s32[2,32]{1,0:T(2,128)S(1)} copy-done((s32[2,32]{1,0:T(2,128)S(1)}, s32[2,32]{1,0:T(2,128)}, u32[]{:S(2)}) %copy-start.10) | copy-done | bytes 280
  1.7 0.0 copy-done.11
  1.7 0.0 copy-done.12
  1.7 0.1 copy-done.9
  1.9 2.3 %first_sends.1 = (f32[3,56,128]{2,1,0:T(8,128)S(1)}, f32[3,56,128]{2,1,0:T(8,128)S(1)}, f32[3,56,128]{2,1,0:T(8,128)S(1)}, f32[21,4,128]{2,1,0:T(4,128)S(1)}, bf...) custom-call(f32[288,56]{1,0:T(8,128)S(1)} %bitcast.20, ...), custom_call_target="tpu_custom_call" | custom-call | flops 8000000 | bytes 8000000 | tf_op jit(solution)/shard_map/first_sends/pallas_call | solution.py:564
  4.2 2.6 %collective-permute-start = (f32[72,128]{1,0:T(8,128)S(1)}, f32[72,128]{1,0:T(8,128)S(1)}, u32[]{:S(2)}, u32[]{:S(2)}) collective-permute-start(f32[72,128]{1,0:T(8,128)S(1)} %get-tuple-element.37), channel_id=1, source_target_pairs={{0,8},{8,0},{16,24},{24,16},{32,40},{40,32},{48,56},{56,48},{64,72... | collective-permute-start | bytes 110600 | tf_op jit(solution)/shard_map/ppermute | solution.py:579
  6.8 5.0 %collective-permute-start.1 = (f32[72,128]{1,0:T(8,128)S(1)}, f32[72,128]{1,0:T(8,128)S(1)}, u32[]{:S(2)}, u32[]{:S(2)}) collective-permute-start(f32[72,128]{1,0:T(8,128)S(1)} %get-tuple-element.38), channel_id=1, source_target_pairs={{8,16},{16,8},{24,32},{32,24},{40,48},{48,40},{56,64},{64,56},{72,... | collective-permute-start | bytes 110600 | tf_op jit(solution)/shard_map/ppermute | solution.py:585
  11.8 2.1 %collective-permute-start.3 = (f32[72,128]{1,0:T(8,128)S(1)}, f32[72,128]{1,0:T(8,128)S(1)}, u32[]{:S(2)}, u32[]{:S(2)}) collective-permute-start(f32[72,128]{1,0:T(8,128)S(1)} %get-tuple-element.39), channel_id=1, source_target_pairs={{1,2},{2,1},{3,4},{4,3},{5,6},{6,5},{9,10},{10,9},{11,12},{12,11},... | collective-permute-start | bytes 110600 | tf_op jit(solution)/shard_map/ppermute | solution.py:585
  13.9 5.5 %collective-permute-start.2 = (f32[72,128]{1,0:T(8,128)S(1)}, f32[72,128]{1,0:T(8,128)S(1)}, u32[]{:S(2)}, u32[]{:S(2)}) collective-permute-start(f32[72,128]{1,0:T(8,128)S(1)} %get-tuple-element.39), channel_id=1, source_target_pairs={{0,1},{1,0},{2,3},{3,2},{4,5},{5,4},{6,7},{7,6},{8,9},{9,8},{10,11... | collective-permute-start | bytes 110600 | tf_op jit(solution)/shard_map/ppermute | solution.py:579
  19.4 0.0 copy-start.8
  19.5 0.0 copy-start.7
  19.5 0.0 copy-start.13
  19.5 0.0 copy-start.14
  19.5 0.0 copy-start.15
  19.6 0.6 %copy-done.8 = s32[4,32]{1,0:T(4,128)S(1)} copy-done((s32[4,32]{1,0:T(4,128)S(1)}, s32[4,32]{1,0:T(4,128)}, u32[]{:S(2)}) %copy-start.8) | copy-done | bytes 536
  20.1 0.0 copy-done.7
  20.2 0.0 copy-done.15
  20.2 1.2 %first_local.1 = (f32[3,56,128]{2,1,0:T(8,128)S(1)}, f32[3,96,128]{2,1,0:T(8,128)S(1)}, f32[3,96,128]{2,1,0:T(8,128)S(1)}, bf16[168,168]{1,0:T(8,128)(2,1)S(1)},...) custom-call(f32[3,56,128]{2,1,0:T(8,128)S(1)} %get-tuple-element.40., ...), custom_call_target="tpu_custom_call" | custom-call | flops 4000000 | bytes 4000000 | tf_op jit(solution)/shard_map/first_local/pallas_call | solution.py:564
  21.3 0.0 collective-permute-done.twin
  21.4 0.0 collective-permute-done.3.beyond
  21.4 3.0 %advance.1 = (f32[3,56,128]{2,1,0:T(8,128)S(1)}, f32[3,56,128]{2,1,0:T(8,128)S(1)}, f32[72,128]{1,0:T(8,128)S(1)}, f32[72,128]{1,0:T(8,128)S(1)}, f32[72,128]{1,0:T(8,128)S(1)}, /*index=5*/f32[96,128]{1,0:T(8,128)S(1)}) custom-call(f32[72,128]{1,0:T(8,128)S(1)} %collective-permute-done.twin, f32[72,128]{1,0:T(8,128)S(1)} %collective-permute-done.1.across, ...), custom_call_target="tpu_custom_call" | custom-call | flops 8000000 | bytes 8000000 | tf_op jit(solution)/shard_map/advance/pallas_call | solution.py:564
  24.4 2.8 %collective-permute-start.6 = (f32[96,128]{1,0:T(8,128)S(1)}, f32[96,128]{1,0:T(8,128)S(1)}, u32[]{:S(2)}, u32[]{:S(2)}) collective-permute-start(f32[96,128]{1,0:T(8,128)S(1)} %get-tuple-element.57.sent), channel_id=1, source_target_pairs={{0,1},{1,0},{2,3},{3,2},{4,5},{5,4},{6,7},{7,6},{8,9},{9,8},{10,11... | collective-permute-start | bytes 147464 | tf_op jit(solution)/shard_map/ppermute | solution.py:579
  27.2 1.9 %collective-permute-start.4 = (f32[72,128]{1,0:T(8,128)S(1)}, f32[72,128]{1,0:T(8,128)S(1)}, u32[]{:S(2)}, u32[]{:S(2)}) collective-permute-start(f32[72,128]{1,0:T(8,128)S(1)} %get-tuple-element.55), channel_id=1, source_target_pairs={{0,8},{8,0},{16,24},{24,16},{32,40},{40,32},{48,56},{56,48},{64,72... | collective-permute-start | bytes 110600 | tf_op jit(solution)/shard_map/ppermute | solution.py:579
  29.1 5.6 %collective-permute-start.5 = (f32[72,128]{1,0:T(8,128)S(1)}, f32[72,128]{1,0:T(8,128)S(1)}, u32[]{:S(2)}, u32[]{:S(2)}) collective-permute-start(f32[72,128]{1,0:T(8,128)S(1)} %get-tuple-element.56), channel_id=1, source_target_pairs={{8,16},{16,8},{24,32},{32,24},{40,48},{48,40},{56,64},{64,56},{72,... | collective-permute-start | bytes 110600 | tf_op jit(solution)/shard_map/ppermute | solution.py:585
  34.7 1.9 %collective-permute-start.7 = (f32[72,128]{1,0:T(8,128)S(1)}, f32[72,128]{1,0:T(8,128)S(1)}, u32[]{:S(2)}, u32[]{:S(2)}) collective-permute-start(f32[72,128]{1,0:T(8,128)S(1)} %get-tuple-element.58), channel_id=1, source_target_pairs={{1,2},{2,1},{3,4},{4,3},{5,6},{6,5},{9,10},{10,9},{11,12},{12,11},... | collective-permute-start | bytes 110600 | tf_op jit(solution)/shard_map/ppermute | solution.py:585
  36.6 0.7 %later_local.1 = (f32[3,56,128]{2,1,0:T(8,128)S(1)}, f32[3,96,128]{2,1,0:T(8,128)S(1)}, f32[3,96,128]{2,1,0:T(8,128)S(1)}) custom-call(f32[3,56,128]{2,1,0:T(8,128)S(1)} %get-tuple-element.59.values, f32[3,56,128]{2,1,0:T(8,128)S(1)} %get-tuple-element.60.base, f32[21,4,128]{2,1,0:T(4,128)S(1)} %get-tuple-element.42.jac_coefs, ...), custom_call_target="tpu_custom_call" | custom-call | flops 4000000 | bytes 4000000 | tf_op jit(solution)/shard_map/later_local/pallas_call | solution.py:564
  37.3 0.4 collective-permute-done.5.across
  37.7 1.7 %collective-permute-done.7.beyond = f32[72,128]{1,0:T(8,128)S(1)} collective-permute-done((f32[72,128]{1,0:T(8,128)S(1)}, f32[72,128]{1,0:T(8,128)S(1)}, u32[]{:S(2)}, u32[]{:S(2)}) %collective-permute-start.7) | collective-permute-done | bytes 36896 | tf_op jit(solution)/shard_map/ppermute | solution.py:585
  39.4 1.6 %combine.1 = f32[288,56]{1,0:T(8,128)} custom-call(f32[72,128]{1,0:T(8,128)S(1)} %collective-permute-done.4.twin, f32[72,128]{1,0:T(8,128)S(1)} %collective-permute-done.5.across, f32[96,128]{1,0:T(8,128)S(1)} %collective-permute-done.6.pair, f32[72,128]{1,0:T(8,128)S(1)} %collective-permute-done.7.beyond, bf16[384,512]{1,0:T(8,128)(2,1)S(1)} %get-tuple-element.44.halo, ...), custom_call_target="tpu_custom_call" | custom-call | flops 4000000 | bytes 4000000 | tf_op jit(solution)/shard_map/combine/pallas_call | solution.py:564
  (26 shorter events, 0.1 us)
Async XLA Ops:
  0.0 1.2 %copy-start = (f32[12,56,21]{1,2,0:T(8,128)S(1)}, f32[12,56,21]{1,2,0:T(8,128)}, u32[]{:S(2)}) copy-start(f32[12,56,21]{1,2,0:T(8,128)} %param.24) | copy-start | bytes 169348
  0.0 1.2 %copy-start.1 = (f32[3,9,9,32]{3,0,2,1:T(4,128)S(1)}, f32[3,9,9,32]{3,0,2,1:T(4,128)}, u32[]{:S(2)}) copy-start(f32[3,9,9,32]{3,0,2,1:T(4,128)} %param.19) | copy-start | bytes 93316
  0.0 1.2 %copy-start.4 = (f32[9,56,32]{1,2,0:T(8,128)S(1)}, f32[9,56,32]{1,2,0:T(8,128)}, u32[]{:S(2)}) copy-start(f32[9,56,32]{1,2,0:T(8,128)} %param.18) | copy-start | bytes 193540
  0.0 0.9 %copy-start.17 = (f32[3,56,56]{2,1,0:T(8,128)S(1)}, f32[3,56,56]{2,1,0:T(8,128)}, u32[]{:S(2)}) copy-start(f32[3,56,56]{2,1,0:T(8,128)} %stiffness.1) | copy-start | bytes 112900
  1.0 0.7 %copy-start.10 = (s32[2,32]{1,0:T(2,128)S(1)}, s32[2,32]{1,0:T(2,128)}, u32[]{:S(2)}) copy-start(s32[2,32]{1,0:T(2,128)} %strike_orient.1) | copy-start | bytes 772
  1.0 0.7 %copy-start.11 = (s32[2,16]{1,0:T(2,128)S(1)}, s32[2,16]{1,0:T(2,128)}, u32[]{:S(2)}) copy-start(s32[2,16]{1,0:T(2,128)} %depth_sends.1) | copy-start | bytes 388
  1.0 0.7 %copy-start.12 = (s32[2,16]{1,0:T(2,128)S(1)}, s32[2,16]{1,0:T(2,128)}, u32[]{:S(2)}) copy-start(s32[2,16]{1,0:T(2,128)} %depth_orient.1) | copy-start | bytes 388
  1.0 18.6 %copy-start.5 = (f32[3,56,56]{2,1,0:T(8,128)S(1)}, f32[3,56,56]{2,1,0:T(8,128)}, u32[]{:S(2)}) copy-start(f32[3,56,56]{2,1,0:T(8,128)} %volume.1) | copy-start | bytes 112900
  1.0 18.6 %copy-start.16 = (s32[32]{0:T(128)S(1)}, s32[32]{0:T(128)}, u32[]{:S(2)}) copy-start(s32[32]{0:T(128)} %param.35) | copy-start | bytes 388
  1.2 0.7 %copy-start.9 = (s32[2,32]{1,0:T(2,128)S(1)}, s32[2,32]{1,0:T(2,128)}, u32[]{:S(2)}) copy-start(s32[2,32]{1,0:T(2,128)} %strike_sends.1) | copy-start | bytes 772
  1.8 17.7 %copy-start.2 = (f32[4,9,9,32]{3,0,2,1:T(4,128)S(1)}, f32[4,9,9,32]{3,0,2,1:T(4,128)}, u32[]{:S(2)}) copy-start(f32[4,9,9,32]{3,0,2,1:T(4,128)} %param.20) | copy-start | bytes 124420
  1.8 17.7 %copy-start.3 = (f32[4,9,9,32]{3,0,2,1:T(4,128)S(1)}, f32[4,9,9,32]{3,0,2,1:T(4,128)}, u32[]{:S(2)}) copy-start(f32[4,9,9,32]{3,0,2,1:T(4,128)} %param.21) | copy-start | bytes 124420
  1.9 17.7 %copy-start.6 = (f32[4,21,56]{2,0,1:T(4,128)S(1)}, f32[4,21,56]{2,0,1:T(4,128)}, u32[]{:S(2)}) copy-start(f32[4,21,56]{2,0,1:T(4,128)} %param.25) | copy-start | bytes 56452
  4.2 17.2 %collective-permute-start = (f32[72,128]{1,0:T(8,128)S(1)}, f32[72,128]{1,0:T(8,128)S(1)}, u32[]{:S(2)}, u32[]{:S(2)}) collective-permute-start(f32[72,128]{1,0:T(8,128)S(1)} %get-tuple-element.37), channel_id=1, source_target_pairs={{0,8},{8,0},{16,24},{24,16},{32,40},{40,32},{48,56},{56,48},{64,72... | collective-permute-start | bytes 110600 | tf_op jit(solution)/shard_map/ppermute | solution.py:579
  6.8 14.6 %collective-permute-start.1 = (f32[72,128]{1,0:T(8,128)S(1)}, f32[72,128]{1,0:T(8,128)S(1)}, u32[]{:S(2)}, u32[]{:S(2)}) collective-permute-start(f32[72,128]{1,0:T(8,128)S(1)} %get-tuple-element.38), channel_id=1, source_target_pairs={{8,16},{16,8},{24,32},{32,24},{40,48},{48,40},{56,64},{64,56},{72,... | collective-permute-start | bytes 110600 | tf_op jit(solution)/shard_map/ppermute | solution.py:585
  11.8 9.6 %collective-permute-start.3 = (f32[72,128]{1,0:T(8,128)S(1)}, f32[72,128]{1,0:T(8,128)S(1)}, u32[]{:S(2)}, u32[]{:S(2)}) collective-permute-start(f32[72,128]{1,0:T(8,128)S(1)} %get-tuple-element.39), channel_id=1, source_target_pairs={{1,2},{2,1},{3,4},{4,3},{5,6},{6,5},{9,10},{10,9},{11,12},{12,11},... | collective-permute-start | bytes 110600 | tf_op jit(solution)/shard_map/ppermute | solution.py:585
  13.9 7.5 %collective-permute-start.2 = (f32[72,128]{1,0:T(8,128)S(1)}, f32[72,128]{1,0:T(8,128)S(1)}, u32[]{:S(2)}, u32[]{:S(2)}) collective-permute-start(f32[72,128]{1,0:T(8,128)S(1)} %get-tuple-element.39), channel_id=1, source_target_pairs={{0,1},{1,0},{2,3},{3,2},{4,5},{5,4},{6,7},{7,6},{8,9},{9,8},{10,11... | collective-permute-start | bytes 110600 | tf_op jit(solution)/shard_map/ppermute | solution.py:579
  19.4 0.7 %copy-start.8 = (s32[4,32]{1,0:T(4,128)S(1)}, s32[4,32]{1,0:T(4,128)}, u32[]{:S(2)}) copy-start(s32[4,32]{1,0:T(4,128)} %face_orient.1) | copy-start | bytes 1540
  19.5 0.7 %copy-start.7 = (s32[4,32]{1,0:T(4,128)S(1)}, s32[4,32]{1,0:T(4,128)}, u32[]{:S(2)}) copy-start(s32[4,32]{1,0:T(4,128)} %neighbours.1) | copy-start | bytes 1540
  19.5 0.7 %copy-start.13 = (s32[32]{0:T(128)S(1)}, s32[32]{0:T(128)}, u32[]{:S(2)}) copy-start(s32[32]{0:T(128)} %param.27) | copy-start | bytes 388
  19.5 0.7 %copy-start.14 = (f32[32]{0:T(128)S(1)}, f32[32]{0:T(128)}, u32[]{:S(2)}) copy-start(f32[32]{0:T(128)} %param.26) | copy-start | bytes 388
  19.5 0.7 %copy-start.15 = (s32[32]{0:T(128)S(1)}, s32[32]{0:T(128)}, u32[]{:S(2)}) copy-start(s32[32]{0:T(128)} %param.34) | copy-start | bytes 388
  24.4 15.0 %collective-permute-start.6 = (f32[96,128]{1,0:T(8,128)S(1)}, f32[96,128]{1,0:T(8,128)S(1)}, u32[]{:S(2)}, u32[]{:S(2)}) collective-permute-start(f32[96,128]{1,0:T(8,128)S(1)} %get-tuple-element.57.sent), channel_id=1, source_target_pairs={{0,1},{1,0},{2,3},{3,2},{4,5},{5,4},{6,7},{7,6},{8,9},{9,8},{10,11... | collective-permute-start | bytes 147464 | tf_op jit(solution)/shard_map/ppermute | solution.py:579
  27.2 10.1 %collective-permute-start.4 = (f32[72,128]{1,0:T(8,128)S(1)}, f32[72,128]{1,0:T(8,128)S(1)}, u32[]{:S(2)}, u32[]{:S(2)}) collective-permute-start(f32[72,128]{1,0:T(8,128)S(1)} %get-tuple-element.55), channel_id=1, source_target_pairs={{0,8},{8,0},{16,24},{24,16},{32,40},{40,32},{48,56},{56,48},{64,72... | collective-permute-start | bytes 110600 | tf_op jit(solution)/shard_map/ppermute | solution.py:579
  29.1 8.6 %collective-permute-start.5 = (f32[72,128]{1,0:T(8,128)S(1)}, f32[72,128]{1,0:T(8,128)S(1)}, u32[]{:S(2)}, u32[]{:S(2)}) collective-permute-start(f32[72,128]{1,0:T(8,128)S(1)} %get-tuple-element.56), channel_id=1, source_target_pairs={{8,16},{16,8},{24,32},{32,24},{40,48},{48,40},{56,64},{64,56},{72,... | collective-permute-start | bytes 110600 | tf_op jit(solution)/shard_map/ppermute | solution.py:585
  34.7 4.7 %collective-permute-start.7 = (f32[72,128]{1,0:T(8,128)S(1)}, f32[72,128]{1,0:T(8,128)S(1)}, u32[]{:S(2)}, u32[]{:S(2)}) collective-permute-start(f32[72,128]{1,0:T(8,128)S(1)} %get-tuple-element.58), channel_id=1, source_target_pairs={{1,2},{2,1},{3,4},{4,3},{5,6},{6,5},{9,10},{10,9},{11,12},{12,11},... | collective-permute-start | bytes 110600 | tf_op jit(solution)/shard_map/ppermute | solution.py:585

commit v2 on v1

--- a/solution.py
+++ b/solution.py
@@ -16,8 +16,7 @@
 LANES = 128
 TILES = 3
 COEFS = 21
-CHUNKS = ((0, 32), (32, 24))
-FAULT_ROW, CLUSTER_ROW, NEAR_ROW, ROWS = 0, 1, 2, 8
+FAULT_ROW, CLUSTER_ROW, ELEM_ROW, SEND_ROW, NEAR_ROW, BEHIND_ROW, ROWS = 0, 1, 2, 3, 6, 10, 16
 
 fast_step = 0.5
 f32 = jnp.float32
@@ -60,7 +59,7 @@
         for into in range(2):
             for turn in range(4):
                 target[(out * 2 + into) * 4 + turn, 0:kinds, :] = across(
-                    [source[4 * out + g, 4 * into + (g - turn) % 4] for g in range(4)]
+                    [source[4 * out + (g + turn) % 4, 4 * into + g] for g in range(4)]
                 )
         target[16 + out, 0:kinds, :] = across([source[4 * out + g, 8] for g in range(4)])
         target[18 + out, 0:kinds, :] = across([source[8, 4 * out + g] for g in range(4)])
@@ -70,41 +69,45 @@
 
 
 def contract(coefs, terms):
-    totals = [None, None, None]
-
-    def add(which, kind, slot, values):
-        product = coefs[slot, kind : kind + 1, :] * values
-        totals[which] = product if totals[which] is None else totals[which] + product
-
-    for kind, tiles in terms:
-        for into in range(2):
-            for turn in range(4):
-                turned = pltpu.roll(tiles[into], WIDE * turn, 1) if turn else tiles[into]
-                for out in range(2):
-                    add(out, kind, (out * 2 + into) * 4 + turn, turned)
-                if turn == 0:
-                    add(2, kind, 18 + into, turned)
-        for out in range(2):
-            add(out, kind, 16 + out, tiles[2])
-        add(2, kind, 20, tiles[2])
-    last = totals[2]
+    def product(slot, kind, values):
+        return coefs[slot, kind : kind + 1, :] * values
+
+    def total(products):
+        result = products[0]
+        for other in products[1:]:
+            result = result + other
+        return result
+
+    found = []
+    for out in range(2):
+        sums = []
+        for turn in range(4):
+            products = [
+                product((out * 2 + into) * 4 + turn, kind, tiles[into])
+                for kind, tiles in terms
+                for into in range(2)
+            ]
+            if turn == 0:
+                products += [product(16 + out, kind, tiles[2]) for kind, tiles in terms]
+            moved = total(products)
+            sums.append(pltpu.roll(moved, WIDE * turn, 1) if turn else moved)
+        found.append(total(sums))
+    last = total(
+        [product(18 + into, kind, tiles[into]) for kind, tiles in terms for into in range(2)]
+        + [product(20, kind, tiles[2]) for kind, tiles in terms]
+    )
     last = last + pltpu.roll(last, 2 * WIDE, 1)
     last = last + pltpu.roll(last, WIDE, 1)
-    return totals[0], totals[1], last
+    return found[0], found[1], last
 
 
 def volume_like(tiles, weights3, coefs):
-    applied = mm(weights3, stacked(tiles))
-    pieces = []
-    for start, size in CHUNKS:
-        terms = []
-        for d in range(3):
-            rows = applied[BASIS * d + start : BASIS * d + start + size]
-            terms.append((d, [rows[:, LANES * t : LANES * (t + 1)] for t in range(TILES)]))
-        pieces.append(contract(coefs, terms))
-    return [
-        jnp.concatenate([piece[t] for piece in pieces], axis=0) for t in range(TILES)
+    whole = mm(weights3, stacked(tiles))
+    applied = [whole[:, LANES * t : LANES * (t + 1)] for t in range(TILES)]
+    terms = [
+        (d, [part[BASIS * d : BASIS * (d + 1)] for part in applied]) for d in range(3)
     ]
+    return list(contract(coefs, terms))
 
 
 def integrals(tiles, weights3, coefs, with_second):
@@ -187,42 +190,35 @@
         ref[t] = tiles[t]
 
 
-def weights_kernel(stiffness, stiff3_out):
-    stiff3_out[...] = left3(jnp.concatenate([-stiffness[d].T for d in range(3)], axis=0))
-
-
-def plan_sends(strike_sends, strike_orient, depth_sends, depth_orient, pickers_out, rows_out):
-    strike_odd = lax.axis_index("strike") % 2
-    depth_odd = lax.axis_index("depth") % 2
-
-    def either(table, odd):
-        twin = table[1:2, :] * (1 - odd) + table[0:1, :] * odd
-        across = table[0:1, :] * (1 - odd) + table[1:2, :] * odd
-        return twin, across
-
-    def jobs(strike, depth):
-        twin, across = either(strike, strike_odd)
-        return [
-            lane_tiled(twin),
-            lane_tiled(across),
-            lane_tiled(jnp.concatenate(either(depth, depth_odd), axis=1)),
-        ]
-
-    elements = jobs(strike_sends, depth_sends)
-    labels = jobs(strike_orient, depth_orient)
-    for j in range(3):
-        pickers_out[:, LANES * j : LANES * (j + 1)] = picking(elements[j])
-        rows_out[j : j + 1, :] = labels[j]
-
-
-def plan_faces(neighbours, face_orient, near_pickers_out, halo_out, marks_out):
+def either(table, axis):
+    odd = lax.axis_index(axis) % 2
+    twin = table[1:2, :] * (1 - odd) + table[0:1, :] * odd
+    across = table[0:1, :] * (1 - odd) + table[1:2, :] * odd
+    return twin, across
+
+
+def plan_kernel(strike_sends, pickers_out):
+    for j, elements in enumerate(either(strike_sends, "strike")):
+        pickers_out[:, LANES * j : LANES * (j + 1)] = picking(lane_tiled(elements))
+
+
+def plan_depth(depth_sends):
+    return picking(lane_tiled(jnp.concatenate(either(depth_sends, "depth"), axis=1)))
+
+
+def send_labels(strike_orient, depth_orient):
+    rows = [lane_tiled(row) for row in either(strike_orient, "strike")]
+    rows.append(lane_tiled(jnp.concatenate(either(depth_orient, "depth"), axis=1)))
+    return rows
+
+
+def plan_faces(rows, near_pickers_out, halo_out):
     strike_odd = lax.axis_index("strike") % 2
     depth_odd = lax.axis_index("depth") % 2
     sublane, lane = iotas(LANES, LANES)
     group = (lane // WIDE) * WIDE
     for f in range(FACES):
-        behind = lane_tiled(neighbours[f : f + 1, :])
-        marks_out[NEAR_ROW + f : NEAR_ROW + f + 1, :] = lane_tiled(face_orient[f : f + 1, :])
+        behind = rows[BEHIND_ROW + f : BEHIND_ROW + f + 1, :]
         columns = slice(LANES * f, LANES * (f + 1))
         local = jnp.where(behind < WIDE, behind, -4 * LANES)
         near_pickers_out[:, columns] = one_hot(sublane == local + group)
@@ -243,30 +239,40 @@
 def send_kernel(
     state,
     jacobians,
+    stiffness,
     face_proj,
-    strike_sends,
+    strike_pickers,
     strike_orient,
     depth_sends,
     depth_orient,
-    stiff3,
+    neighbours,
+    face_orient,
+    cluster,
+    strength,
+    fault_elem,
+    fault_proj,
     base_out,
     first_out,
     second_out,
     jac_coefs,
+    stiff3_out,
     proj3_out,
     pickers_out,
     rows_out,
+    reals_out,
     twin_out,
     across_out,
     depth_out,
+    pair_out,
 ):
     build_coefs(jacobians, jac_coefs)
-    plan_sends(strike_sends, strike_orient, depth_sends, depth_orient, pickers_out, rows_out)
+    stiff3 = left3(jnp.concatenate([-stiffness[d].T for d in range(3)], axis=0))
+    stiff3_out[...] = stiff3
     tiles = [state[LANES * t : LANES * (t + 1), :].T for t in range(2)]
     last = state[2 * LANES : 2 * LANES + WIDE, :]
     tiles.append(jnp.concatenate([last] * 4, axis=0).T)
     store_tiles(base_out, tiles)
-    first, second = integrals(tiles, stiff3[...], jac_coefs, True)
+    first, second = integrals(tiles, stiff3, jac_coefs, True)
     store_tiles(first_out, first)
     store_tiles(second_out, second)
     margin = jnp.zeros((FACE_ROWS - FACE_BASIS, BASIS), f32)
@@ -274,19 +280,35 @@
         jnp.concatenate([piece for m in range(PROJS) for piece in (face_proj[m], margin)], axis=0)
     )
     proj3_out[...] = proj3
-    send(first, pickers_out, rows_out, proj3, twin_out, across_out, depth_out)
+    pickers_out[:, 0 : 2 * LANES] = strike_pickers[...]
+    pickers_out[:, 2 * LANES : 3 * LANES] = plan_depth(depth_sends)
+    for j, row in enumerate(send_labels(strike_orient, depth_orient)):
+        rows_out[SEND_ROW + j : SEND_ROW + j + 1, :] = row
+    send(first, pickers_out, rows_out, proj3, twin_out, across_out, depth_out, pair_out)
+    rows_out[FAULT_ROW : FAULT_ROW + 1, :] = lane_tiled(fault_proj[...])
+    rows_out[CLUSTER_ROW : CLUSTER_ROW + 1, :] = lane_tiled(cluster[...])
+    rows_out[ELEM_ROW : ELEM_ROW + 1, :] = lane_tiled(fault_elem[...])
+    for f in range(FACES):
+        rows_out[NEAR_ROW + f : NEAR_ROW + f + 1, :] = lane_tiled(face_orient[f : f + 1, :])
+        rows_out[BEHIND_ROW + f : BEHIND_ROW + f + 1, :] = lane_tiled(neighbours[f : f + 1, :])
+    reals_out[0:1, :] = lane_tiled(strength[...])
+    odd = lax.axis_index("depth") % 2
+    reals_out[1:2, :] = jnp.where(iotas(1, LANES)[1] * 0 + odd == 0, 1.0, -1.0)
 
 
 def send(values, pickers, rows, proj3, *outs):
     found = picked_traces(
         values,
         pickers[...],
-        [rows[j : j + 1, :] for j in range(3)],
+        [rows[SEND_ROW + j : SEND_ROW + j + 1, :] for j in range(3)],
         proj3,
     )
-    for out, pieces in zip(outs, found):
+    for out, pieces in zip(outs, (*found, found[2])):
         for t in range(TILES):
             out[FACE_ROWS * t : FACE_ROWS * (t + 1), :] = pieces[t]
+        spare = out.shape[0] - TILES * FACE_ROWS
+        if spare:
+            out[TILES * FACE_ROWS :, :] = jnp.zeros((spare, LANES), f32)
 
 
 def local_part(values, base, vol3, jac_coefs, own3, local_coefs, pickers, labels, proj3, outs):
@@ -310,8 +332,8 @@
             near_out[t, at : at + FACE_ROWS, :] = near[f][t]
 
 
-def near_labels(marks):
-    return [marks[NEAR_ROW + f : NEAR_ROW + f + 1, :] for f in range(FACES)]
+def near_labels(rows):
+    return [rows[NEAR_ROW + f : NEAR_ROW + f + 1, :] for f in range(FACES)]
 
 
 def prepare_kernel(
@@ -319,17 +341,12 @@
     base,
     jac_coefs,
     proj3,
-    neighbours,
-    face_orient,
+    rows,
     volume,
     face_proj,
     flux_local,
     flux_neigh,
     face_lift,
-    cluster,
-    strength,
-    fault_elem,
-    fault_proj,
     pre_out,
     flux_out,
     near_out,
@@ -341,16 +358,10 @@
     near_pickers_out,
     halo_out,
     fault_pickers_out,
-    marks_out,
-    reals_out,
 ):
-    depth_odd = lax.axis_index("depth") % 2
-    fault_pickers_out[...] = jnp.concatenate(fault_pickers(fault_elem), axis=0)
-    marks_out[FAULT_ROW : FAULT_ROW + 1, :] = lane_tiled(fault_proj[...])
-    marks_out[CLUSTER_ROW : CLUSTER_ROW + 1, :] = lane_tiled(cluster[...])
-    reals_out[0:1, :] = lane_tiled(strength[...])
-    reals_out[1:2, :] = jnp.where(iotas(1, LANES)[1] * 0 + depth_odd == 0, 1.0, -1.0)
-    plan_faces(neighbours, face_orient, near_pickers_out, halo_out, marks_out)
+    picks = fault_pickers(rows[ELEM_ROW : ELEM_ROW + 1, :])
+    fault_pickers_out[...] = jnp.concatenate(picks, axis=0)
+    plan_faces(rows, near_pickers_out, halo_out)
     vol3 = left3(jnp.concatenate([volume[d].T for d in range(3)], axis=0))
     vol3_out[...] = vol3
     margin = jnp.zeros((FACE_ROWS - FACE_BASIS, BASIS), f32)
@@ -373,7 +384,7 @@
         own3,
         local_coefs,
         near_pickers_out[...],
-        near_labels(marks_out),
+        near_labels(rows),
         proj3[...],
         (pre_out, flux_out, near_out),
     )
@@ -385,7 +396,7 @@
     jac_coefs,
     proj3,
     pickers,
-    marks,
+    rows,
     vol3,
     own3,
     local_coefs,
@@ -401,7 +412,7 @@
         own3[...],
         local_coefs,
         pickers[...],
-        near_labels(marks),
+        near_labels(rows),
         proj3[...],
         (pre_out, flux_out, near_out),
     )
@@ -412,8 +423,8 @@
     lane = iotas(rows, LANES)[1]
     blocks = [
         twin[...],
-        across[...],
-        jnp.where(lane % WIDE < WIDE // 2, pair[0:rows, :], beyond[...]),
+        across[0:rows, :],
+        jnp.where(lane % WIDE < WIDE // 2, pair[0:rows, :], beyond[0:rows, :]),
     ]
     parts = [split(block) for block in blocks]
     left = jnp.concatenate(
@@ -447,7 +458,7 @@
 def fault_pickers(fault_elem):
     sublane, lane = iotas(LANES, LANES)
     group = lane // WIDE
-    source = lane_tiled(fault_elem[...]) + jnp.where(group == 1, WIDE, 3 * WIDE)
+    source = fault_elem + jnp.where(group == 1, WIDE, 3 * WIDE)
     hit = sublane == source
     return [
         one_hot(hit & (group == 0)),
@@ -475,7 +486,6 @@
     rows,
     proj3,
     fault_picker,
-    marks,
     advanced_out,
     later_out,
     twin_out,
@@ -487,21 +497,20 @@
     advanced = lifted(pre, terms, lift3)
     store_tiles(advanced_out, advanced)
     repeated = integrals(advanced, stiff3[...], jac_coefs, False)[0]
-    is_fast = marks[CLUSTER_ROW : CLUSTER_ROW + 1, :] == 0
+    is_fast = rows[CLUSTER_ROW : CLUSTER_ROW + 1, :] == 0
     later = [jnp.where(is_fast, repeated[t], second[t]) for t in range(TILES)]
     store_tiles(later_out, later)
-    send(later, pickers, rows, proj3[...], twin_out, across_out, depth_out)
+    send(later, pickers, rows, proj3[...], twin_out, across_out, depth_out, pair_out)
     parts = []
     for t in range(TILES):
         parts.append(jnp.concatenate(split(first[t] + later[t]), axis=0))
     moved = mm(jnp.concatenate(parts, axis=1).astype(bf16), fault_picker[...])
     own = traces(
         [(moved[0:BASIS], moved[BASIS : 2 * BASIS])],
-        [marks[FAULT_ROW : FAULT_ROW + 1, :]],
+        [rows[FAULT_ROW : FAULT_ROW + 1, :]],
         proj3[...],
     )[0]
-    pair_out[0 : TILES * FACE_ROWS, :] = depth_out[...]
-    pair_out[TILES * FACE_ROWS :, :] = own
+    pair_out[TILES * FACE_ROWS : TILES * FACE_ROWS + FACE_ROWS, :] = own
 
 
 def final_kernel(
@@ -516,14 +525,14 @@
     pre,
     lift3,
     sent,
-    marks,
+    rows,
     reals,
     fault_picker,
     result,
 ):
     at = TILES * FACE_ROWS
-    own = sent[at:, :]
-    other = pair[at:, :]
+    own = sent[at : at + FACE_ROWS, :]
+    other = pair[at : at + FACE_ROWS, :]
     limit = reals[0:1, :]
     side = reals[1:2, :]
     group = iotas(FACE_ROWS, LANES)[1] // WIDE
@@ -538,7 +547,7 @@
     factor = limit / jnp.maximum(jnp.sqrt(square + mate), limit)
     traction = shear * factor
     jump = jnp.where(group < 2, traction, side * (traction - shear))
-    face = marks[FAULT_ROW : FAULT_ROW + 1, :] // 3
+    face = rows[FAULT_ROW : FAULT_ROW + 1, :] // 3
     placed = jnp.concatenate([jnp.where(face == f, jump, 0.0) for f in range(FACES)], axis=0)
     spread = lax.dot_general(
         jnp.concatenate(split(placed), axis=0).astype(bf16),
@@ -556,7 +565,9 @@
     result[2 * LANES : 2 * LANES + WIDE, :] = new[2].T[3 * WIDE : 4 * WIDE, :]
 
 
-COSTS = dict(weights=100000, first_sends=8, first_local=4, advance=8, later_local=4, combine=4)
+FIRST_SPARE = (16, 8, 24)
+LATER_SPARE = (16, 8, 24)
+COSTS = dict(plan=100000, first_sends=100000, first_local=4, advance=8, later_local=4, combine=4)
 
 
 def call(kernel, name, outs, *operands):
@@ -628,12 +639,13 @@
     faces = ((TILES, FACES * FACE_ROWS, LANES), f32)
     coefs = ((COEFS, 4, LANES), f32)
     message = ((TILES * FACE_ROWS, LANES), f32)
-    longer = ((TILES * FACE_ROWS + FACE_ROWS, LANES), f32)
-
-    (stiff3,) = call(
-        weights_kernel, "weights", [((3 * BASIS, 3 * BASIS), bf16)], stiffness
-    )
-    base, first, second, jac_coefs, proj3, pickers, rows, twin, across, sideways = call(
+    sized = [((TILES * FACE_ROWS + more, LANES), f32) for more in FIRST_SPARE]
+    resized = [((TILES * FACE_ROWS + more, LANES), f32) for more in LATER_SPARE]
+
+    (strike_pickers,) = call(
+        plan_kernel, "plan", [((LANES, 2 * LANES), bf16)], strike_sends
+    )
+    base, first, second, jac_coefs, stiff3, proj3, pickers, rows, reals, *messages = call(
         send_kernel,
         "first_sends",
         [
@@ -641,23 +653,31 @@
             full,
             full,
             coefs,
+            ((3 * BASIS, 3 * BASIS), bf16),
             ((PROJS * FACE_ROWS, 3 * BASIS), bf16),
             ((LANES, 3 * LANES), bf16),
             ((ROWS, LANES), jnp.int32),
+            ((8, LANES), f32),
             message,
-            message,
-            message,
+            *sized,
         ],
         state,
         jac,
+        stiffness,
         proj,
-        strike_sends,
+        strike_pickers,
         strike_orient,
         depth_sends,
         depth_orient,
-        stiff3,
-    )
-    arrived = exchanged(twin, across, sideways, sideways)
+        neighbours,
+        face_orient,
+        cluster,
+        strength,
+        fault_elem,
+        fault_proj,
+    )
+    twin, across, sideways, pair = messages
+    arrived = exchanged(twin, across, pair, sideways)
     pre, flux, near, vol3, own3, local_coefs, neigh_coefs, *rest = call(
         prepare_kernel,
         "first_local",
@@ -673,30 +693,23 @@
             ((LANES, FACES * LANES), bf16),
             ((3 * LANES, FACES * LANES), bf16),
             ((TILES * LANES, LANES), bf16),
-            ((ROWS, LANES), jnp.int32),
-            ((8, LANES), f32),
         ],
         first,
         base,
         jac_coefs,
         proj3,
-        neighbours,
-        face_orient,
+        rows,
         volume,
         proj,
         local,
         neigh,
         lift,
-        cluster,
-        strength,
-        fault_elem,
-        fault_proj,
-    )
-    lift3, near_pickers, halo, fault_picker, marks, reals = rest
+    )
+    lift3, near_pickers, halo, fault_picker = rest
     advanced, later, twin, across, sideways, pair = call(
         middle_kernel,
         "advance",
-        [full, full, message, message, message, longer],
+        [full, full, message, *resized],
         *arrived,
         halo,
         near,
@@ -712,7 +725,6 @@
         rows,
         proj3,
         fault_picker,
-        marks,
     )
     arrived = exchanged(twin, across, pair, sideways)
     pre, flux, near = call(
@@ -724,7 +736,7 @@
         jac_coefs,
         proj3,
         near_pickers,
-        marks,
+        rows,
         vol3,
         own3,
         local_coefs,
@@ -741,7 +753,7 @@
         pre,
         lift3,
         pair,
-        marks,
+        rows,
         reals,
         fault_picker,
     )

time: 41.4 us -> 38.1 us (0.920)
  the two profiles are of different devices: /device:TPU:215 before, /device:TPU:207 now
where the time goes in v2:
time: 38.1 us; the launch traced here: 37.7 us
  starting transfers between devices  26.6 us (70%)
  Pallas kernels  8.75 us (23%)
  local copies, waits for them, and re-layouts  1.48 us (4%)
  waiting for transfers between devices  0.57 us (1%)
    ppermute x4, starting transfers between devices, with_other_side(): return lax.ppermute(message, axis, pairs)  18.8 us
    pallas_call x6, Pallas kernels, call(): pl.pallas_call(kernel, out_shape=[jax.ShapeDtypeStruct(shape, dtype) for...  8.75 us
    ppermute x4, starting transfers between devices, with_twin(): return lax.ppermute(message, axis, [(i, i ^ 1) for i in range(length)])  7.84 us
    unnamed x36, local copies, waits for them, and re-layouts  1.48 us
  transfers between devices with their start and end apart: 8, of which 2 were waited for; matrix products, arithmetic and copies ran while one was open for 0% of the time, Pallas kernels for 5%

profile of v2, /device:TPU:207, one launch (start us, length us, event | category | flops | bytes accessed | tf_op | source)
XLA Modules:
  0.0 37.7 jit_solution(10270557175395576103)
XLA Ops:
  0.0 0.7 %copy-done.10 = s32[2,32]{1,0:T(2,128)S(1)} copy-done((s32[2,32]{1,0:T(2,128)S(1)}, s32[2,32]{1,0:T(2,128)}, u32[]{:S(2)}) %copy-start.10) | copy-done | bytes 280
  0.8 0.1 plan.1.strike_pickers
  0.9 0.0 copy-start.8
  0.9 0.0 copy-start.11
  0.9 0.0 copy-start.14
  0.9 0.0 copy-done.7
  1.0 0.1 copy-done.5
  1.0 0.1 copy-done.6
  1.1 0.4 %copy-done.9 = s32[4,32]{1,0:T(4,128)S(1)} copy-done((s32[4,32]{1,0:T(4,128)S(1)}, s32[4,32]{1,0:T(4,128)}, u32[]{:S(2)}) %copy-start.9) | copy-done | bytes 536
  1.5 0.0 copy-done.12
  1.5 0.0 copy-done.13
  1.5 0.0 copy-done.16
  1.5 0.0 copy-done.17
  1.6 0.1 copy-done.8
  1.6 0.0 copy-done.11
  1.7 0.0 copy-start.4
  1.7 2.4 %first_sends.1 = (f32[3,56,128]{2,1,0:T(8,128)S(1)}, f32[3,56,128]{2,1,0:T(8,128)S(1)}, f32[3,56,128]{2,1,0:T(8,128)S(1)}, f32[21,4,128]{2,1,0:T(4,128)S(1)}, bf...) custom-call(f32[288,56]{1,0:T(8,128)S(1)} %bitcast.21, ...), custom_call_target="tpu_custom_call" | custom-call | flops 99999997952 | bytes 99999997952 | tf_op jit(solution)/shard_map/first_sends/pallas_call | solution.py:575
  4.1 2.1 %collective-permute-start.2 = (f32[96,128]{1,0:T(8,128)S(1)}, f32[96,128]{1,0:T(8,128)S(1)}, u32[]{:S(2)}, u32[]{:S(2)}) collective-permute-start(f32[96,128]{1,0:T(8,128)S(1)} %get-tuple-element.40), channel_id=1, source_target_pairs={{0,1},{1,0},{2,3},{3,2},{4,5},{5,4},{6,7},{7,6},{8,9},{9,8},{10,11... | collective-permute-start | bytes 147464 | tf_op jit(solution)/shard_map/ppermute | solution.py:590
  6.1 6.0 %collective-permute-start.1 = (f32[88,128]{1,0:T(8,128)S(1)}, f32[88,128]{1,0:T(8,128)S(1)}, u32[]{:S(2)}, u32[]{:S(2)}) collective-permute-start(f32[88,128]{1,0:T(8,128)S(1)} %get-tuple-element.39), channel_id=1, source_target_pairs={{8,16},{16,8},{24,32},{32,24},{40,48},{48,40},{56,64},{64,56},{72,... | collective-permute-start | bytes 135176 | tf_op jit(solution)/shard_map/ppermute | solution.py:596
  12.1 4.3 %collective-permute-start.3 = (f32[80,128]{1,0:T(8,128)S(1)}, f32[80,128]{1,0:T(8,128)S(1)}, u32[]{:S(2)}, u32[]{:S(2)}) collective-permute-start(f32[80,128]{1,0:T(8,128)S(1)} %get-tuple-element.41), channel_id=1, source_target_pairs={{1,2},{2,1},{3,4},{4,3},{5,6},{6,5},{9,10},{10,9},{11,12},{12,11},... | collective-permute-start | bytes 122888 | tf_op jit(solution)/shard_map/ppermute | solution.py:596
  16.5 1.9 %collective-permute-start = (f32[72,128]{1,0:T(8,128)S(1)}, f32[72,128]{1,0:T(8,128)S(1)}, u32[]{:S(2)}, u32[]{:S(2)}) collective-permute-start(f32[72,128]{1,0:T(8,128)S(1)} %get-tuple-element.38), channel_id=1, source_target_pairs={{0,8},{8,0},{16,24},{24,16},{32,40},{40,32},{48,56},{56,48},{64,72... | collective-permute-start | bytes 110600 | tf_op jit(solution)/shard_map/ppermute | solution.py:590
  18.4 1.0 %first_local.1 = (f32[3,56,128]{2,1,0:T(8,128)S(1)}, f32[3,96,128]{2,1,0:T(8,128)S(1)}, f32[3,96,128]{2,1,0:T(8,128)S(1)}, bf16[168,168]{1,0:T(8,128)(2,1)S(1)},...) custom-call(f32[3,56,128]{2,1,0:T(8,128)S(1)} %get-tuple-element.42., ...), custom_call_target="tpu_custom_call" | custom-call | flops 4000000 | bytes 4000000 | tf_op jit(solution)/shard_map/first_local/pallas_call | solution.py:575
  19.5 0.1 collective-permute-done.twin
  19.6 0.0 collective-permute-done.3.beyond
  19.6 2.9 %advance.1 = (f32[3,56,128]{2,1,0:T(8,128)S(1)}, f32[3,56,128]{2,1,0:T(8,128)S(1)}, f32[72,128]{1,0:T(8,128)S(1)}, f32[88,128]{1,0:T(8,128)S(1)}, f32[80,128]{1,0:T(8,128)S(1)}, /*index=5*/f32[96,128]{1,0:T(8,128)S(1)}) custom-call(f32[72,128]{1,0:T(8,128)S(1)} %collective-permute-done.twin, f32[88,128]{1,0:T(8,128)S(1)} %collective-permute-done.1.across, ...), custom_call_target="tpu_custom_call" | custom-call | flops 8000000 | bytes 8000000 | tf_op jit(solution)/shard_map/advance/pallas_call | solution.py:575
  22.5 1.9 %collective-permute-start.6 = (f32[96,128]{1,0:T(8,128)S(1)}, f32[96,128]{1,0:T(8,128)S(1)}, u32[]{:S(2)}, u32[]{:S(2)}) collective-permute-start(f32[96,128]{1,0:T(8,128)S(1)} %get-tuple-element.59.sent), channel_id=1, source_target_pairs={{0,1},{1,0},{2,3},{3,2},{4,5},{5,4},{6,7},{7,6},{8,9},{9,8},{10,11... | collective-permute-start | bytes 147464 | tf_op jit(solution)/shard_map/ppermute | solution.py:590
  24.4 3.4 %collective-permute-start.5 = (f32[88,128]{1,0:T(8,128)S(1)}, f32[88,128]{1,0:T(8,128)S(1)}, u32[]{:S(2)}, u32[]{:S(2)}) collective-permute-start(f32[88,128]{1,0:T(8,128)S(1)} %get-tuple-element.58), channel_id=1, source_target_pairs={{8,16},{16,8},{24,32},{32,24},{40,48},{48,40},{56,64},{64,56},{72,... | collective-permute-start | bytes 135176 | tf_op jit(solution)/shard_map/ppermute | solution.py:596
  27.9 5.1 %collective-permute-start.7 = (f32[80,128]{1,0:T(8,128)S(1)}, f32[80,128]{1,0:T(8,128)S(1)}, u32[]{:S(2)}, u32[]{:S(2)}) collective-permute-start(f32[80,128]{1,0:T(8,128)S(1)} %get-tuple-element.60), channel_id=1, source_target_pairs={{1,2},{2,1},{3,4},{4,3},{5,6},{6,5},{9,10},{10,9},{11,12},{12,11},... | collective-permute-start | bytes 122888 | tf_op jit(solution)/shard_map/ppermute | solution.py:596
  32.9 1.9 %collective-permute-start.4 = (f32[72,128]{1,0:T(8,128)S(1)}, f32[72,128]{1,0:T(8,128)S(1)}, u32[]{:S(2)}, u32[]{:S(2)}) collective-permute-start(f32[72,128]{1,0:T(8,128)S(1)} %get-tuple-element.57), channel_id=1, source_target_pairs={{0,8},{8,0},{16,24},{24,16},{32,40},{40,32},{48,56},{56,48},{64,72... | collective-permute-start | bytes 110600 | tf_op jit(solution)/shard_map/ppermute | solution.py:590
  34.9 0.7 %later_local.1 = (f32[3,56,128]{2,1,0:T(8,128)S(1)}, f32[3,96,128]{2,1,0:T(8,128)S(1)}, f32[3,96,128]{2,1,0:T(8,128)S(1)}) custom-call(f32[3,56,128]{2,1,0:T(8,128)S(1)} %get-tuple-element.61.values, f32[3,56,128]{2,1,0:T(8,128)S(1)} %get-tuple-element.62.base, f32[21,4,128]{2,1,0:T(4,128)S(1)} %get-tuple-element.44.jac_coefs, ...), custom_call_target="tpu_custom_call" | custom-call | flops 4000000 | bytes 4000000 | tf_op jit(solution)/shard_map/later_local/pallas_call | solution.py:575
  35.6 0.5 %collective-permute-done.4.twin = f32[72,128]{1,0:T(8,128)S(1)} collective-permute-done((f32[72,128]{1,0:T(8,128)S(1)}, f32[72,128]{1,0:T(8,128)S(1)}, u32[]{:S(2)}, u32[]{:S(2)}) %collective-permute-start.4) | collective-permute-done | bytes 36896 | tf_op jit(solution)/shard_map/ppermute | solution.py:590
  36.1 1.6 %combine.1 = f32[288,56]{1,0:T(8,128)} custom-call(f32[72,128]{1,0:T(8,128)S(1)} %collective-permute-done.4.twin, f32[88,128]{1,0:T(8,128)S(1)} %collective-permute-done.5.across, f32[96,128]{1,0:T(8,128)S(1)} %collective-permute-done.6.pair, f32[80,128]{1,0:T(8,128)S(1)} %collective-permute-done.7.beyond, bf16[384,512]{1,0:T(8,128)(2,1)S(1)} %get-tuple-element.47.halo, ...), custom_call_target="tpu_custom_call" | custom-call | flops 4000000 | bytes 4000000 | tf_op jit(solution)/shard_map/combine/pallas_call | solution.py:575
  (26 shorter events, 0.1 us)
Async XLA Ops:
  0.0 0.9 %copy-start.2 = (f32[12,56,21]{1,2,0:T(8,128)S(1)}, f32[12,56,21]{1,2,0:T(8,128)}, u32[]{:S(2)}) copy-start(f32[12,56,21]{1,2,0:T(8,128)} %param.24) | copy-start | bytes 169348
  0.0 1.0 %copy-start.7 = (f32[3,56,56]{2,1,0:T(8,128)S(1)}, f32[3,56,56]{2,1,0:T(8,128)}, u32[]{:S(2)}) copy-start(f32[3,56,56]{2,1,0:T(8,128)} %stiffness.1) | copy-start | bytes 112900
  0.0 1.0 %copy-start.5 = (f32[3,9,9,32]{3,0,2,1:T(4,128)S(1)}, f32[3,9,9,32]{3,0,2,1:T(4,128)}, u32[]{:S(2)}) copy-start(f32[3,9,9,32]{3,0,2,1:T(4,128)} %param.19) | copy-start | bytes 93316
  0.0 1.1 %copy-start.6 = (f32[9,56,32]{1,2,0:T(8,128)S(1)}, f32[9,56,32]{1,2,0:T(8,128)}, u32[]{:S(2)}) copy-start(f32[9,56,32]{1,2,0:T(8,128)} %param.18) | copy-start | bytes 193540
  0.0 0.7 %copy-start.10 = (s32[2,32]{1,0:T(2,128)S(1)}, s32[2,32]{1,0:T(2,128)}, u32[]{:S(2)}) copy-start(s32[2,32]{1,0:T(2,128)} %strike_sends.1) | copy-start | bytes 772
  0.8 0.7 %copy-start.9 = (s32[4,32]{1,0:T(4,128)S(1)}, s32[4,32]{1,0:T(4,128)}, u32[]{:S(2)}) copy-start(s32[4,32]{1,0:T(4,128)} %face_orient.1) | copy-start | bytes 1540
  0.8 0.8 %copy-start.12 = (s32[2,16]{1,0:T(2,128)S(1)}, s32[2,16]{1,0:T(2,128)}, u32[]{:S(2)}) copy-start(s32[2,16]{1,0:T(2,128)} %depth_sends.1) | copy-start | bytes 388
  0.8 0.8 %copy-start.13 = (s32[2,16]{1,0:T(2,128)S(1)}, s32[2,16]{1,0:T(2,128)}, u32[]{:S(2)}) copy-start(s32[2,16]{1,0:T(2,128)} %depth_orient.1) | copy-start | bytes 388
  0.8 0.8 %copy-start.15 = (f32[32]{0:T(128)S(1)}, f32[32]{0:T(128)}, u32[]{:S(2)}) copy-start(f32[32]{0:T(128)} %param.26) | copy-start | bytes 388
  0.8 0.8 %copy-start.16 = (s32[32]{0:T(128)S(1)}, s32[32]{0:T(128)}, u32[]{:S(2)}) copy-start(s32[32]{0:T(128)} %param.34) | copy-start | bytes 388
  0.8 0.8 %copy-start.17 = (s32[32]{0:T(128)S(1)}, s32[32]{0:T(128)}, u32[]{:S(2)}) copy-start(s32[32]{0:T(128)} %param.35) | copy-start | bytes 388
  0.9 0.7 %copy-start.8 = (s32[4,32]{1,0:T(4,128)S(1)}, s32[4,32]{1,0:T(4,128)}, u32[]{:S(2)}) copy-start(s32[4,32]{1,0:T(4,128)} %neighbours.1) | copy-start | bytes 1540
  0.9 0.7 %copy-start.11 = (s32[2,32]{1,0:T(2,128)S(1)}, s32[2,32]{1,0:T(2,128)}, u32[]{:S(2)}) copy-start(s32[2,32]{1,0:T(2,128)} %strike_orient.1) | copy-start | bytes 772
  0.9 0.7 %copy-start.14 = (s32[32]{0:T(128)S(1)}, s32[32]{0:T(128)}, u32[]{:S(2)}) copy-start(s32[32]{0:T(128)} %param.27) | copy-start | bytes 388
  1.6 16.7 %copy-start = (f32[4,9,9,32]{3,0,2,1:T(4,128)S(1)}, f32[4,9,9,32]{3,0,2,1:T(4,128)}, u32[]{:S(2)}) copy-start(f32[4,9,9,32]{3,0,2,1:T(4,128)} %param.20) | copy-start | bytes 124420
  1.7 16.7 %copy-start.1 = (f32[4,9,9,32]{3,0,2,1:T(4,128)S(1)}, f32[4,9,9,32]{3,0,2,1:T(4,128)}, u32[]{:S(2)}) copy-start(f32[4,9,9,32]{3,0,2,1:T(4,128)} %param.21) | copy-start | bytes 124420
  1.7 16.7 %copy-start.3 = (f32[3,56,56]{2,1,0:T(8,128)S(1)}, f32[3,56,56]{2,1,0:T(8,128)}, u32[]{:S(2)}) copy-start(f32[3,56,56]{2,1,0:T(8,128)} %volume.1) | copy-start | bytes 112900
  1.7 16.7 %copy-start.4 = (f32[4,21,56]{2,0,1:T(4,128)S(1)}, f32[4,21,56]{2,0,1:T(4,128)}, u32[]{:S(2)}) copy-start(f32[4,21,56]{2,0,1:T(4,128)} %param.25) | copy-start | bytes 56452
  4.1 15.5 %collective-permute-start.2 = (f32[96,128]{1,0:T(8,128)S(1)}, f32[96,128]{1,0:T(8,128)S(1)}, u32[]{:S(2)}, u32[]{:S(2)}) collective-permute-start(f32[96,128]{1,0:T(8,128)S(1)} %get-tuple-element.40), channel_id=1, source_target_pairs={{0,1},{1,0},{2,3},{3,2},{4,5},{5,4},{6,7},{7,6},{8,9},{9,8},{10,11... | collective-permute-start | bytes 147464 | tf_op jit(solution)/shard_map/ppermute | solution.py:590
  6.1 13.4 %collective-permute-start.1 = (f32[88,128]{1,0:T(8,128)S(1)}, f32[88,128]{1,0:T(8,128)S(1)}, u32[]{:S(2)}, u32[]{:S(2)}) collective-permute-start(f32[88,128]{1,0:T(8,128)S(1)} %get-tuple-element.39), channel_id=1, source_target_pairs={{8,16},{16,8},{24,32},{32,24},{40,48},{48,40},{56,64},{64,56},{72,... | collective-permute-start | bytes 135176 | tf_op jit(solution)/shard_map/ppermute | solution.py:596
  12.1 7.5 %collective-permute-start.3 = (f32[80,128]{1,0:T(8,128)S(1)}, f32[80,128]{1,0:T(8,128)S(1)}, u32[]{:S(2)}, u32[]{:S(2)}) collective-permute-start(f32[80,128]{1,0:T(8,128)S(1)} %get-tuple-element.41), channel_id=1, source_target_pairs={{1,2},{2,1},{3,4},{4,3},{5,6},{6,5},{9,10},{10,9},{11,12},{12,11},... | collective-permute-start | bytes 122888 | tf_op jit(solution)/shard_map/ppermute | solution.py:596
  16.5 3.1 %collective-permute-start = (f32[72,128]{1,0:T(8,128)S(1)}, f32[72,128]{1,0:T(8,128)S(1)}, u32[]{:S(2)}, u32[]{:S(2)}) collective-permute-start(f32[72,128]{1,0:T(8,128)S(1)} %get-tuple-element.38), channel_id=1, source_target_pairs={{0,8},{8,0},{16,24},{24,16},{32,40},{40,32},{48,56},{56,48},{64,72... | collective-permute-start | bytes 110600 | tf_op jit(solution)/shard_map/ppermute | solution.py:590
  22.5 13.6 %collective-permute-start.6 = (f32[96,128]{1,0:T(8,128)S(1)}, f32[96,128]{1,0:T(8,128)S(1)}, u32[]{:S(2)}, u32[]{:S(2)}) collective-permute-start(f32[96,128]{1,0:T(8,128)S(1)} %get-tuple-element.59.sent), channel_id=1, source_target_pairs={{0,1},{1,0},{2,3},{3,2},{4,5},{5,4},{6,7},{7,6},{8,9},{9,8},{10,11... | collective-permute-start | bytes 147464 | tf_op jit(solution)/shard_map/ppermute | solution.py:590
  24.4 11.6 %collective-permute-start.5 = (f32[88,128]{1,0:T(8,128)S(1)}, f32[88,128]{1,0:T(8,128)S(1)}, u32[]{:S(2)}, u32[]{:S(2)}) collective-permute-start(f32[88,128]{1,0:T(8,128)S(1)} %get-tuple-element.58), channel_id=1, source_target_pairs={{8,16},{16,8},{24,32},{32,24},{40,48},{48,40},{56,64},{64,56},{72,... | collective-permute-start | bytes 135176 | tf_op jit(solution)/shard_map/ppermute | solution.py:596
  27.9 8.2 %collective-permute-start.7 = (f32[80,128]{1,0:T(8,128)S(1)}, f32[80,128]{1,0:T(8,128)S(1)}, u32[]{:S(2)}, u32[]{:S(2)}) collective-permute-start(f32[80,128]{1,0:T(8,128)S(1)} %get-tuple-element.60), channel_id=1, source_target_pairs={{1,2},{2,1},{3,4},{4,3},{5,6},{6,5},{9,10},{10,9},{11,12},{12,11},... | collective-permute-start | bytes 122888 | tf_op jit(solution)/shard_map/ppermute | solution.py:596
  32.9 3.1 %collective-permute-start.4 = (f32[72,128]{1,0:T(8,128)S(1)}, f32[72,128]{1,0:T(8,128)S(1)}, u32[]{:S(2)}, u32[]{:S(2)}) collective-permute-start(f32[72,128]{1,0:T(8,128)S(1)} %get-tuple-element.57), channel_id=1, source_target_pairs={{0,8},{8,0},{16,24},{24,16},{32,40},{40,32},{48,56},{56,48},{64,72... | collective-permute-start | bytes 110600 | tf_op jit(solution)/shard_map/ppermute | solution.py:590

commit v3 on v2

--- a/solution.py
+++ b/solution.py
@@ -163,7 +163,7 @@
     return found
 
 
-def picked_traces(tiles, pickers, labels, proj3):
+def picked_traces(tiles, pickers, labels, proj3, extra=None):
     parts = []
     for tile in tiles:
         parts.extend(split(tile))
@@ -177,8 +177,12 @@
             at = 2 * BASIS * t
             gathered.append((column[at : at + BASIS], column[at + BASIS : at + 2 * BASIS]))
             marks.append(labels[j])
+    if extra is not None:
+        gathered.append(extra[0])
+        marks.append(extra[1])
     found = traces(gathered, marks, proj3)
-    return [found[TILES * j : TILES * (j + 1)] for j in range(jobs)]
+    picked = [found[TILES * j : TILES * (j + 1)] for j in range(jobs)]
+    return picked if extra is None else (picked, found[-1])
 
 
 def load_tiles(ref):
@@ -190,25 +194,22 @@
         ref[t] = tiles[t]
 
 
-def either(table, axis):
-    odd = lax.axis_index(axis) % 2
+def place_kernel(odd_out):
+    lane = iotas(1, LANES)[1]
+    for i, axis in enumerate(("strike", "depth")):
+        odd_out[i : i + 1, :] = lane * 0 + lax.axis_index(axis) % 2
+
+
+def either(table, odd):
+    odd = odd[:, 0 : table.shape[1]]
     twin = table[1:2, :] * (1 - odd) + table[0:1, :] * odd
     across = table[0:1, :] * (1 - odd) + table[1:2, :] * odd
     return twin, across
 
 
-def plan_kernel(strike_sends, pickers_out):
-    for j, elements in enumerate(either(strike_sends, "strike")):
-        pickers_out[:, LANES * j : LANES * (j + 1)] = picking(lane_tiled(elements))
-
-
-def plan_depth(depth_sends):
-    return picking(lane_tiled(jnp.concatenate(either(depth_sends, "depth"), axis=1)))
-
-
-def send_labels(strike_orient, depth_orient):
-    rows = [lane_tiled(row) for row in either(strike_orient, "strike")]
-    rows.append(lane_tiled(jnp.concatenate(either(depth_orient, "depth"), axis=1)))
+def send_rows(strike, depth, odd):
+    rows = [lane_tiled(row) for row in either(strike, odd[0:1, :])]
+    rows.append(lane_tiled(jnp.concatenate(either(depth, odd[1:2, :]), axis=1)))
     return rows
 
 
@@ -241,7 +242,8 @@
     jacobians,
     stiffness,
     face_proj,
-    strike_pickers,
+    odd,
+    strike_sends,
     strike_orient,
     depth_sends,
     depth_orient,
@@ -280,11 +282,11 @@
         jnp.concatenate([piece for m in range(PROJS) for piece in (face_proj[m], margin)], axis=0)
     )
     proj3_out[...] = proj3
-    pickers_out[:, 0 : 2 * LANES] = strike_pickers[...]
-    pickers_out[:, 2 * LANES : 3 * LANES] = plan_depth(depth_sends)
-    for j, row in enumerate(send_labels(strike_orient, depth_orient)):
+    for j, row in enumerate(send_rows(strike_sends, depth_sends, odd[...])):
+        pickers_out[:, LANES * j : LANES * (j + 1)] = picking(row)
+    for j, row in enumerate(send_rows(strike_orient, depth_orient, odd[...])):
         rows_out[SEND_ROW + j : SEND_ROW + j + 1, :] = row
-    send(first, pickers_out, rows_out, proj3, twin_out, across_out, depth_out, pair_out)
+    send(first, pickers_out, rows_out, proj3, (twin_out, across_out, depth_out, pair_out))
     rows_out[FAULT_ROW : FAULT_ROW + 1, :] = lane_tiled(fault_proj[...])
     rows_out[CLUSTER_ROW : CLUSTER_ROW + 1, :] = lane_tiled(cluster[...])
     rows_out[ELEM_ROW : ELEM_ROW + 1, :] = lane_tiled(fault_elem[...])
@@ -292,23 +294,22 @@
         rows_out[NEAR_ROW + f : NEAR_ROW + f + 1, :] = lane_tiled(face_orient[f : f + 1, :])
         rows_out[BEHIND_ROW + f : BEHIND_ROW + f + 1, :] = lane_tiled(neighbours[f : f + 1, :])
     reals_out[0:1, :] = lane_tiled(strength[...])
-    odd = lax.axis_index("depth") % 2
-    reals_out[1:2, :] = jnp.where(iotas(1, LANES)[1] * 0 + odd == 0, 1.0, -1.0)
-
-
-def send(values, pickers, rows, proj3, *outs):
-    found = picked_traces(
-        values,
-        pickers[...],
-        [rows[SEND_ROW + j : SEND_ROW + j + 1, :] for j in range(3)],
-        proj3,
-    )
+    reals_out[1:2, :] = jnp.where(odd[1:2, :] == 0, 1.0, -1.0)
+
+
+def send(values, pickers, rows, proj3, outs, extra=None):
+    labels = [rows[SEND_ROW + j : SEND_ROW + j + 1, :] for j in range(3)]
+    found = picked_traces(values, pickers[...], labels, proj3, extra)
+    if extra is not None:
+        found, own = found
     for out, pieces in zip(outs, (*found, found[2])):
         for t in range(TILES):
             out[FACE_ROWS * t : FACE_ROWS * (t + 1), :] = pieces[t]
         spare = out.shape[0] - TILES * FACE_ROWS
         if spare:
             out[TILES * FACE_ROWS :, :] = jnp.zeros((spare, LANES), f32)
+    if extra is not None:
+        outs[3][TILES * FACE_ROWS : TILES * FACE_ROWS + FACE_ROWS, :] = own
 
 
 def local_part(values, base, vol3, jac_coefs, own3, local_coefs, pickers, labels, proj3, outs):
@@ -500,17 +501,13 @@
     is_fast = rows[CLUSTER_ROW : CLUSTER_ROW + 1, :] == 0
     later = [jnp.where(is_fast, repeated[t], second[t]) for t in range(TILES)]
     store_tiles(later_out, later)
-    send(later, pickers, rows, proj3[...], twin_out, across_out, depth_out, pair_out)
     parts = []
     for t in range(TILES):
         parts.append(jnp.concatenate(split(first[t] + later[t]), axis=0))
     moved = mm(jnp.concatenate(parts, axis=1).astype(bf16), fault_picker[...])
-    own = traces(
-        [(moved[0:BASIS], moved[BASIS : 2 * BASIS])],
-        [rows[FAULT_ROW : FAULT_ROW + 1, :]],
-        proj3[...],
-    )[0]
-    pair_out[TILES * FACE_ROWS : TILES * FACE_ROWS + FACE_ROWS, :] = own
+    fault = (moved[0:BASIS], moved[BASIS : 2 * BASIS]), rows[FAULT_ROW : FAULT_ROW + 1, :]
+    outs = (twin_out, across_out, depth_out, pair_out)
+    send(later, pickers, rows, proj3[...], outs, fault)
 
 
 def final_kernel(
@@ -567,7 +564,7 @@
 
 FIRST_SPARE = (16, 8, 24)
 LATER_SPARE = (16, 8, 24)
-COSTS = dict(plan=100000, first_sends=100000, first_local=4, advance=8, later_local=4, combine=4)
+COSTS = dict(place=100000, first_sends=100000, first_local=4, advance=8, later_local=4, combine=4)
 
 
 def call(kernel, name, outs, *operands):
@@ -642,9 +639,7 @@
     sized = [((TILES * FACE_ROWS + more, LANES), f32) for more in FIRST_SPARE]
     resized = [((TILES * FACE_ROWS + more, LANES), f32) for more in LATER_SPARE]
 
-    (strike_pickers,) = call(
-        plan_kernel, "plan", [((LANES, 2 * LANES), bf16)], strike_sends
-    )
+    (odd,) = call(place_kernel, "place", [((8, LANES), jnp.int32)])
     base, first, second, jac_coefs, stiff3, proj3, pickers, rows, reals, *messages = call(
         send_kernel,
         "first_sends",
@@ -665,7 +660,8 @@
         jac,
         stiffness,
         proj,
-        strike_pickers,
+        odd,
+        strike_sends,
         strike_orient,
         depth_sends,
         depth_orient,

time: 38.1 us -> 37.4 us (0.982)
  the two profiles are of different devices: /device:TPU:207 before, /device:TPU:265 now
where the time goes in v3:
time: 37.4 us; the launch traced here: 37.1 us
  starting transfers between devices  27.1 us (72%)
  Pallas kernels  8.43 us (23%)
  local copies, waits for them, and re-layouts  1.03 us (3%)
    ppermute x4, starting transfers between devices, with_other_side(): return lax.ppermute(message, axis, pairs)  16.7 us
    ppermute x4, starting transfers between devices, with_twin(): return lax.ppermute(message, axis, [(i, i ^ 1) for i in range(length)])  10.4 us
    pallas_call x6, Pallas kernels, call(): pl.pallas_call(kernel, out_shape=[jax.ShapeDtypeStruct(shape, dtype) for...  8.43 us
    unnamed x36, local copies, waits for them, and re-layouts  1.03 us
  transfers between devices with their start and end apart: 8, of which 1 were waited for; matrix products, arithmetic and copies ran while one was open for 0% of the time, Pallas kernels for 5%

profile of v3, /device:TPU:265, one launch (start us, length us, event | category | flops | bytes accessed | tf_op | source)
XLA Modules:
  0.0 37.1 jit_solution(143225349279168128)
XLA Ops:
  0.1 0.0 copy-start.8
  0.1 0.0 copy-start.10
  0.1 0.0 copy-start.14
  0.1 0.8 %copy-done.2 = f32[12,56,21]{1,2,0:T(8,128)S(1)} copy-done((f32[12,56,21]{1,2,0:T(8,128)S(1)}, f32[12,56,21]{1,2,0:T(8,128)}, u32[]{:S(2)}) %copy-start.2) | copy-done | bytes 56472
  0.9 0.1 copy-done.7
  1.0 0.1 copy-done.5
  1.0 0.1 copy-done.6
  1.2 0.0 copy-start
  1.2 0.0 copy-start.1
  1.2 0.0 copy-start.3
  1.2 0.0 copy-start.4
  1.2 2.4 %first_sends.1 = (f32[3,56,128]{2,1,0:T(8,128)S(1)}, f32[3,56,128]{2,1,0:T(8,128)S(1)}, f32[3,56,128]{2,1,0:T(8,128)S(1)}, f32[21,4,128]{2,1,0:T(4,128)S(1)}, bf...) custom-call(f32[288,56]{1,0:T(8,128)S(1)} %bitcast.21, ...), custom_call_target="tpu_custom_call" | custom-call | flops 99999997952 | bytes 99999997952 | tf_op jit(solution)/shard_map/first_sends/pallas_call | solution.py:572
  3.6 2.1 %collective-permute-start.2 = (f32[96,128]{1,0:T(8,128)S(1)}, f32[96,128]{1,0:T(8,128)S(1)}, u32[]{:S(2)}, u32[]{:S(2)}) collective-permute-start(f32[96,128]{1,0:T(8,128)S(1)} %get-tuple-element.40), channel_id=1, source_target_pairs={{0,1},{1,0},{2,3},{3,2},{4,5},{5,4},{6,7},{7,6},{8,9},{9,8},{10,11... | collective-permute-start | bytes 147464 | tf_op jit(solution)/shard_map/ppermute | solution.py:587
  5.7 3.9 %collective-permute-start.1 = (f32[88,128]{1,0:T(8,128)S(1)}, f32[88,128]{1,0:T(8,128)S(1)}, u32[]{:S(2)}, u32[]{:S(2)}) collective-permute-start(f32[88,128]{1,0:T(8,128)S(1)} %get-tuple-element.39), channel_id=1, source_target_pairs={{8,16},{16,8},{24,32},{32,24},{40,48},{48,40},{56,64},{64,56},{72,... | collective-permute-start | bytes 135176 | tf_op jit(solution)/shard_map/ppermute | solution.py:593
  9.6 4.3 %collective-permute-start.3 = (f32[80,128]{1,0:T(8,128)S(1)}, f32[80,128]{1,0:T(8,128)S(1)}, u32[]{:S(2)}, u32[]{:S(2)}) collective-permute-start(f32[80,128]{1,0:T(8,128)S(1)} %get-tuple-element.41), channel_id=1, source_target_pairs={{1,2},{2,1},{3,4},{4,3},{5,6},{6,5},{9,10},{10,9},{11,12},{12,11},... | collective-permute-start | bytes 122888 | tf_op jit(solution)/shard_map/ppermute | solution.py:593
  14.0 2.1 %collective-permute-start = (f32[72,128]{1,0:T(8,128)S(1)}, f32[72,128]{1,0:T(8,128)S(1)}, u32[]{:S(2)}, u32[]{:S(2)}) collective-permute-start(f32[72,128]{1,0:T(8,128)S(1)} %get-tuple-element.38), channel_id=1, source_target_pairs={{0,8},{8,0},{16,24},{24,16},{32,40},{40,32},{48,56},{56,48},{64,72... | collective-permute-start | bytes 110600 | tf_op jit(solution)/shard_map/ppermute | solution.py:587
  16.1 1.0 %first_local.1 = (f32[3,56,128]{2,1,0:T(8,128)S(1)}, f32[3,96,128]{2,1,0:T(8,128)S(1)}, f32[3,96,128]{2,1,0:T(8,128)S(1)}, bf16[168,168]{1,0:T(8,128)(2,1)S(1)},...) custom-call(f32[3,56,128]{2,1,0:T(8,128)S(1)} %get-tuple-element.42., ...), custom_call_target="tpu_custom_call" | custom-call | flops 4000000 | bytes 4000000 | tf_op jit(solution)/shard_map/first_local/pallas_call | solution.py:572
  17.2 0.0 collective-permute-done.twin
  17.2 0.0 collective-permute-done.3.beyond
  17.2 0.0 collective-permute-done.1.across
  17.2 0.0 collective-permute-done.2.pair
  17.2 2.7 %advance.1 = (f32[3,56,128]{2,1,0:T(8,128)S(1)}, f32[3,56,128]{2,1,0:T(8,128)S(1)}, f32[72,128]{1,0:T(8,128)S(1)}, f32[88,128]{1,0:T(8,128)S(1)}, f32[80,128]{1,0:T(8,128)S(1)}, /*index=5*/f32[96,128]{1,0:T(8,128)S(1)}) custom-call(f32[72,128]{1,0:T(8,128)S(1)} %collective-permute-done.twin, f32[88,128]{1,0:T(8,128)S(1)} %collective-permute-done.1.across, ...), custom_call_target="tpu_custom_call" | custom-call | flops 8000000 | bytes 8000000 | tf_op jit(solution)/shard_map/advance/pallas_call | solution.py:572
  19.9 1.9 %collective-permute-start.6 = (f32[96,128]{1,0:T(8,128)S(1)}, f32[96,128]{1,0:T(8,128)S(1)}, u32[]{:S(2)}, u32[]{:S(2)}) collective-permute-start(f32[96,128]{1,0:T(8,128)S(1)} %get-tuple-element.59.sent), channel_id=1, source_target_pairs={{0,1},{1,0},{2,3},{3,2},{4,5},{5,4},{6,7},{7,6},{8,9},{9,8},{10,11... | collective-permute-start | bytes 147464 | tf_op jit(solution)/shard_map/ppermute | solution.py:587
  21.8 3.3 %collective-permute-start.5 = (f32[88,128]{1,0:T(8,128)S(1)}, f32[88,128]{1,0:T(8,128)S(1)}, u32[]{:S(2)}, u32[]{:S(2)}) collective-permute-start(f32[88,128]{1,0:T(8,128)S(1)} %get-tuple-element.58), channel_id=1, source_target_pairs={{8,16},{16,8},{24,32},{32,24},{40,48},{48,40},{56,64},{64,56},{72,... | collective-permute-start | bytes 135176 | tf_op jit(solution)/shard_map/ppermute | solution.py:593
  25.1 5.1 %collective-permute-start.7 = (f32[80,128]{1,0:T(8,128)S(1)}, f32[80,128]{1,0:T(8,128)S(1)}, u32[]{:S(2)}, u32[]{:S(2)}) collective-permute-start(f32[80,128]{1,0:T(8,128)S(1)} %get-tuple-element.60), channel_id=1, source_target_pairs={{1,2},{2,1},{3,4},{4,3},{5,6},{6,5},{9,10},{10,9},{11,12},{12,11},... | collective-permute-start | bytes 122888 | tf_op jit(solution)/shard_map/ppermute | solution.py:593
  30.3 4.3 %collective-permute-start.4 = (f32[72,128]{1,0:T(8,128)S(1)}, f32[72,128]{1,0:T(8,128)S(1)}, u32[]{:S(2)}, u32[]{:S(2)}) collective-permute-start(f32[72,128]{1,0:T(8,128)S(1)} %get-tuple-element.57), channel_id=1, source_target_pairs={{0,8},{8,0},{16,24},{24,16},{32,40},{40,32},{48,56},{56,48},{64,72... | collective-permute-start | bytes 110600 | tf_op jit(solution)/shard_map/ppermute | solution.py:587
  34.6 0.7 %later_local.1 = (f32[3,56,128]{2,1,0:T(8,128)S(1)}, f32[3,96,128]{2,1,0:T(8,128)S(1)}, f32[3,96,128]{2,1,0:T(8,128)S(1)}) custom-call(f32[3,56,128]{2,1,0:T(8,128)S(1)} %get-tuple-element.61.values, f32[3,56,128]{2,1,0:T(8,128)S(1)} %get-tuple-element.62.base, f32[21,4,128]{2,1,0:T(4,128)S(1)} %get-tuple-element.44.jac_coefs, ...), custom_call_target="tpu_custom_call" | custom-call | flops 4000000 | bytes 4000000 | tf_op jit(solution)/shard_map/later_local/pallas_call | solution.py:572
  35.3 0.1 collective-permute-done.4.twin
  35.4 0.0 collective-permute-done.7.beyond
  35.4 0.0 collective-permute-done.5.across
  35.4 0.0 collective-permute-done.6.pair
  35.5 1.6 %combine.1 = f32[288,56]{1,0:T(8,128)} custom-call(f32[72,128]{1,0:T(8,128)S(1)} %collective-permute-done.4.twin, f32[88,128]{1,0:T(8,128)S(1)} %collective-permute-done.5.across, f32[96,128]{1,0:T(8,128)S(1)} %collective-permute-done.6.pair, f32[80,128]{1,0:T(8,128)S(1)} %collective-permute-done.7.beyond, bf16[384,512]{1,0:T(8,128)(2,1)S(1)} %get-tuple-element.47.halo, ...), custom_call_target="tpu_custom_call" | custom-call | flops 4000000 | bytes 4000000 | tf_op jit(solution)/shard_map/combine/pallas_call | solution.py:572
  (26 shorter events, 0.1 us)
Async XLA Ops:
  0.0 0.9 %copy-start.2 = (f32[12,56,21]{1,2,0:T(8,128)S(1)}, f32[12,56,21]{1,2,0:T(8,128)}, u32[]{:S(2)}) copy-start(f32[12,56,21]{1,2,0:T(8,128)} %param.24) | copy-start | bytes 169348
  0.0 1.0 %copy-start.7 = (f32[3,56,56]{2,1,0:T(8,128)S(1)}, f32[3,56,56]{2,1,0:T(8,128)}, u32[]{:S(2)}) copy-start(f32[3,56,56]{2,1,0:T(8,128)} %stiffness.1) | copy-start | bytes 112900
  0.0 1.0 %copy-start.5 = (f32[3,9,9,32]{3,0,2,1:T(4,128)S(1)}, f32[3,9,9,32]{3,0,2,1:T(4,128)}, u32[]{:S(2)}) copy-start(f32[3,9,9,32]{3,0,2,1:T(4,128)} %param.19) | copy-start | bytes 93316
  0.0 1.1 %copy-start.6 = (f32[9,56,32]{1,2,0:T(8,128)S(1)}, f32[9,56,32]{1,2,0:T(8,128)}, u32[]{:S(2)}) copy-start(f32[9,56,32]{1,2,0:T(8,128)} %param.18) | copy-start | bytes 193540
  0.0 1.1 %copy-start.9 = (s32[4,32]{1,0:T(4,128)S(1)}, s32[4,32]{1,0:T(4,128)}, u32[]{:S(2)}) copy-start(s32[4,32]{1,0:T(4,128)} %face_orient.1) | copy-start | bytes 1540
  0.0 1.1 %copy-start.11 = (s32[2,32]{1,0:T(2,128)S(1)}, s32[2,32]{1,0:T(2,128)}, u32[]{:S(2)}) copy-start(s32[2,32]{1,0:T(2,128)} %strike_orient.1) | copy-start | bytes 772
  0.0 1.1 %copy-start.12 = (s32[2,16]{1,0:T(2,128)S(1)}, s32[2,16]{1,0:T(2,128)}, u32[]{:S(2)}) copy-start(s32[2,16]{1,0:T(2,128)} %depth_sends.1) | copy-start | bytes 388
  0.0 1.1 %copy-start.13 = (s32[2,16]{1,0:T(2,128)S(1)}, s32[2,16]{1,0:T(2,128)}, u32[]{:S(2)}) copy-start(s32[2,16]{1,0:T(2,128)} %depth_orient.1) | copy-start | bytes 388
  0.1 1.1 %copy-start.15 = (f32[32]{0:T(128)S(1)}, f32[32]{0:T(128)}, u32[]{:S(2)}) copy-start(f32[32]{0:T(128)} %param.26) | copy-start | bytes 388
  0.1 1.1 %copy-start.16 = (s32[32]{0:T(128)S(1)}, s32[32]{0:T(128)}, u32[]{:S(2)}) copy-start(s32[32]{0:T(128)} %param.34) | copy-start | bytes 388
  0.1 1.1 %copy-start.17 = (s32[32]{0:T(128)S(1)}, s32[32]{0:T(128)}, u32[]{:S(2)}) copy-start(s32[32]{0:T(128)} %param.35) | copy-start | bytes 388
  0.1 1.0 %copy-start.8 = (s32[4,32]{1,0:T(4,128)S(1)}, s32[4,32]{1,0:T(4,128)}, u32[]{:S(2)}) copy-start(s32[4,32]{1,0:T(4,128)} %neighbours.1) | copy-start | bytes 1540
  0.1 1.0 %copy-start.10 = (s32[2,32]{1,0:T(2,128)S(1)}, s32[2,32]{1,0:T(2,128)}, u32[]{:S(2)}) copy-start(s32[2,32]{1,0:T(2,128)} %strike_sends.1) | copy-start | bytes 772
  0.1 1.0 %copy-start.14 = (s32[32]{0:T(128)S(1)}, s32[32]{0:T(128)}, u32[]{:S(2)}) copy-start(s32[32]{0:T(128)} %param.27) | copy-start | bytes 388
  1.2 14.9 %copy-start = (f32[4,9,9,32]{3,0,2,1:T(4,128)S(1)}, f32[4,9,9,32]{3,0,2,1:T(4,128)}, u32[]{:S(2)}) copy-start(f32[4,9,9,32]{3,0,2,1:T(4,128)} %param.20) | copy-start | bytes 124420
  1.2 14.9 %copy-start.1 = (f32[4,9,9,32]{3,0,2,1:T(4,128)S(1)}, f32[4,9,9,32]{3,0,2,1:T(4,128)}, u32[]{:S(2)}) copy-start(f32[4,9,9,32]{3,0,2,1:T(4,128)} %param.21) | copy-start | bytes 124420
  1.2 14.9 %copy-start.3 = (f32[3,56,56]{2,1,0:T(8,128)S(1)}, f32[3,56,56]{2,1,0:T(8,128)}, u32[]{:S(2)}) copy-start(f32[3,56,56]{2,1,0:T(8,128)} %volume.1) | copy-start | bytes 112900
  1.2 14.9 %copy-start.4 = (f32[4,21,56]{2,0,1:T(4,128)S(1)}, f32[4,21,56]{2,0,1:T(4,128)}, u32[]{:S(2)}) copy-start(f32[4,21,56]{2,0,1:T(4,128)} %param.25) | copy-start | bytes 56452
  3.6 13.6 %collective-permute-start.2 = (f32[96,128]{1,0:T(8,128)S(1)}, f32[96,128]{1,0:T(8,128)S(1)}, u32[]{:S(2)}, u32[]{:S(2)}) collective-permute-start(f32[96,128]{1,0:T(8,128)S(1)} %get-tuple-element.40), channel_id=1, source_target_pairs={{0,1},{1,0},{2,3},{3,2},{4,5},{5,4},{6,7},{7,6},{8,9},{9,8},{10,11... | collective-permute-start | bytes 147464 | tf_op jit(solution)/shard_map/ppermute | solution.py:587
  5.7 11.5 %collective-permute-start.1 = (f32[88,128]{1,0:T(8,128)S(1)}, f32[88,128]{1,0:T(8,128)S(1)}, u32[]{:S(2)}, u32[]{:S(2)}) collective-permute-start(f32[88,128]{1,0:T(8,128)S(1)} %get-tuple-element.39), channel_id=1, source_target_pairs={{8,16},{16,8},{24,32},{32,24},{40,48},{48,40},{56,64},{64,56},{72,... | collective-permute-start | bytes 135176 | tf_op jit(solution)/shard_map/ppermute | solution.py:593
  9.6 7.6 %collective-permute-start.3 = (f32[80,128]{1,0:T(8,128)S(1)}, f32[80,128]{1,0:T(8,128)S(1)}, u32[]{:S(2)}, u32[]{:S(2)}) collective-permute-start(f32[80,128]{1,0:T(8,128)S(1)} %get-tuple-element.41), channel_id=1, source_target_pairs={{1,2},{2,1},{3,4},{4,3},{5,6},{6,5},{9,10},{10,9},{11,12},{12,11},... | collective-permute-start | bytes 122888 | tf_op jit(solution)/shard_map/ppermute | solution.py:593
  14.0 3.2 %collective-permute-start = (f32[72,128]{1,0:T(8,128)S(1)}, f32[72,128]{1,0:T(8,128)S(1)}, u32[]{:S(2)}, u32[]{:S(2)}) collective-permute-start(f32[72,128]{1,0:T(8,128)S(1)} %get-tuple-element.38), channel_id=1, source_target_pairs={{0,8},{8,0},{16,24},{24,16},{32,40},{40,32},{48,56},{56,48},{64,72... | collective-permute-start | bytes 110600 | tf_op jit(solution)/shard_map/ppermute | solution.py:587
  19.9 15.5 %collective-permute-start.6 = (f32[96,128]{1,0:T(8,128)S(1)}, f32[96,128]{1,0:T(8,128)S(1)}, u32[]{:S(2)}, u32[]{:S(2)}) collective-permute-start(f32[96,128]{1,0:T(8,128)S(1)} %get-tuple-element.59.sent), channel_id=1, source_target_pairs={{0,1},{1,0},{2,3},{3,2},{4,5},{5,4},{6,7},{7,6},{8,9},{9,8},{10,11... | collective-permute-start | bytes 147464 | tf_op jit(solution)/shard_map/ppermute | solution.py:587
  21.8 13.6 %collective-permute-start.5 = (f32[88,128]{1,0:T(8,128)S(1)}, f32[88,128]{1,0:T(8,128)S(1)}, u32[]{:S(2)}, u32[]{:S(2)}) collective-permute-start(f32[88,128]{1,0:T(8,128)S(1)} %get-tuple-element.58), channel_id=1, source_target_pairs={{8,16},{16,8},{24,32},{32,24},{40,48},{48,40},{56,64},{64,56},{72,... | collective-permute-start | bytes 135176 | tf_op jit(solution)/shard_map/ppermute | solution.py:593
  25.1 10.3 %collective-permute-start.7 = (f32[80,128]{1,0:T(8,128)S(1)}, f32[80,128]{1,0:T(8,128)S(1)}, u32[]{:S(2)}, u32[]{:S(2)}) collective-permute-start(f32[80,128]{1,0:T(8,128)S(1)} %get-tuple-element.60), channel_id=1, source_target_pairs={{1,2},{2,1},{3,4},{4,3},{5,6},{6,5},{9,10},{10,9},{11,12},{12,11},... | collective-permute-start | bytes 122888 | tf_op jit(solution)/shard_map/ppermute | solution.py:593
  30.3 5.2 %collective-permute-start.4 = (f32[72,128]{1,0:T(8,128)S(1)}, f32[72,128]{1,0:T(8,128)S(1)}, u32[]{:S(2)}, u32[]{:S(2)}) collective-permute-start(f32[72,128]{1,0:T(8,128)S(1)} %get-tuple-element.57), channel_id=1, source_target_pairs={{0,8},{8,0},{16,24},{24,16},{32,40},{40,32},{48,56},{56,48},{64,72... | collective-permute-start | bytes 110600 | tf_op jit(solution)/shard_map/ppermute | solution.py:587

commit v4 on v3

--- a/solution.py
+++ b/solution.py
@@ -101,13 +101,20 @@
     return found[0], found[1], last
 
 
-def volume_like(tiles, weights3, coefs):
-    whole = mm(weights3, stacked(tiles))
-    applied = [whole[:, LANES * t : LANES * (t + 1)] for t in range(TILES)]
+def by_lanes(product):
+    return [product[:, LANES * t : LANES * (t + 1)] for t in range(TILES)]
+
+
+def volume_terms(product, coefs):
+    applied = by_lanes(product)
     terms = [
         (d, [part[BASIS * d : BASIS * (d + 1)] for part in applied]) for d in range(3)
     ]
     return list(contract(coefs, terms))
+
+
+def volume_like(tiles, weights3, coefs):
+    return volume_terms(mm(weights3, stacked(tiles)), coefs)
 
 
 def integrals(tiles, weights3, coefs, with_second):
@@ -312,17 +319,17 @@
         outs[3][TILES * FACE_ROWS : TILES * FACE_ROWS + FACE_ROWS, :] = own
 
 
-def local_part(values, base, vol3, jac_coefs, own3, local_coefs, pickers, labels, proj3, outs):
+def local_part(values, base, inner3, jac_coefs, local_coefs, pickers, labels, proj3, outs):
     pre_out, flux_out, near_out = outs
-    interior = volume_like(values, vol3, jac_coefs)
+    product = mm(inner3, stacked(values))
+    interior = volume_terms(product, jac_coefs)
     for t in range(TILES):
         pre_out[t] = base[t] + interior[t]
-    own = mm(own3, stacked(values))
     for f in range(FACES):
         at = FACE_ROWS * f
-        rows = own[at : at + FACE_ROWS]
+        rows = product[3 * BASIS + at : 3 * BASIS + at + FACE_ROWS]
         fluxes = contract(
-            local_coefs, [(f, [rows[:, LANES * t : LANES * (t + 1)] for t in range(TILES)])]
+            local_coefs, [(f, by_lanes(rows))]
         )
         for t in range(TILES):
             flux_out[t, at : at + FACE_ROWS, :] = fluxes[t]
@@ -351,8 +358,7 @@
     pre_out,
     flux_out,
     near_out,
-    vol3_out,
-    own3_out,
+    inner3_out,
     local_coefs,
     neigh_coefs,
     lift3_out,
@@ -363,13 +369,12 @@
     picks = fault_pickers(rows[ELEM_ROW : ELEM_ROW + 1, :])
     fault_pickers_out[...] = jnp.concatenate(picks, axis=0)
     plan_faces(rows, near_pickers_out, halo_out)
-    vol3 = left3(jnp.concatenate([volume[d].T for d in range(3)], axis=0))
-    vol3_out[...] = vol3
     margin = jnp.zeros((FACE_ROWS - FACE_BASIS, BASIS), f32)
-    own3 = left3(
-        jnp.concatenate([piece for f in range(FACES) for piece in (face_proj[3 * f], margin)], axis=0)
-    )
-    own3_out[...] = own3
+    pieces = [volume[d].T for d in range(3)]
+    for f in range(FACES):
+        pieces += [face_proj[3 * f], margin]
+    inner3 = left3(jnp.concatenate(pieces, axis=0))
+    inner3_out[...] = inner3
     build_coefs(flux_local, local_coefs)
     build_coefs(flux_neigh, neigh_coefs)
     lift3_out[...] = left3(
@@ -380,9 +385,8 @@
     local_part(
         load_tiles(values),
         load_tiles(base),
-        vol3,
+        inner3,
         jac_coefs,
-        own3,
         local_coefs,
         near_pickers_out[...],
         near_labels(rows),
@@ -398,8 +402,7 @@
     proj3,
     pickers,
     rows,
-    vol3,
-    own3,
+    inner3,
     local_coefs,
     pre_out,
     flux_out,
@@ -408,9 +411,8 @@
     local_part(
         load_tiles(values),
         load_tiles(base),
-        vol3[...],
+        inner3[...],
         jac_coefs,
-        own3[...],
         local_coefs,
         pickers[...],
         near_labels(rows),
@@ -562,7 +564,7 @@
     result[2 * LANES : 2 * LANES + WIDE, :] = new[2].T[3 * WIDE : 4 * WIDE, :]
 
 
-FIRST_SPARE = (16, 8, 24)
+FIRST_SPARE = (24, 8, 16)
 LATER_SPARE = (16, 8, 24)
 COSTS = dict(place=100000, first_sends=100000, first_local=4, advance=8, later_local=4, combine=4)
 
@@ -674,15 +676,14 @@
     )
     twin, across, sideways, pair = messages
     arrived = exchanged(twin, across, pair, sideways)
-    pre, flux, near, vol3, own3, local_coefs, neigh_coefs, *rest = call(
+    pre, flux, near, inner3, local_coefs, neigh_coefs, *rest = call(
         prepare_kernel,
         "first_local",
         [
             full,
             faces,
             faces,
-            ((3 * BASIS, 3 * BASIS), bf16),
-            ((FACES * FACE_ROWS, 3 * BASIS), bf16),
+            ((3 * BASIS + FACES * FACE_ROWS, 3 * BASIS), bf16),
             coefs,
             coefs,
             ((BASIS, 3 * FACES * FACE_ROWS), bf16),
@@ -733,8 +734,7 @@
         proj3,
         near_pickers,
         rows,
-        vol3,
-        own3,
+        inner3,
         local_coefs,
     )
     (result,) = call(

time: 37.4 us -> 37.4 us (level)
  the two profiles are of different devices: /device:TPU:265 before, /device:TPU:207 now
where the time goes in v4:
time: 37.4 us; the launch traced here: 37 us
  starting transfers between devices  26.7 us (71%)
  Pallas kernels  8.41 us (22%)
  local copies, waits for them, and re-layouts  1.03 us (3%)
  waiting for transfers between devices  0.58 us (2%)
    ppermute x4, starting transfers between devices, with_other_side(): return lax.ppermute(message, axis, pairs)  18.9 us
    pallas_call x6, Pallas kernels, call(): pl.pallas_call(kernel, out_shape=[jax.ShapeDtypeStruct(shape, dtype) for...  8.41 us
    ppermute x4, starting transfers between devices, with_twin(): return lax.ppermute(message, axis, [(i, i ^ 1) for i in range(length)])  7.84 us
    unnamed x36, local copies, waits for them, and re-layouts  1.03 us
  transfers between devices with their start and end apart: 8, of which 2 were waited for; matrix products, arithmetic and copies ran while one was open for 0% of the time, Pallas kernels for 5%

profile of v4, /device:TPU:207, one launch (start us, length us, event | category | flops | bytes accessed | tf_op | source)
XLA Modules:
  0.0 37.0 jit_solution(5798782167546417515)
XLA Ops:
  0.1 0.0 copy-start.8
  0.1 0.0 copy-start.10
  0.1 0.0 copy-start.14
  0.1 0.8 %copy-done.2 = f32[12,56,21]{1,2,0:T(8,128)S(1)} copy-done((f32[12,56,21]{1,2,0:T(8,128)S(1)}, f32[12,56,21]{1,2,0:T(8,128)}, u32[]{:S(2)}) %copy-start.2) | copy-done | bytes 56472
  0.9 0.1 copy-done.7
  1.0 0.1 copy-done.5
  1.0 0.1 copy-done.6
  1.2 0.0 copy-start
  1.2 0.0 copy-start.1
  1.2 0.0 copy-start.3
  1.2 0.0 copy-start.4
  1.2 2.4 %first_sends.1 = (f32[3,56,128]{2,1,0:T(8,128)S(1)}, f32[3,56,128]{2,1,0:T(8,128)S(1)}, f32[3,56,128]{2,1,0:T(8,128)S(1)}, f32[21,4,128]{2,1,0:T(4,128)S(1)}, bf...) custom-call(f32[288,56]{1,0:T(8,128)S(1)} %bitcast.21, ...), custom_call_target="tpu_custom_call" | custom-call | flops 99999997952 | bytes 99999997952 | tf_op jit(solution)/shard_map/first_sends/pallas_call | solution.py:574
  3.6 5.7 %collective-permute-start.1 = (f32[96,128]{1,0:T(8,128)S(1)}, f32[96,128]{1,0:T(8,128)S(1)}, u32[]{:S(2)}, u32[]{:S(2)}) collective-permute-start(f32[96,128]{1,0:T(8,128)S(1)} %get-tuple-element.38), channel_id=1, source_target_pairs={{8,16},{16,8},{24,32},{32,24},{40,48},{48,40},{56,64},{64,56},{72,... | collective-permute-start | bytes 147464 | tf_op jit(solution)/shard_map/ppermute | solution.py:595
  9.3 2.1 %collective-permute-start.2 = (f32[88,128]{1,0:T(8,128)S(1)}, f32[88,128]{1,0:T(8,128)S(1)}, u32[]{:S(2)}, u32[]{:S(2)}) collective-permute-start(f32[88,128]{1,0:T(8,128)S(1)} %get-tuple-element.39), channel_id=1, source_target_pairs={{0,1},{1,0},{2,3},{3,2},{4,5},{5,4},{6,7},{7,6},{8,9},{9,8},{10,11... | collective-permute-start | bytes 135176 | tf_op jit(solution)/shard_map/ppermute | solution.py:589
  11.4 4.3 %collective-permute-start.3 = (f32[80,128]{1,0:T(8,128)S(1)}, f32[80,128]{1,0:T(8,128)S(1)}, u32[]{:S(2)}, u32[]{:S(2)}) collective-permute-start(f32[80,128]{1,0:T(8,128)S(1)} %get-tuple-element.40), channel_id=1, source_target_pairs={{1,2},{2,1},{3,4},{4,3},{5,6},{6,5},{9,10},{10,9},{11,12},{12,11},... | collective-permute-start | bytes 122888 | tf_op jit(solution)/shard_map/ppermute | solution.py:595
  15.7 1.9 %collective-permute-start = (f32[72,128]{1,0:T(8,128)S(1)}, f32[72,128]{1,0:T(8,128)S(1)}, u32[]{:S(2)}, u32[]{:S(2)}) collective-permute-start(f32[72,128]{1,0:T(8,128)S(1)} %get-tuple-element.37), channel_id=1, source_target_pairs={{0,8},{8,0},{16,24},{24,16},{32,40},{40,32},{48,56},{56,48},{64,72... | collective-permute-start | bytes 110600 | tf_op jit(solution)/shard_map/ppermute | solution.py:589
  17.7 1.0 %first_local.1 = (f32[3,56,128]{2,1,0:T(8,128)S(1)}, f32[3,96,128]{2,1,0:T(8,128)S(1)}, f32[3,96,128]{2,1,0:T(8,128)S(1)}, bf16[264,168]{1,0:T(8,128)(2,1)S(1)},...) custom-call(f32[3,56,128]{2,1,0:T(8,128)S(1)} %get-tuple-element.41., ...), custom_call_target="tpu_custom_call" | custom-call | flops 4000000 | bytes 4000000 | tf_op jit(solution)/shard_map/first_local/pallas_call | solution.py:574
  18.7 0.1 collective-permute-done.twin
  18.8 0.0 collective-permute-done.3.beyond
  18.8 0.0 collective-permute-done.2.pair
  18.8 0.0 collective-permute-done.1.across
  18.8 2.7 %advance.1 = (f32[3,56,128]{2,1,0:T(8,128)S(1)}, f32[3,56,128]{2,1,0:T(8,128)S(1)}, f32[72,128]{1,0:T(8,128)S(1)}, f32[88,128]{1,0:T(8,128)S(1)}, f32[80,128]{1,0:T(8,128)S(1)}, /*index=5*/f32[96,128]{1,0:T(8,128)S(1)}) custom-call(f32[72,128]{1,0:T(8,128)S(1)} %collective-permute-done.twin, f32[96,128]{1,0:T(8,128)S(1)} %collective-permute-done.1.across, ...), custom_call_target="tpu_custom_call" | custom-call | flops 8000000 | bytes 8000000 | tf_op jit(solution)/shard_map/advance/pallas_call | solution.py:574
  21.5 1.9 %collective-permute-start.6 = (f32[96,128]{1,0:T(8,128)S(1)}, f32[96,128]{1,0:T(8,128)S(1)}, u32[]{:S(2)}, u32[]{:S(2)}) collective-permute-start(f32[96,128]{1,0:T(8,128)S(1)} %get-tuple-element.58.sent), channel_id=1, source_target_pairs={{0,1},{1,0},{2,3},{3,2},{4,5},{5,4},{6,7},{7,6},{8,9},{9,8},{10,11... | collective-permute-start | bytes 147464 | tf_op jit(solution)/shard_map/ppermute | solution.py:589
  23.4 3.8 %collective-permute-start.5 = (f32[88,128]{1,0:T(8,128)S(1)}, f32[88,128]{1,0:T(8,128)S(1)}, u32[]{:S(2)}, u32[]{:S(2)}) collective-permute-start(f32[88,128]{1,0:T(8,128)S(1)} %get-tuple-element.57), channel_id=1, source_target_pairs={{8,16},{16,8},{24,32},{32,24},{40,48},{48,40},{56,64},{64,56},{72,... | collective-permute-start | bytes 135176 | tf_op jit(solution)/shard_map/ppermute | solution.py:595
  27.2 5.1 %collective-permute-start.7 = (f32[80,128]{1,0:T(8,128)S(1)}, f32[80,128]{1,0:T(8,128)S(1)}, u32[]{:S(2)}, u32[]{:S(2)}) collective-permute-start(f32[80,128]{1,0:T(8,128)S(1)} %get-tuple-element.59), channel_id=1, source_target_pairs={{1,2},{2,1},{3,4},{4,3},{5,6},{6,5},{9,10},{10,9},{11,12},{12,11},... | collective-permute-start | bytes 122888 | tf_op jit(solution)/shard_map/ppermute | solution.py:595
  32.3 1.9 %collective-permute-start.4 = (f32[72,128]{1,0:T(8,128)S(1)}, f32[72,128]{1,0:T(8,128)S(1)}, u32[]{:S(2)}, u32[]{:S(2)}) collective-permute-start(f32[72,128]{1,0:T(8,128)S(1)} %get-tuple-element.56), channel_id=1, source_target_pairs={{0,8},{8,0},{16,24},{24,16},{32,40},{40,32},{48,56},{56,48},{64,72... | collective-permute-start | bytes 110600 | tf_op jit(solution)/shard_map/ppermute | solution.py:589
  34.2 0.7 %later_local.1 = (f32[3,56,128]{2,1,0:T(8,128)S(1)}, f32[3,96,128]{2,1,0:T(8,128)S(1)}, f32[3,96,128]{2,1,0:T(8,128)S(1)}) custom-call(f32[3,56,128]{2,1,0:T(8,128)S(1)} %get-tuple-element.60.values, f32[3,56,128]{2,1,0:T(8,128)S(1)} %get-tuple-element.61.base, f32[21,4,128]{2,1,0:T(4,128)S(1)} %get-tuple-element.43.jac_coefs, ...), custom_call_target="tpu_custom_call" | custom-call | flops 4000000 | bytes 4000000 | tf_op jit(solution)/shard_map/later_local/pallas_call | solution.py:574
  35.0 0.5 %collective-permute-done.4.twin = f32[72,128]{1,0:T(8,128)S(1)} collective-permute-done((f32[72,128]{1,0:T(8,128)S(1)}, f32[72,128]{1,0:T(8,128)S(1)}, u32[]{:S(2)}, u32[]{:S(2)}) %collective-permute-start.4) | collective-permute-done | bytes 36896 | tf_op jit(solution)/shard_map/ppermute | solution.py:589
  35.4 0.0 collective-permute-done.7.beyond
  35.4 0.0 collective-permute-done.5.across
  35.4 0.0 collective-permute-done.6.pair
  35.4 1.6 %combine.1 = f32[288,56]{1,0:T(8,128)} custom-call(f32[72,128]{1,0:T(8,128)S(1)} %collective-permute-done.4.twin, f32[88,128]{1,0:T(8,128)S(1)} %collective-permute-done.5.across, f32[96,128]{1,0:T(8,128)S(1)} %collective-permute-done.6.pair, f32[80,128]{1,0:T(8,128)S(1)} %collective-permute-done.7.beyond, bf16[384,512]{1,0:T(8,128)(2,1)S(1)} %get-tuple-element.46.halo, ...), custom_call_target="tpu_custom_call" | custom-call | flops 4000000 | bytes 4000000 | tf_op jit(solution)/shard_map/combine/pallas_call | solution.py:574
  (26 shorter events, 0.1 us)
Async XLA Ops:
  0.0 0.9 %copy-start.2 = (f32[12,56,21]{1,2,0:T(8,128)S(1)}, f32[12,56,21]{1,2,0:T(8,128)}, u32[]{:S(2)}) copy-start(f32[12,56,21]{1,2,0:T(8,128)} %param.24) | copy-start | bytes 169348
  0.0 1.0 %copy-start.7 = (f32[3,56,56]{2,1,0:T(8,128)S(1)}, f32[3,56,56]{2,1,0:T(8,128)}, u32[]{:S(2)}) copy-start(f32[3,56,56]{2,1,0:T(8,128)} %stiffness.1) | copy-start | bytes 112900
  0.0 1.0 %copy-start.5 = (f32[3,9,9,32]{3,0,2,1:T(4,128)S(1)}, f32[3,9,9,32]{3,0,2,1:T(4,128)}, u32[]{:S(2)}) copy-start(f32[3,9,9,32]{3,0,2,1:T(4,128)} %param.19) | copy-start | bytes 93316
  0.0 1.1 %copy-start.6 = (f32[9,56,32]{1,2,0:T(8,128)S(1)}, f32[9,56,32]{1,2,0:T(8,128)}, u32[]{:S(2)}) copy-start(f32[9,56,32]{1,2,0:T(8,128)} %param.18) | copy-start | bytes 193540
  0.0 1.1 %copy-start.9 = (s32[4,32]{1,0:T(4,128)S(1)}, s32[4,32]{1,0:T(4,128)}, u32[]{:S(2)}) copy-start(s32[4,32]{1,0:T(4,128)} %face_orient.1) | copy-start | bytes 1540
  0.0 1.1 %copy-start.11 = (s32[2,32]{1,0:T(2,128)S(1)}, s32[2,32]{1,0:T(2,128)}, u32[]{:S(2)}) copy-start(s32[2,32]{1,0:T(2,128)} %strike_orient.1) | copy-start | bytes 772
  0.0 1.1 %copy-start.12 = (s32[2,16]{1,0:T(2,128)S(1)}, s32[2,16]{1,0:T(2,128)}, u32[]{:S(2)}) copy-start(s32[2,16]{1,0:T(2,128)} %depth_sends.1) | copy-start | bytes 388
  0.0 1.1 %copy-start.13 = (s32[2,16]{1,0:T(2,128)S(1)}, s32[2,16]{1,0:T(2,128)}, u32[]{:S(2)}) copy-start(s32[2,16]{1,0:T(2,128)} %depth_orient.1) | copy-start | bytes 388
  0.1 1.1 %copy-start.15 = (f32[32]{0:T(128)S(1)}, f32[32]{0:T(128)}, u32[]{:S(2)}) copy-start(f32[32]{0:T(128)} %param.26) | copy-start | bytes 388
  0.1 1.1 %copy-start.16 = (s32[32]{0:T(128)S(1)}, s32[32]{0:T(128)}, u32[]{:S(2)}) copy-start(s32[32]{0:T(128)} %param.34) | copy-start | bytes 388
  0.1 1.1 %copy-start.17 = (s32[32]{0:T(128)S(1)}, s32[32]{0:T(128)}, u32[]{:S(2)}) copy-start(s32[32]{0:T(128)} %param.35) | copy-start | bytes 388
  0.1 1.0 %copy-start.8 = (s32[4,32]{1,0:T(4,128)S(1)}, s32[4,32]{1,0:T(4,128)}, u32[]{:S(2)}) copy-start(s32[4,32]{1,0:T(4,128)} %neighbours.1) | copy-start | bytes 1540
  0.1 1.0 %copy-start.10 = (s32[2,32]{1,0:T(2,128)S(1)}, s32[2,32]{1,0:T(2,128)}, u32[]{:S(2)}) copy-start(s32[2,32]{1,0:T(2,128)} %strike_sends.1) | copy-start | bytes 772
  0.1 1.0 %copy-start.14 = (s32[32]{0:T(128)S(1)}, s32[32]{0:T(128)}, u32[]{:S(2)}) copy-start(s32[32]{0:T(128)} %param.27) | copy-start | bytes 388
  1.2 16.5 %copy-start = (f32[4,9,9,32]{3,0,2,1:T(4,128)S(1)}, f32[4,9,9,32]{3,0,2,1:T(4,128)}, u32[]{:S(2)}) copy-start(f32[4,9,9,32]{3,0,2,1:T(4,128)} %param.20) | copy-start | bytes 124420
  1.2 16.5 %copy-start.1 = (f32[4,9,9,32]{3,0,2,1:T(4,128)S(1)}, f32[4,9,9,32]{3,0,2,1:T(4,128)}, u32[]{:S(2)}) copy-start(f32[4,9,9,32]{3,0,2,1:T(4,128)} %param.21) | copy-start | bytes 124420
  1.2 16.5 %copy-start.3 = (f32[3,56,56]{2,1,0:T(8,128)S(1)}, f32[3,56,56]{2,1,0:T(8,128)}, u32[]{:S(2)}) copy-start(f32[3,56,56]{2,1,0:T(8,128)} %volume.1) | copy-start | bytes 112900
  1.2 16.5 %copy-start.4 = (f32[4,21,56]{2,0,1:T(4,128)S(1)}, f32[4,21,56]{2,0,1:T(4,128)}, u32[]{:S(2)}) copy-start(f32[4,21,56]{2,0,1:T(4,128)} %param.25) | copy-start | bytes 56452
  3.6 15.2 %collective-permute-start.1 = (f32[96,128]{1,0:T(8,128)S(1)}, f32[96,128]{1,0:T(8,128)S(1)}, u32[]{:S(2)}, u32[]{:S(2)}) collective-permute-start(f32[96,128]{1,0:T(8,128)S(1)} %get-tuple-element.38), channel_id=1, source_target_pairs={{8,16},{16,8},{24,32},{32,24},{40,48},{48,40},{56,64},{64,56},{72,... | collective-permute-start | bytes 147464 | tf_op jit(solution)/shard_map/ppermute | solution.py:595
  9.3 9.5 %collective-permute-start.2 = (f32[88,128]{1,0:T(8,128)S(1)}, f32[88,128]{1,0:T(8,128)S(1)}, u32[]{:S(2)}, u32[]{:S(2)}) collective-permute-start(f32[88,128]{1,0:T(8,128)S(1)} %get-tuple-element.39), channel_id=1, source_target_pairs={{0,1},{1,0},{2,3},{3,2},{4,5},{5,4},{6,7},{7,6},{8,9},{9,8},{10,11... | collective-permute-start | bytes 135176 | tf_op jit(solution)/shard_map/ppermute | solution.py:589
  11.4 7.4 %collective-permute-start.3 = (f32[80,128]{1,0:T(8,128)S(1)}, f32[80,128]{1,0:T(8,128)S(1)}, u32[]{:S(2)}, u32[]{:S(2)}) collective-permute-start(f32[80,128]{1,0:T(8,128)S(1)} %get-tuple-element.40), channel_id=1, source_target_pairs={{1,2},{2,1},{3,4},{4,3},{5,6},{6,5},{9,10},{10,9},{11,12},{12,11},... | collective-permute-start | bytes 122888 | tf_op jit(solution)/shard_map/ppermute | solution.py:595
  15.7 3.1 %collective-permute-start = (f32[72,128]{1,0:T(8,128)S(1)}, f32[72,128]{1,0:T(8,128)S(1)}, u32[]{:S(2)}, u32[]{:S(2)}) collective-permute-start(f32[72,128]{1,0:T(8,128)S(1)} %get-tuple-element.37), channel_id=1, source_target_pairs={{0,8},{8,0},{16,24},{24,16},{32,40},{40,32},{48,56},{56,48},{64,72... | collective-permute-start | bytes 110600 | tf_op jit(solution)/shard_map/ppermute | solution.py:589
  21.5 13.9 %collective-permute-start.6 = (f32[96,128]{1,0:T(8,128)S(1)}, f32[96,128]{1,0:T(8,128)S(1)}, u32[]{:S(2)}, u32[]{:S(2)}) collective-permute-start(f32[96,128]{1,0:T(8,128)S(1)} %get-tuple-element.58.sent), channel_id=1, source_target_pairs={{0,1},{1,0},{2,3},{3,2},{4,5},{5,4},{6,7},{7,6},{8,9},{9,8},{10,11... | collective-permute-start | bytes 147464 | tf_op jit(solution)/shard_map/ppermute | solution.py:589
  23.4 12.0 %collective-permute-start.5 = (f32[88,128]{1,0:T(8,128)S(1)}, f32[88,128]{1,0:T(8,128)S(1)}, u32[]{:S(2)}, u32[]{:S(2)}) collective-permute-start(f32[88,128]{1,0:T(8,128)S(1)} %get-tuple-element.57), channel_id=1, source_target_pairs={{8,16},{16,8},{24,32},{32,24},{40,48},{48,40},{56,64},{64,56},{72,... | collective-permute-start | bytes 135176 | tf_op jit(solution)/shard_map/ppermute | solution.py:595
  27.2 8.2 %collective-permute-start.7 = (f32[80,128]{1,0:T(8,128)S(1)}, f32[80,128]{1,0:T(8,128)S(1)}, u32[]{:S(2)}, u32[]{:S(2)}) collective-permute-start(f32[80,128]{1,0:T(8,128)S(1)} %get-tuple-element.59), channel_id=1, source_target_pairs={{1,2},{2,1},{3,4},{4,3},{5,6},{6,5},{9,10},{10,9},{11,12},{12,11},... | collective-permute-start | bytes 122888 | tf_op jit(solution)/shard_map/ppermute | solution.py:595
  32.3 3.1 %collective-permute-start.4 = (f32[72,128]{1,0:T(8,128)S(1)}, f32[72,128]{1,0:T(8,128)S(1)}, u32[]{:S(2)}, u32[]{:S(2)}) collective-permute-start(f32[72,128]{1,0:T(8,128)S(1)} %get-tuple-element.56), channel_id=1, source_target_pairs={{0,8},{8,0},{16,24},{24,16},{32,40},{40,32},{48,56},{56,48},{64,72... | collective-permute-start | bytes 110600 | tf_op jit(solution)/shard_map/ppermute | solution.py:589

commit v5 on v3

--- a/solution.py
+++ b/solution.py
@@ -562,7 +562,7 @@
     result[2 * LANES : 2 * LANES + WIDE, :] = new[2].T[3 * WIDE : 4 * WIDE, :]
 
 
-FIRST_SPARE = (16, 8, 24)
+FIRST_SPARE = (24, 8, 16)
 LATER_SPARE = (16, 8, 24)
 COSTS = dict(place=100000, first_sends=100000, first_local=4, advance=8, later_local=4, combine=4)
 

time: 37.4 us -> 37.4 us (level)
  the two profiles are of different devices: /device:TPU:265 before, /device:TPU:207 now
where the time goes in v5:
time: 37.4 us; the launch traced here: 37 us
  starting transfers between devices  26.7 us (71%)
  Pallas kernels  8.42 us (23%)
  local copies, waits for them, and re-layouts  1.03 us (3%)
  waiting for transfers between devices  0.57 us (2%)
    ppermute x4, starting transfers between devices, with_other_side(): return lax.ppermute(message, axis, pairs)  18.9 us
    pallas_call x6, Pallas kernels, call(): pl.pallas_call(kernel, out_shape=[jax.ShapeDtypeStruct(shape, dtype) for...  8.42 us
    ppermute x4, starting transfers between devices, with_twin(): return lax.ppermute(message, axis, [(i, i ^ 1) for i in range(length)])  7.84 us
    unnamed x36, local copies, waits for them, and re-layouts  1.03 us
  transfers between devices with their start and end apart: 8, of which 2 were waited for; matrix products, arithmetic and copies ran while one was open for 0% of the time, Pallas kernels for 5%

profile of v5, /device:TPU:207, one launch (start us, length us, event | category | flops | bytes accessed | tf_op | source)
XLA Modules:
  0.0 37.0 jit_solution(3203711772091485907)
XLA Ops:
  0.1 0.0 copy-start.8
  0.1 0.0 copy-start.10
  0.1 0.0 copy-start.14
  0.1 0.8 %copy-done.2 = f32[12,56,21]{1,2,0:T(8,128)S(1)} copy-done((f32[12,56,21]{1,2,0:T(8,128)S(1)}, f32[12,56,21]{1,2,0:T(8,128)}, u32[]{:S(2)}) %copy-start.2) | copy-done | bytes 56472
  0.9 0.1 copy-done.7
  1.0 0.1 copy-done.5
  1.0 0.1 copy-done.6
  1.2 0.0 copy-start
  1.2 0.0 copy-start.1
  1.2 0.0 copy-start.3
  1.2 0.0 copy-start.4
  1.2 2.4 %first_sends.1 = (f32[3,56,128]{2,1,0:T(8,128)S(1)}, f32[3,56,128]{2,1,0:T(8,128)S(1)}, f32[3,56,128]{2,1,0:T(8,128)S(1)}, f32[21,4,128]{2,1,0:T(4,128)S(1)}, bf...) custom-call(f32[288,56]{1,0:T(8,128)S(1)} %bitcast.21, ...), custom_call_target="tpu_custom_call" | custom-call | flops 99999997952 | bytes 99999997952 | tf_op jit(solution)/shard_map/first_sends/pallas_call | solution.py:572
  3.6 5.7 %collective-permute-start.1 = (f32[96,128]{1,0:T(8,128)S(1)}, f32[96,128]{1,0:T(8,128)S(1)}, u32[]{:S(2)}, u32[]{:S(2)}) collective-permute-start(f32[96,128]{1,0:T(8,128)S(1)} %get-tuple-element.39), channel_id=1, source_target_pairs={{8,16},{16,8},{24,32},{32,24},{40,48},{48,40},{56,64},{64,56},{72,... | collective-permute-start | bytes 147464 | tf_op jit(solution)/shard_map/ppermute | solution.py:593
  9.3 2.1 %collective-permute-start.2 = (f32[88,128]{1,0:T(8,128)S(1)}, f32[88,128]{1,0:T(8,128)S(1)}, u32[]{:S(2)}, u32[]{:S(2)}) collective-permute-start(f32[88,128]{1,0:T(8,128)S(1)} %get-tuple-element.40), channel_id=1, source_target_pairs={{0,1},{1,0},{2,3},{3,2},{4,5},{5,4},{6,7},{7,6},{8,9},{9,8},{10,11... | collective-permute-start | bytes 135176 | tf_op jit(solution)/shard_map/ppermute | solution.py:587
  11.4 4.3 %collective-permute-start.3 = (f32[80,128]{1,0:T(8,128)S(1)}, f32[80,128]{1,0:T(8,128)S(1)}, u32[]{:S(2)}, u32[]{:S(2)}) collective-permute-start(f32[80,128]{1,0:T(8,128)S(1)} %get-tuple-element.41), channel_id=1, source_target_pairs={{1,2},{2,1},{3,4},{4,3},{5,6},{6,5},{9,10},{10,9},{11,12},{12,11},... | collective-permute-start | bytes 122888 | tf_op jit(solution)/shard_map/ppermute | solution.py:593
  15.7 1.9 %collective-permute-start = (f32[72,128]{1,0:T(8,128)S(1)}, f32[72,128]{1,0:T(8,128)S(1)}, u32[]{:S(2)}, u32[]{:S(2)}) collective-permute-start(f32[72,128]{1,0:T(8,128)S(1)} %get-tuple-element.38), channel_id=1, source_target_pairs={{0,8},{8,0},{16,24},{24,16},{32,40},{40,32},{48,56},{56,48},{64,72... | collective-permute-start | bytes 110600 | tf_op jit(solution)/shard_map/ppermute | solution.py:587
  17.7 1.0 %first_local.1 = (f32[3,56,128]{2,1,0:T(8,128)S(1)}, f32[3,96,128]{2,1,0:T(8,128)S(1)}, f32[3,96,128]{2,1,0:T(8,128)S(1)}, bf16[168,168]{1,0:T(8,128)(2,1)S(1)},...) custom-call(f32[3,56,128]{2,1,0:T(8,128)S(1)} %get-tuple-element.42., ...), custom_call_target="tpu_custom_call" | custom-call | flops 4000000 | bytes 4000000 | tf_op jit(solution)/shard_map/first_local/pallas_call | solution.py:572
  18.7 0.1 collective-permute-done.twin
  18.8 0.0 collective-permute-done.3.beyond
  18.8 0.0 collective-permute-done.2.pair
  18.8 0.0 collective-permute-done.1.across
  18.8 2.7 %advance.1 = (f32[3,56,128]{2,1,0:T(8,128)S(1)}, f32[3,56,128]{2,1,0:T(8,128)S(1)}, f32[72,128]{1,0:T(8,128)S(1)}, f32[88,128]{1,0:T(8,128)S(1)}, f32[80,128]{1,0:T(8,128)S(1)}, /*index=5*/f32[96,128]{1,0:T(8,128)S(1)}) custom-call(f32[72,128]{1,0:T(8,128)S(1)} %collective-permute-done.twin, f32[96,128]{1,0:T(8,128)S(1)} %collective-permute-done.1.across, ...), custom_call_target="tpu_custom_call" | custom-call | flops 8000000 | bytes 8000000 | tf_op jit(solution)/shard_map/advance/pallas_call | solution.py:572
  21.5 1.9 %collective-permute-start.6 = (f32[96,128]{1,0:T(8,128)S(1)}, f32[96,128]{1,0:T(8,128)S(1)}, u32[]{:S(2)}, u32[]{:S(2)}) collective-permute-start(f32[96,128]{1,0:T(8,128)S(1)} %get-tuple-element.59.sent), channel_id=1, source_target_pairs={{0,1},{1,0},{2,3},{3,2},{4,5},{5,4},{6,7},{7,6},{8,9},{9,8},{10,11... | collective-permute-start | bytes 147464 | tf_op jit(solution)/shard_map/ppermute | solution.py:587
  23.4 3.8 %collective-permute-start.5 = (f32[88,128]{1,0:T(8,128)S(1)}, f32[88,128]{1,0:T(8,128)S(1)}, u32[]{:S(2)}, u32[]{:S(2)}) collective-permute-start(f32[88,128]{1,0:T(8,128)S(1)} %get-tuple-element.58), channel_id=1, source_target_pairs={{8,16},{16,8},{24,32},{32,24},{40,48},{48,40},{56,64},{64,56},{72,... | collective-permute-start | bytes 135176 | tf_op jit(solution)/shard_map/ppermute | solution.py:593
  27.2 5.1 %collective-permute-start.7 = (f32[80,128]{1,0:T(8,128)S(1)}, f32[80,128]{1,0:T(8,128)S(1)}, u32[]{:S(2)}, u32[]{:S(2)}) collective-permute-start(f32[80,128]{1,0:T(8,128)S(1)} %get-tuple-element.60), channel_id=1, source_target_pairs={{1,2},{2,1},{3,4},{4,3},{5,6},{6,5},{9,10},{10,9},{11,12},{12,11},... | collective-permute-start | bytes 122888 | tf_op jit(solution)/shard_map/ppermute | solution.py:593
  32.3 1.9 %collective-permute-start.4 = (f32[72,128]{1,0:T(8,128)S(1)}, f32[72,128]{1,0:T(8,128)S(1)}, u32[]{:S(2)}, u32[]{:S(2)}) collective-permute-start(f32[72,128]{1,0:T(8,128)S(1)} %get-tuple-element.57), channel_id=1, source_target_pairs={{0,8},{8,0},{16,24},{24,16},{32,40},{40,32},{48,56},{56,48},{64,72... | collective-permute-start | bytes 110600 | tf_op jit(solution)/shard_map/ppermute | solution.py:587
  34.2 0.7 %later_local.1 = (f32[3,56,128]{2,1,0:T(8,128)S(1)}, f32[3,96,128]{2,1,0:T(8,128)S(1)}, f32[3,96,128]{2,1,0:T(8,128)S(1)}) custom-call(f32[3,56,128]{2,1,0:T(8,128)S(1)} %get-tuple-element.61.values, f32[3,56,128]{2,1,0:T(8,128)S(1)} %get-tuple-element.62.base, f32[21,4,128]{2,1,0:T(4,128)S(1)} %get-tuple-element.44.jac_coefs, ...), custom_call_target="tpu_custom_call" | custom-call | flops 4000000 | bytes 4000000 | tf_op jit(solution)/shard_map/later_local/pallas_call | solution.py:572
  35.0 0.5 %collective-permute-done.4.twin = f32[72,128]{1,0:T(8,128)S(1)} collective-permute-done((f32[72,128]{1,0:T(8,128)S(1)}, f32[72,128]{1,0:T(8,128)S(1)}, u32[]{:S(2)}, u32[]{:S(2)}) %collective-permute-start.4) | collective-permute-done | bytes 36896 | tf_op jit(solution)/shard_map/ppermute | solution.py:587
  35.4 0.0 collective-permute-done.7.beyond
  35.4 0.0 collective-permute-done.5.across
  35.4 0.0 collective-permute-done.6.pair
  35.4 1.6 %combine.1 = f32[288,56]{1,0:T(8,128)} custom-call(f32[72,128]{1,0:T(8,128)S(1)} %collective-permute-done.4.twin, f32[88,128]{1,0:T(8,128)S(1)} %collective-permute-done.5.across, f32[96,128]{1,0:T(8,128)S(1)} %collective-permute-done.6.pair, f32[80,128]{1,0:T(8,128)S(1)} %collective-permute-done.7.beyond, bf16[384,512]{1,0:T(8,128)(2,1)S(1)} %get-tuple-element.47.halo, ...), custom_call_target="tpu_custom_call" | custom-call | flops 4000000 | bytes 4000000 | tf_op jit(solution)/shard_map/combine/pallas_call | solution.py:572
  (26 shorter events, 0.1 us)
Async XLA Ops:
  0.0 0.9 %copy-start.2 = (f32[12,56,21]{1,2,0:T(8,128)S(1)}, f32[12,56,21]{1,2,0:T(8,128)}, u32[]{:S(2)}) copy-start(f32[12,56,21]{1,2,0:T(8,128)} %param.24) | copy-start | bytes 169348
  0.0 1.0 %copy-start.7 = (f32[3,56,56]{2,1,0:T(8,128)S(1)}, f32[3,56,56]{2,1,0:T(8,128)}, u32[]{:S(2)}) copy-start(f32[3,56,56]{2,1,0:T(8,128)} %stiffness.1) | copy-start | bytes 112900
  0.0 1.0 %copy-start.5 = (f32[3,9,9,32]{3,0,2,1:T(4,128)S(1)}, f32[3,9,9,32]{3,0,2,1:T(4,128)}, u32[]{:S(2)}) copy-start(f32[3,9,9,32]{3,0,2,1:T(4,128)} %param.19) | copy-start | bytes 93316
  0.0 1.1 %copy-start.6 = (f32[9,56,32]{1,2,0:T(8,128)S(1)}, f32[9,56,32]{1,2,0:T(8,128)}, u32[]{:S(2)}) copy-start(f32[9,56,32]{1,2,0:T(8,128)} %param.18) | copy-start | bytes 193540
  0.0 1.1 %copy-start.9 = (s32[4,32]{1,0:T(4,128)S(1)}, s32[4,32]{1,0:T(4,128)}, u32[]{:S(2)}) copy-start(s32[4,32]{1,0:T(4,128)} %face_orient.1) | copy-start | bytes 1540
  0.0 1.1 %copy-start.11 = (s32[2,32]{1,0:T(2,128)S(1)}, s32[2,32]{1,0:T(2,128)}, u32[]{:S(2)}) copy-start(s32[2,32]{1,0:T(2,128)} %strike_orient.1) | copy-start | bytes 772
  0.0 1.1 %copy-start.12 = (s32[2,16]{1,0:T(2,128)S(1)}, s32[2,16]{1,0:T(2,128)}, u32[]{:S(2)}) copy-start(s32[2,16]{1,0:T(2,128)} %depth_sends.1) | copy-start | bytes 388
  0.0 1.1 %copy-start.13 = (s32[2,16]{1,0:T(2,128)S(1)}, s32[2,16]{1,0:T(2,128)}, u32[]{:S(2)}) copy-start(s32[2,16]{1,0:T(2,128)} %depth_orient.1) | copy-start | bytes 388
  0.1 1.1 %copy-start.15 = (f32[32]{0:T(128)S(1)}, f32[32]{0:T(128)}, u32[]{:S(2)}) copy-start(f32[32]{0:T(128)} %param.26) | copy-start | bytes 388
  0.1 1.1 %copy-start.16 = (s32[32]{0:T(128)S(1)}, s32[32]{0:T(128)}, u32[]{:S(2)}) copy-start(s32[32]{0:T(128)} %param.34) | copy-start | bytes 388
  0.1 1.1 %copy-start.17 = (s32[32]{0:T(128)S(1)}, s32[32]{0:T(128)}, u32[]{:S(2)}) copy-start(s32[32]{0:T(128)} %param.35) | copy-start | bytes 388
  0.1 1.0 %copy-start.8 = (s32[4,32]{1,0:T(4,128)S(1)}, s32[4,32]{1,0:T(4,128)}, u32[]{:S(2)}) copy-start(s32[4,32]{1,0:T(4,128)} %neighbours.1) | copy-start | bytes 1540
  0.1 1.0 %copy-start.10 = (s32[2,32]{1,0:T(2,128)S(1)}, s32[2,32]{1,0:T(2,128)}, u32[]{:S(2)}) copy-start(s32[2,32]{1,0:T(2,128)} %strike_sends.1) | copy-start | bytes 772
  0.1 1.0 %copy-start.14 = (s32[32]{0:T(128)S(1)}, s32[32]{0:T(128)}, u32[]{:S(2)}) copy-start(s32[32]{0:T(128)} %param.27) | copy-start | bytes 388
  1.2 16.5 %copy-start = (f32[4,9,9,32]{3,0,2,1:T(4,128)S(1)}, f32[4,9,9,32]{3,0,2,1:T(4,128)}, u32[]{:S(2)}) copy-start(f32[4,9,9,32]{3,0,2,1:T(4,128)} %param.20) | copy-start | bytes 124420
  1.2 16.5 %copy-start.1 = (f32[4,9,9,32]{3,0,2,1:T(4,128)S(1)}, f32[4,9,9,32]{3,0,2,1:T(4,128)}, u32[]{:S(2)}) copy-start(f32[4,9,9,32]{3,0,2,1:T(4,128)} %param.21) | copy-start | bytes 124420
  1.2 16.5 %copy-start.3 = (f32[3,56,56]{2,1,0:T(8,128)S(1)}, f32[3,56,56]{2,1,0:T(8,128)}, u32[]{:S(2)}) copy-start(f32[3,56,56]{2,1,0:T(8,128)} %volume.1) | copy-start | bytes 112900
  1.2 16.5 %copy-start.4 = (f32[4,21,56]{2,0,1:T(4,128)S(1)}, f32[4,21,56]{2,0,1:T(4,128)}, u32[]{:S(2)}) copy-start(f32[4,21,56]{2,0,1:T(4,128)} %param.25) | copy-start | bytes 56452
  3.6 15.2 %collective-permute-start.1 = (f32[96,128]{1,0:T(8,128)S(1)}, f32[96,128]{1,0:T(8,128)S(1)}, u32[]{:S(2)}, u32[]{:S(2)}) collective-permute-start(f32[96,128]{1,0:T(8,128)S(1)} %get-tuple-element.39), channel_id=1, source_target_pairs={{8,16},{16,8},{24,32},{32,24},{40,48},{48,40},{56,64},{64,56},{72,... | collective-permute-start | bytes 147464 | tf_op jit(solution)/shard_map/ppermute | solution.py:593
  9.3 9.5 %collective-permute-start.2 = (f32[88,128]{1,0:T(8,128)S(1)}, f32[88,128]{1,0:T(8,128)S(1)}, u32[]{:S(2)}, u32[]{:S(2)}) collective-permute-start(f32[88,128]{1,0:T(8,128)S(1)} %get-tuple-element.40), channel_id=1, source_target_pairs={{0,1},{1,0},{2,3},{3,2},{4,5},{5,4},{6,7},{7,6},{8,9},{9,8},{10,11... | collective-permute-start | bytes 135176 | tf_op jit(solution)/shard_map/ppermute | solution.py:587
  11.4 7.4 %collective-permute-start.3 = (f32[80,128]{1,0:T(8,128)S(1)}, f32[80,128]{1,0:T(8,128)S(1)}, u32[]{:S(2)}, u32[]{:S(2)}) collective-permute-start(f32[80,128]{1,0:T(8,128)S(1)} %get-tuple-element.41), channel_id=1, source_target_pairs={{1,2},{2,1},{3,4},{4,3},{5,6},{6,5},{9,10},{10,9},{11,12},{12,11},... | collective-permute-start | bytes 122888 | tf_op jit(solution)/shard_map/ppermute | solution.py:593
  15.7 3.1 %collective-permute-start = (f32[72,128]{1,0:T(8,128)S(1)}, f32[72,128]{1,0:T(8,128)S(1)}, u32[]{:S(2)}, u32[]{:S(2)}) collective-permute-start(f32[72,128]{1,0:T(8,128)S(1)} %get-tuple-element.38), channel_id=1, source_target_pairs={{0,8},{8,0},{16,24},{24,16},{32,40},{40,32},{48,56},{56,48},{64,72... | collective-permute-start | bytes 110600 | tf_op jit(solution)/shard_map/ppermute | solution.py:587
  21.5 13.9 %collective-permute-start.6 = (f32[96,128]{1,0:T(8,128)S(1)}, f32[96,128]{1,0:T(8,128)S(1)}, u32[]{:S(2)}, u32[]{:S(2)}) collective-permute-start(f32[96,128]{1,0:T(8,128)S(1)} %get-tuple-element.59.sent), channel_id=1, source_target_pairs={{0,1},{1,0},{2,3},{3,2},{4,5},{5,4},{6,7},{7,6},{8,9},{9,8},{10,11... | collective-permute-start | bytes 147464 | tf_op jit(solution)/shard_map/ppermute | solution.py:587
  23.4 12.0 %collective-permute-start.5 = (f32[88,128]{1,0:T(8,128)S(1)}, f32[88,128]{1,0:T(8,128)S(1)}, u32[]{:S(2)}, u32[]{:S(2)}) collective-permute-start(f32[88,128]{1,0:T(8,128)S(1)} %get-tuple-element.58), channel_id=1, source_target_pairs={{8,16},{16,8},{24,32},{32,24},{40,48},{48,40},{56,64},{64,56},{72,... | collective-permute-start | bytes 135176 | tf_op jit(solution)/shard_map/ppermute | solution.py:593
  27.2 8.2 %collective-permute-start.7 = (f32[80,128]{1,0:T(8,128)S(1)}, f32[80,128]{1,0:T(8,128)S(1)}, u32[]{:S(2)}, u32[]{:S(2)}) collective-permute-start(f32[80,128]{1,0:T(8,128)S(1)} %get-tuple-element.60), channel_id=1, source_target_pairs={{1,2},{2,1},{3,4},{4,3},{5,6},{6,5},{9,10},{10,9},{11,12},{12,11},... | collective-permute-start | bytes 122888 | tf_op jit(solution)/shard_map/ppermute | solution.py:593
  32.3 3.1 %collective-permute-start.4 = (f32[72,128]{1,0:T(8,128)S(1)}, f32[72,128]{1,0:T(8,128)S(1)}, u32[]{:S(2)}, u32[]{:S(2)}) collective-permute-start(f32[72,128]{1,0:T(8,128)S(1)} %get-tuple-element.57), channel_id=1, source_target_pairs={{0,8},{8,0},{16,24},{24,16},{32,40},{40,32},{48,56},{56,48},{64,72... | collective-permute-start | bytes 110600 | tf_op jit(solution)/shard_map/ppermute | solution.py:587
